TPU v7x, 32 devices: a whole 2x2x4 slice. The times are simulated.
32 devices in a mesh: tm: 4 (over y, x), lat: 8 (over z, core).
Axes of the slice: x: 2, y: 2, z: 4, core: 2. Of those that a mesh axis runs over, the one named last changes fastest.
Arguments:
- cotangent: float32 [16, 128, 2048], P('tm', 'lat'), may hold values from -6 to 6
- iterates: float32 [3, 16, 128, 2048], P(None, 'tm', 'lat'), may hold values from -6 to 6
- range_field: float32 [128, 2048], P('lat', 'tm'), may hold values from 0.05 to 1
Outputs:
- noise_cotangent: float32 [16, 128, 2048], P('tm', 'lat')
- range_gradient: float32 [128, 2048], P('lat', 'tm')
All inputs are finite; a program needn't handle non-finite values.
Results may differ from a plain program's by a relative error of at most 0.0001.
Values sent between devices are 32-bit elements; how exact they have to be, the bound alone decides.
No kernel may reach another device: no remote copies, remote signals or barrier semaphores. Data moves between devices by JAX's collectives and lax.ppermute only.
A program may use at most 64 MiB of HBM per device.

v0:
```python
import math

import jax
import jax.numpy as jnp
from jax import lax
from jax.sharding import PartitionSpec as P


def extended(cells, sides, width):
    for axis, dim in sides:
        count = lax.axis_size(axis)
        ends = count - 1
        head = lax.slice_in_dim(cells, 0, width, axis=dim)
        tail = lax.slice_in_dim(cells, cells.shape[dim] - width, cells.shape[dim], axis=dim)
        cells = jnp.concatenate(
            [
                lax.ppermute(tail, axis, [(i, (i + 1) % count) for i in range(ends)]),
                cells,
                lax.ppermute(head, axis, [((i + 1) % count, i) for i in range(ends)]),
            ],
            axis=dim,
        )
    return cells


def step_weights():
    centre_value = 6.525
    spread_value = 6.475
    root_order = (3, 0, 2, 1)
    return [
        1.0 / (centre_value + spread_value * math.cos(math.pi * (2 * section + 1) / 8.0))
        for section in root_order
    ]


def stencil(field, coefficient, previous, following, upper_row, lower_row):
    longitude = jnp.roll(field, 1, 2) + jnp.roll(field, -1, 2)
    return (
        (coefficient[None, :, :] + 6.0) * field
        - upper_row
        - lower_row
        - longitude
        - previous
        - following
    )


def body(cotangent, iterates, range_field):
    weights = step_weights()
    range_rows = lax.all_gather(range_field, "tm", axis=1, tiled=True)
    adjoint = cotangent
    noise_cot = weights[3] * cotangent
    gradient = jnp.zeros(range_field.shape, jnp.float32)
    for section in (3, 2, 1):
        own_cells = adjoint
        product_sum = -weights[section] * jnp.sum(own_cells * iterates[section - 1], axis=0)
        gradient = gradient + lax.psum_scatter(product_sum, "tm", scatter_dimension=1, tiled=True)
        timed = extended(adjoint, (("tm", 0),), 1)
        rowed = extended(adjoint, (("lat", 1),), 1)
        applied = stencil(adjoint, range_rows, timed[:-2], timed[2:], rowed[:, 2:], rowed[:, :-2])
        adjoint = adjoint - weights[section] * applied
        noise_cot = noise_cot + weights[section - 1] * adjoint
    return (noise_cot, gradient)


def solution(mesh):
    placed = (P("tm", "lat", None), P(None, "tm", "lat", None), P("lat", "tm"))
    return jax.shard_map(
        body,
        mesh=mesh,
        in_specs=placed,
        out_specs=(P("tm", "lat", None), P("lat", "tm")),
        check_vma=False,
    )
```

profile of v0, /device:TPU:0, one launch (start us, length us, event | category | flops | bytes accessed | tf_op | source)
XLA Modules:
  0.0 91.3 jit_solution(2317200315176423946)
XLA Ops:
  7.2 0.0 reduce-scatter.2.cloned.1.call-start
  7.2 1.1 %fusion.37 = (f32[4,1,2048]{2,1,0:T(1,128)S(1)}, f32[4,1,2048]{2,1,0:T(1,128)S(1)}) fusion(f32[4,16,2048]{2,1,0:T(8,128)} %param.3), kind=kLoop, calls=%fused_computation.56 | loop fusion | bytes 131072 | tf_op jit(solution)/shard_map/slice | solution.py:13
  8.4 1.3 %collective-permute-start = (f32[4,1,2048]{2,1,0:T(1,128)S(1)}, f32[4,1,2048]{2,1,0:T(1,128)S(1)}, u32[]{:S(2)}, u32[]{:S(2)}) collective-permute-start(f32[4,1,2048]{2,1,0:T(1,128)S(1)} %get-tuple-element.26), channel_id=1, source_target_pairs={{1,0},{2,1},{3,2},{4,3},{5,4},{6,5},{7,6},{9,8},{10,9},{11,10},{12... | collective-permute-start | bytes 98312 | tf_op jit(solution)/shard_map/ppermute | solution.py:19
  9.7 3.0 %collective-permute-start.1 = (f32[4,1,2048]{2,1,0:T(1,128)S(1)}, f32[4,1,2048]{2,1,0:T(1,128)S(1)}, u32[]{:S(2)}, u32[]{:S(2)}) collective-permute-start(f32[4,1,2048]{2,1,0:T(1,128)S(1)} %get-tuple-element.27), channel_id=1, source_target_pairs={{0,1},{1,2},{2,3},{3,4},{4,5},{5,6},{6,7},{8,9},{9,10},{10,11},{11... | collective-permute-start | bytes 98312 | tf_op jit(solution)/shard_map/ppermute | solution.py:17
  12.7 1.0 %fusion.38 = (f32[1,16,2048]{2,1,0:T(8,128)S(1)}, f32[1,16,2048]{2,1,0:T(8,128)S(1)}) fusion(f32[4,16,2048]{2,1,0:T(8,128)} %param.3), kind=kLoop, calls=%fused_computation.57 | loop fusion | bytes 524288 | tf_op jit(solution)/shard_map/slice | solution.py:14
  13.7 4.8 %collective-permute-start.2 = (f32[1,16,2048]{2,1,0:T(8,128)S(1)}, f32[1,16,2048]{2,1,0:T(8,128)S(1)}, u32[]{:S(2)}, u32[]{:S(2)}) collective-permute-start(f32[1,16,2048]{2,1,0:T(8,128)S(1)} %get-tuple-element.28), channel_id=1, source_target_pairs={{0,8},{8,16},{16,24},{1,9},{9,17},{17,25},{2,10},{10,18},{18,26},{... | collective-permute-start | bytes 393224 | tf_op jit(solution)/shard_map/ppermute | solution.py:17
  18.6 1.3 %collective-permute-start.3 = (f32[1,16,2048]{2,1,0:T(8,128)S(1)}, f32[1,16,2048]{2,1,0:T(8,128)S(1)}, u32[]{:S(2)}, u32[]{:S(2)}) collective-permute-start(f32[1,16,2048]{2,1,0:T(8,128)S(1)} %get-tuple-element.29), channel_id=1, source_target_pairs={{8,0},{16,8},{24,16},{9,1},{17,9},{25,17},{10,2},{18,10},{26,18},{... | collective-permute-start | bytes 393224 | tf_op jit(solution)/shard_map/ppermute | solution.py:19
  19.9 1.4 %fusion.35 = (f32[4,16,2047]{2,1,0:T(8,128)S(1)}, f32[4,16,2047]{2,1,0:T(8,128)S(1)}) fusion(f32[4,16,2048]{2,1,0:T(8,128)} %param.3), kind=kLoop, calls=%fused_computation.54 | loop fusion | bytes 2096128 | tf_op jit(solution)/shard_map/jit(_roll_static)/slice | solution.py:37
  21.3 10.5 %all_gather.3 = f32[16,2048]{1,0:T(8,128)S(1)} all-gather(f32[16,512]{1,0:T(8,128)S(1)} %copy-done.2), channel_id=1, replica_groups=mesh['tm'=4,'lat'=8] {'tm'}, dimensions={1}, use_global_device_ids=true | all-gather | bytes 163840 | tf_op jit(solution)/shard_map/all_gather | solution.py:50
  31.8 0.1 fusion.36
  31.9 0.3 fusion.18
  32.4 0.2 fusion.33
  32.6 1.4 %collective-permute-start.4 = (f32[4,1,2048]{2,1,0:T(1,128)S(1)}, f32[4,1,2048]{2,1,0:T(1,128)S(1)}, u32[]{:S(2)}, u32[]{:S(2)}) collective-permute-start(f32[4,1,2048]{2,1,0:T(1,128)S(1)} %get-tuple-element.14), channel_id=1, source_target_pairs={{1,0},{2,1},{3,2},{4,3},{5,4},{6,5},{7,6},{9,8},{10,9},{11,10},{12... | collective-permute-start | bytes 98312 | tf_op jit(solution)/shard_map/ppermute | solution.py:19
  34.0 3.0 %collective-permute-start.5 = (f32[4,1,2048]{2,1,0:T(1,128)S(1)}, f32[4,1,2048]{2,1,0:T(1,128)S(1)}, u32[]{:S(2)}, u32[]{:S(2)}) collective-permute-start(f32[4,1,2048]{2,1,0:T(1,128)S(1)} %get-tuple-element.15), channel_id=1, source_target_pairs={{0,1},{1,2},{2,3},{3,4},{4,5},{5,6},{6,7},{8,9},{9,10},{10,11},{11... | collective-permute-start | bytes 98312 | tf_op jit(solution)/shard_map/ppermute | solution.py:17
  37.0 2.5 %collective-permute-start.6 = (f32[1,16,2048]{2,1,0:T(8,128)S(1)}, f32[1,16,2048]{2,1,0:T(8,128)S(1)}, u32[]{:S(2)}, u32[]{:S(2)}) collective-permute-start(f32[1,16,2048]{2,1,0:T(8,128)S(1)} %get-tuple-element.20), channel_id=1, source_target_pairs={{0,8},{8,16},{16,24},{1,9},{9,17},{17,25},{2,10},{10,18},{18,26},{... | collective-permute-start | bytes 393224 | tf_op jit(solution)/shard_map/ppermute | solution.py:17
  39.5 1.3 %collective-permute-start.7 = (f32[1,16,2048]{2,1,0:T(8,128)S(1)}, f32[1,16,2048]{2,1,0:T(8,128)S(1)}, u32[]{:S(2)}, u32[]{:S(2)}) collective-permute-start(f32[1,16,2048]{2,1,0:T(8,128)S(1)} %get-tuple-element.21), channel_id=1, source_target_pairs={{8,0},{16,8},{24,16},{9,1},{17,9},{25,17},{10,2},{18,10},{26,18},{... | collective-permute-start | bytes 393224 | tf_op jit(solution)/shard_map/ppermute | solution.py:19
  40.8 0.1 fusion.32
  40.9 2.2 %collective-permute-done.6 = f32[1,16,2048]{2,1,0:T(8,128)S(1)} collective-permute-done((f32[1,16,2048]{2,1,0:T(8,128)S(1)}, f32[1,16,2048]{2,1,0:T(8,128)S(1)}, u32[]{:S(2)}, u32[]{:S(2)}) %collective-permute-start.6) | collective-permute-done | bytes 131104 | tf_op jit(solution)/shard_map/ppermute | solution.py:17
  43.2 4.7 %collective-permute-done.7 = f32[1,16,2048]{2,1,0:T(8,128)S(1)} collective-permute-done((f32[1,16,2048]{2,1,0:T(8,128)S(1)}, f32[1,16,2048]{2,1,0:T(8,128)S(1)}, u32[]{:S(2)}, u32[]{:S(2)}) %collective-permute-start.7) | collective-permute-done | bytes 131104 | tf_op jit(solution)/shard_map/ppermute | solution.py:19
  47.9 0.5 fusion.25
  48.5 0.2 fusion.27
  48.7 1.3 %collective-permute-start.8 = (f32[4,1,2048]{2,1,0:T(1,128)S(1)}, f32[4,1,2048]{2,1,0:T(1,128)S(1)}, u32[]{:S(2)}, u32[]{:S(2)}) collective-permute-start(f32[4,1,2048]{2,1,0:T(1,128)S(1)} %get-tuple-element.10), channel_id=1, source_target_pairs={{1,0},{2,1},{3,2},{4,3},{5,4},{6,5},{7,6},{9,8},{10,9},{11,10},{12... | collective-permute-start | bytes 98312 | tf_op jit(solution)/shard_map/ppermute | solution.py:19
  50.0 3.0 %collective-permute-start.9 = (f32[4,1,2048]{2,1,0:T(1,128)S(1)}, f32[4,1,2048]{2,1,0:T(1,128)S(1)}, u32[]{:S(2)}, u32[]{:S(2)}) collective-permute-start(f32[4,1,2048]{2,1,0:T(1,128)S(1)} %get-tuple-element.11), channel_id=1, source_target_pairs={{0,1},{1,2},{2,3},{3,4},{4,5},{5,6},{6,7},{8,9},{9,10},{10,11},{11... | collective-permute-start | bytes 98312 | tf_op jit(solution)/shard_map/ppermute | solution.py:17
  53.0 4.1 %collective-permute-start.10 = (f32[1,16,2048]{2,1,0:T(8,128)S(1)}, f32[1,16,2048]{2,1,0:T(8,128)S(1)}, u32[]{:S(2)}, u32[]{:S(2)}) collective-permute-start(f32[1,16,2048]{2,1,0:T(8,128)S(1)} %get-tuple-element.12), channel_id=1, source_target_pairs={{0,8},{8,16},{16,24},{1,9},{9,17},{17,25},{2,10},{10,18},{18,26},{... | collective-permute-start | bytes 393224 | tf_op jit(solution)/shard_map/ppermute | solution.py:17
  57.2 1.3 %collective-permute-start.11 = (f32[1,16,2048]{2,1,0:T(8,128)S(1)}, f32[1,16,2048]{2,1,0:T(8,128)S(1)}, u32[]{:S(2)}, u32[]{:S(2)}) collective-permute-start(f32[1,16,2048]{2,1,0:T(8,128)S(1)} %get-tuple-element.13), channel_id=1, source_target_pairs={{8,0},{16,8},{24,16},{9,1},{17,9},{25,17},{10,2},{18,10},{26,18},{... | collective-permute-start | bytes 393224 | tf_op jit(solution)/shard_map/ppermute | solution.py:19
  58.5 0.7 add_add_fusion
  59.2 0.1 fusion.28
  59.2 0.0 reduce-scatter.2.cloned.1.call-update
  59.3 1.4 %collective-permute-done.10 = f32[1,16,2048]{2,1,0:T(8,128)S(1)} collective-permute-done((f32[1,16,2048]{2,1,0:T(8,128)S(1)}, f32[1,16,2048]{2,1,0:T(8,128)S(1)}, u32[]{:S(2)}, u32[]{:S(2)}) %collective-permute-start.10) | collective-permute-done | bytes 131104 | tf_op jit(solution)/shard_map/ppermute | solution.py:17
  60.7 4.7 %collective-permute-done.11 = f32[1,16,2048]{2,1,0:T(8,128)S(1)} collective-permute-done((f32[1,16,2048]{2,1,0:T(8,128)S(1)}, f32[1,16,2048]{2,1,0:T(8,128)S(1)}, u32[]{:S(2)}, u32[]{:S(2)}) %collective-permute-start.11) | collective-permute-done | bytes 131104 | tf_op jit(solution)/shard_map/ppermute | solution.py:19
  65.4 1.2 %fusion.4 = f32[4,16,2048]{2,1,0:T(8,128)} fusion(f32[4,16,2048]{2,1,0:T(8,128)S(1)} %get-tuple-element.5, f32[1,16,2048]{2,1,0:T(8,128)S(1)} %collective-permute-done.11, f32[1,16,2048]{2,1,0:T(8,128)S(1)} %collective-permute-done.10, f32[4,1,2048]{2,1,0:T(1,128)S(1)} %collective-permute-done.9, f32[4,1,2048]{2,1,0:T(1,128)S(1)} %collective-permute-done.8, ...), kind=kLoop, calls=%fused_computation.5 | loop fusion | flops 2883584 | bytes 3604480 | tf_op jit(solution)/shard_map/add | solution.py:62
  66.6 17.8 %reduce-scatter.2.cloned.1.call-done = f32[16,512]{1,0:T(8,128)} async-done(((f32[16,2048]{1,0:T(8,128)}), f32[16,512]{1,0:T(8,128)}) %reduce-scatter.2.cloned.1.call-update) | async-done | bytes 32784 | tf_op jit(solution)/shard_map/reduce_scatter | solution.py:57
  (19 shorter events, 0.2 us)
Async XLA Ops:
  7.2 24.6 %copy-start = (f32[4,16,2048]{2,1,0:T(8,128)S(1)}, f32[4,16,2048]{2,1,0:T(8,128)}, u32[]{:S(2)}) copy-start(f32[4,16,2048]{2,1,0:T(8,128)} %param.3) | copy-start | bytes 1572868
  7.2 14.1 %copy-start.2 = (f32[16,512]{1,0:T(8,128)S(1)}, f32[16,512]{1,0:T(8,128)}, u32[]{:S(2)}) copy-start(f32[16,512]{1,0:T(8,128)} %param.5) | copy-start | bytes 98308
  7.2 77.2 %reduce-scatter.2.cloned.1.call-start = ((), (), s32[]{:S(2)}) async-start(), calls=%async_computation.1 | async-start | bytes 163840 | tf_op jit(solution)/shard_map/reduce_scatter | solution.py:57
  8.4 23.5 %collective-permute-start = (f32[4,1,2048]{2,1,0:T(1,128)S(1)}, f32[4,1,2048]{2,1,0:T(1,128)S(1)}, u32[]{:S(2)}, u32[]{:S(2)}) collective-permute-start(f32[4,1,2048]{2,1,0:T(1,128)S(1)} %get-tuple-element.26), channel_id=1, source_target_pairs={{1,0},{2,1},{3,2},{4,3},{5,4},{6,5},{7,6},{9,8},{10,9},{11,10},{12... | collective-permute-start | bytes 98312 | tf_op jit(solution)/shard_map/ppermute | solution.py:19
  9.7 22.2 %collective-permute-start.1 = (f32[4,1,2048]{2,1,0:T(1,128)S(1)}, f32[4,1,2048]{2,1,0:T(1,128)S(1)}, u32[]{:S(2)}, u32[]{:S(2)}) collective-permute-start(f32[4,1,2048]{2,1,0:T(1,128)S(1)} %get-tuple-element.27), channel_id=1, source_target_pairs={{0,1},{1,2},{2,3},{3,4},{4,5},{5,6},{6,7},{8,9},{9,10},{10,11},{11... | collective-permute-start | bytes 98312 | tf_op jit(solution)/shard_map/ppermute | solution.py:17
  13.7 18.2 %collective-permute-start.2 = (f32[1,16,2048]{2,1,0:T(8,128)S(1)}, f32[1,16,2048]{2,1,0:T(8,128)S(1)}, u32[]{:S(2)}, u32[]{:S(2)}) collective-permute-start(f32[1,16,2048]{2,1,0:T(8,128)S(1)} %get-tuple-element.28), channel_id=1, source_target_pairs={{0,8},{8,16},{16,24},{1,9},{9,17},{17,25},{2,10},{10,18},{18,26},{... | collective-permute-start | bytes 393224 | tf_op jit(solution)/shard_map/ppermute | solution.py:17
  18.6 13.4 %collective-permute-start.3 = (f32[1,16,2048]{2,1,0:T(8,128)S(1)}, f32[1,16,2048]{2,1,0:T(8,128)S(1)}, u32[]{:S(2)}, u32[]{:S(2)}) collective-permute-start(f32[1,16,2048]{2,1,0:T(8,128)S(1)} %get-tuple-element.29), channel_id=1, source_target_pairs={{8,0},{16,8},{24,16},{9,1},{17,9},{25,17},{10,2},{18,10},{26,18},{... | collective-permute-start | bytes 393224 | tf_op jit(solution)/shard_map/ppermute | solution.py:19
  32.3 15.6 %copy-start.1 = (f32[3,4,16,2048]{3,2,1,0:T(8,128)S(1)}, f32[3,4,16,2048]{3,2,1,0:T(8,128)}, u32[]{:S(2)}) copy-start(f32[3,4,16,2048]{3,2,1,0:T(8,128)} %param.4) | copy-start | bytes 4718596
  32.6 8.4 %collective-permute-start.4 = (f32[4,1,2048]{2,1,0:T(1,128)S(1)}, f32[4,1,2048]{2,1,0:T(1,128)S(1)}, u32[]{:S(2)}, u32[]{:S(2)}) collective-permute-start(f32[4,1,2048]{2,1,0:T(1,128)S(1)} %get-tuple-element.14), channel_id=1, source_target_pairs={{1,0},{2,1},{3,2},{4,3},{5,4},{6,5},{7,6},{9,8},{10,9},{11,10},{12... | collective-permute-start | bytes 98312 | tf_op jit(solution)/shard_map/ppermute | solution.py:19
  34.0 6.9 %collective-permute-start.5 = (f32[4,1,2048]{2,1,0:T(1,128)S(1)}, f32[4,1,2048]{2,1,0:T(1,128)S(1)}, u32[]{:S(2)}, u32[]{:S(2)}) collective-permute-start(f32[4,1,2048]{2,1,0:T(1,128)S(1)} %get-tuple-element.15), channel_id=1, source_target_pairs={{0,1},{1,2},{2,3},{3,4},{4,5},{5,6},{6,7},{8,9},{9,10},{10,11},{11... | collective-permute-start | bytes 98312 | tf_op jit(solution)/shard_map/ppermute | solution.py:17
  37.0 6.2 %collective-permute-start.6 = (f32[1,16,2048]{2,1,0:T(8,128)S(1)}, f32[1,16,2048]{2,1,0:T(8,128)S(1)}, u32[]{:S(2)}, u32[]{:S(2)}) collective-permute-start(f32[1,16,2048]{2,1,0:T(8,128)S(1)} %get-tuple-element.20), channel_id=1, source_target_pairs={{0,8},{8,16},{16,24},{1,9},{9,17},{17,25},{2,10},{10,18},{18,26},{... | collective-permute-start | bytes 393224 | tf_op jit(solution)/shard_map/ppermute | solution.py:17
  39.5 8.4 %collective-permute-start.7 = (f32[1,16,2048]{2,1,0:T(8,128)S(1)}, f32[1,16,2048]{2,1,0:T(8,128)S(1)}, u32[]{:S(2)}, u32[]{:S(2)}) collective-permute-start(f32[1,16,2048]{2,1,0:T(8,128)S(1)} %get-tuple-element.21), channel_id=1, source_target_pairs={{8,0},{16,8},{24,16},{9,1},{17,9},{25,17},{10,2},{18,10},{26,18},{... | collective-permute-start | bytes 393224 | tf_op jit(solution)/shard_map/ppermute | solution.py:19
  48.7 10.6 %collective-permute-start.8 = (f32[4,1,2048]{2,1,0:T(1,128)S(1)}, f32[4,1,2048]{2,1,0:T(1,128)S(1)}, u32[]{:S(2)}, u32[]{:S(2)}) collective-permute-start(f32[4,1,2048]{2,1,0:T(1,128)S(1)} %get-tuple-element.10), channel_id=1, source_target_pairs={{1,0},{2,1},{3,2},{4,3},{5,4},{6,5},{7,6},{9,8},{10,9},{11,10},{12... | collective-permute-start | bytes 98312 | tf_op jit(solution)/shard_map/ppermute | solution.py:19
  50.0 9.3 %collective-permute-start.9 = (f32[4,1,2048]{2,1,0:T(1,128)S(1)}, f32[4,1,2048]{2,1,0:T(1,128)S(1)}, u32[]{:S(2)}, u32[]{:S(2)}) collective-permute-start(f32[4,1,2048]{2,1,0:T(1,128)S(1)} %get-tuple-element.11), channel_id=1, source_target_pairs={{0,1},{1,2},{2,3},{3,4},{4,5},{5,6},{6,7},{8,9},{9,10},{10,11},{11... | collective-permute-start | bytes 98312 | tf_op jit(solution)/shard_map/ppermute | solution.py:17
  53.0 7.7 %collective-permute-start.10 = (f32[1,16,2048]{2,1,0:T(8,128)S(1)}, f32[1,16,2048]{2,1,0:T(8,128)S(1)}, u32[]{:S(2)}, u32[]{:S(2)}) collective-permute-start(f32[1,16,2048]{2,1,0:T(8,128)S(1)} %get-tuple-element.12), channel_id=1, source_target_pairs={{0,8},{8,16},{16,24},{1,9},{9,17},{17,25},{2,10},{10,18},{18,26},{... | collective-permute-start | bytes 393224 | tf_op jit(solution)/shard_map/ppermute | solution.py:17
  57.2 8.2 %collective-permute-start.11 = (f32[1,16,2048]{2,1,0:T(8,128)S(1)}, f32[1,16,2048]{2,1,0:T(8,128)S(1)}, u32[]{:S(2)}, u32[]{:S(2)}) collective-permute-start(f32[1,16,2048]{2,1,0:T(8,128)S(1)} %get-tuple-element.13), channel_id=1, source_target_pairs={{8,0},{16,8},{24,16},{9,1},{17,9},{25,17},{10,2},{18,10},{26,18},{... | collective-permute-start | bytes 393224 | tf_op jit(solution)/shard_map/ppermute | solution.py:19
Sparse Core Ops, SparseCore 0:
  59.4 24.9 reduce-scatter.1
where the time goes:
time: 91.7 us; the launch traced here: 91.3 us
  waiting for transfers between devices  30.9 us (34%)
  starting transfers between devices  28.5 us (31%)
  between operations  14.3 us (16%)
  blocking collectives  10.5 us (11%)
  local copies, waits for them, and re-layouts  4.31 us (5%)
  other arithmetic  2.77 us (3%)
    ppermute x6, starting transfers between devices, extended(): lax.ppermute(tail, axis, [(i, (i + 1) % count) for i in range(ends)])  20.6 us
    reduce_scatter x1, waiting for transfers between devices, body(): lax.psum_scatter(product_sum, 'tm', scatter_dimension=1, tiled=True)  17.8 us
    all_gather x1, blocking collectives, body(): range_rows = lax.all_gather(range_field, 'tm', axis=1, tiled=True)  10.5 us
    ppermute x6, waiting for transfers between devices, extended(): lax.ppermute(head, axis, [((i + 1) % count, i) for i in range(ends)])  9.42 us
    ppermute x6, starting transfers between devices, extended(): lax.ppermute(head, axis, [((i + 1) % count, i) for i in range(ends)])  7.88 us
    ppermute x6, waiting for transfers between devices, extended(): lax.ppermute(tail, axis, [(i, (i + 1) % count) for i in range(ends)])  3.69 us
    slice x6, local copies, waits for them, and re-layouts, stencil(): longitude = jnp.roll(field, 1, 2) + jnp.roll(field, -1, 2)  2.04 us
  transfers between devices with their start and end apart: 13, of which 5 were waited for; matrix products, arithmetic and copies ran while one was open for 5% of the time, Pallas kernels for 0%

commit v1 on v0

v1 whole, which is shorter than its diff:
```python
import functools
import math

import jax
import jax.numpy as jnp
from jax import lax
from jax.experimental import pallas as pl
from jax.experimental.pallas import tpu as pltpu
from jax.sharding import PartitionSpec as P

F32 = jnp.float32
LANES = 128
SLICES = 4
HELD = 24


def step_weights():
    centre_value = 6.525
    spread_value = 6.475
    root_order = (3, 0, 2, 1)
    return [
        1.0 / (centre_value + spread_value * math.cos(math.pi * (2 * section + 1) / 8.0))
        for section in root_order
    ]


W0, W1, W2, W3 = step_weights()


def even_pairs(count):
    return [(i, i ^ 1) for i in range(count)]


def odd_pairs(count):
    return [(i, (i + 1) % count if i % 2 else (i - 1) % count) for i in range(count)]


def shape_of(*dims):
    return jax.ShapeDtypeStruct(dims, F32)


def call(kernel, outs, *args, scratch=()):
    spec = pl.BlockSpec(memory_space=pltpu.VMEM)
    many = isinstance(outs, (list, tuple))
    return pl.pallas_call(
        kernel,
        out_shape=outs,
        in_specs=[spec] * len(args),
        out_specs=[spec] * len(outs) if many else spec,
        scratch_shapes=scratch,
        compiler_params=pltpu.CompilerParams(vmem_limit_bytes=12 << 20),
    )(*args)


def each_tile(width, work):
    def step(tile, carry):
        work(tile, pl.ds(pl.multiple_of(tile * LANES, LANES), LANES))
        return carry

    lax.fori_loop(0, width // LANES, step, 0)


def iota(rows, dim):
    return lax.broadcasted_iota(jnp.int32, (rows, LANES), dim)


def down(cells, by):
    return pltpu.roll(cells, by, 0)


def around(ref, index, tile, tiles):
    def cols(at):
        return pl.ds(pl.multiple_of(at * LANES, LANES), LANES)

    cells = ref[index, :, cols(tile)]
    before = ref[index, :, cols(lax.rem(tile + tiles - 1, tiles))]
    after = ref[index, :, cols(lax.rem(tile + 1, tiles))]
    lane = iota(HELD, 1)
    west = pltpu.roll(jnp.where(lane == LANES - 1, before, cells), 1, 1)
    east = pltpu.roll(jnp.where(lane == 0, after, cells), LANES - 1, 1)
    return cells, west + east + (down(cells, 1) + down(cells, HELD - 1))


def places(tm_count):
    t = lax.axis_index("tm")
    odd = lax.rem(t, 2)
    open_side = jnp.where(odd == 1, t < tm_count - 1, t > 0).astype(F32)
    return t, odd, open_side


def mirrored(odd, j):
    return jnp.where(odd == 1, SLICES - 1 - j, j)


def lat_mask(lat_count):
    l = lax.axis_index("lat")
    row = iota(HELD, 0)
    below = (l < lat_count - 1).astype(F32)
    above = (l > 0).astype(F32)
    return jnp.where(row < HELD - 8, 1.0, jnp.where(row < HELD - 4, below, above))


def first_kernel(forward, cot, rng, own, e1, o1, e2, o2):
    _, odd, _ = places(2)
    rows, width = cot.shape[1:]
    chunk = rng.shape[1]
    blocks = width // chunk
    for j in range(SLICES):
        own[j] = cot[pl.ds(mirrored(odd, j), 1)][0]
    for out, j in ((e1, SLICES - 1), (o1, 0)):
        for b in range(blocks):
            out[b * rows : (b + 1) * rows] = own[j, :, b * chunk : (b + 1) * chunk]
        out[blocks * rows :] = rng[...]
    for out, js in ((e2, (SLICES - 2, SLICES - 3)), (o2, (1, 2))):
        for i, j in enumerate(js[: 1 if forward else 2]):
            out[i * rows : (i + 1) * rows] = own[j]


def slab(ref, tile, rows, chunk):
    per = chunk // LANES
    at = pl.multiple_of(lax.div(tile, per) * rows, rows)
    cols = pl.ds(pl.multiple_of(lax.rem(tile, per) * LANES, LANES), LANES)
    return ref[pl.ds(at, rows), cols]


def rows_kernel(forward, own, e1, o1, *refs):
    rows, width = own.shape[1:]
    chunk = e1.shape[1]
    blocks = width // chunk
    if forward:
        rng, far, la, lb, full = refs
        t, _, _ = places(2)
        for piece, owner in (
            (rng[...], t),
            (e1[blocks * rows :], t ^ 1),
            (far[...], t ^ 2),
            (o1[blocks * rows :], t ^ 3),
        ):
            full[:, pl.ds(pl.multiple_of(owner * chunk, chunk), chunk)] = piece
    else:
        gathered, la, lb, full = refs
        full[...] = gathered[...]
    even = lax.rem(lax.axis_index("lat"), 2) == 0
    sub = iota(8, 0)

    def work(tile, cols):
        cells = [own[j, :, cols] for j in range(SLICES)]
        near_e = slab(e1, tile, rows, chunk)
        near_o = slab(o1, tile, rows, chunk)
        field = full[:, cols]

        def low(x):
            return x[:8]

        def high(x):
            return x[rows - 8 :]

        first = (
            jnp.where(sub < 4, low(cells[0]), down(low(cells[1]), 5)),
            jnp.where(sub < 4, low(cells[2]), down(low(cells[3]), 5)),
            jnp.where(sub < 2, low(near_e), jnp.where(sub < 4, down(low(near_o), 2), down(low(field), 4))),
        )
        last = (
            jnp.where(sub >= 4, high(cells[0]), down(high(cells[1]), 3)),
            jnp.where(sub >= 4, high(cells[2]), down(high(cells[3]), 3)),
            jnp.where(sub >= 6, high(near_e), jnp.where(sub >= 4, down(high(near_o), 6), down(high(field), 4))),
        )
        for i in range(3):
            la[i * 8 : i * 8 + 8, cols] = jnp.where(even, last[i], first[i])
            lb[i * 8 : i * 8 + 8, cols] = jnp.where(even, first[i], last[i])

    each_tile(width, work)


def main_kernel(counts, own, e1, o1, full, la, lb, its, u, a3, q, part, grad, rr):
    tm_count, lat_count = counts
    _, odd, open_side = places(tm_count)
    rows, width = own.shape[1:]
    chunk = e1.shape[1]
    tiles = width // LANES
    mask = lat_mask(lat_count)
    even = lax.rem(lax.axis_index("lat"), 2) == 0
    sub = iota(8, 0)

    def gather(tile, cols):
        def joined(body, below, above):
            edge = jnp.where(sub < 4, below, above) * mask[rows:]
            return jnp.concatenate([body, edge], axis=0)

        below = [jnp.where(even, la[i : i + 8, cols], lb[i : i + 8, cols]) for i in (0, 8, 16)]
        above = [jnp.where(even, lb[i : i + 8, cols], la[i : i + 8, cols]) for i in (0, 8, 16)]
        for i in range(2):
            u[1 + 2 * i, :, cols] = joined(own[2 * i, :, cols], below[i], above[i])
            u[2 + 2 * i, :, cols] = joined(own[2 * i + 1, :, cols], down(below[i], 3), down(above[i], 5))
        near_o = joined(slab(o1, tile, rows, chunk), down(below[2], 6), down(above[2], 2))
        u[0, :, cols] = near_o * open_side
        u[SLICES + 1, :, cols] = joined(slab(e1, tile, rows, chunk), below[2], above[2])
        edge = jnp.where(sub < 4, down(below[2], 4), down(above[2], 4))
        rr[:, cols] = jnp.concatenate([full[:, cols], edge], axis=0) + 6.0

    each_tile(width, gather)

    def third(tile, cols):
        keep = (1.0 - W3 * rr[:, cols]) * mask
        pull = W3 * mask
        cells, sums = [], []
        for i in range(SLICES + 2):
            c, s = around(u, i, tile, tiles)
            cells.append(c)
            sums.append(s)
        for i in range(SLICES + 2):
            s = sums[i]
            if i > 0:
                s = s + cells[i - 1]
            if i < SLICES + 1:
                s = s + cells[i + 1]
            out = keep * cells[i] + pull * s
            a3[i, :, cols] = out * open_side if i == 0 else out

    each_tile(width, third)

    def second(tile, cols):
        keep = (1.0 - W2 * rr[:, cols]) * mask
        pull = W2 * mask
        cells = [a3[i, :, cols] for i in range(SLICES + 2)]
        total = jnp.zeros((rows, LANES), F32)
        for j in range(SLICES):
            c, s = around(a3, j + 1, tile, tiles)
            out = keep * c + pull * (s + cells[j] + cells[j + 2])
            q[j, :, cols] = out
            at = mirrored(odd, j)
            now, mid, start = out[:rows], c[:rows], u[j + 1, :rows, cols]
            part[j, :, cols] = W1 * now + W2 * mid + W3 * start
            x1, x2, x3 = (its[k, pl.ds(at, 1), :, cols][0] for k in range(3))
            total = total - (W3 * start * x3 + W2 * mid * x2 + W1 * now * x1)
        grad[:, cols] = total

    each_tile(width, second)


def late_kernel(tm_count, forward, grad, e2, o2, its, *refs):
    _, odd, open_side = places(tm_count)
    rows, width = grad.shape
    if forward:
        mine, g1, g2, g3, passed, total = refs
    else:
        (total,) = refs
    scale = -W1 * W2 * W3

    def work(tile, cols):
        x_o = its[0, pl.ds(mirrored(odd, 0), 1), :, cols][0]
        x_e = its[0, pl.ds(mirrored(odd, SLICES - 1), 1), :, cols][0]
        far_e, far_o = e2[:rows, cols], o2[:rows, cols]
        total[:, cols] = grad[:, cols] + scale * (far_e * x_e + far_o * open_side * x_o)
        if forward:
            passed[0, :, cols] = far_e
            passed[1, :, cols] = far_o

    each_tile(width, work)
    if forward:
        t = lax.axis_index("tm")
        chunk = mine.shape[1]
        for out, owner in ((mine, t), (g1, t ^ 1), (g2, t ^ 2), (g3, t ^ 3)):
            out[...] = total[:, pl.ds(pl.multiple_of(owner * chunk, chunk), chunk)]


def corner_kernel(e2, o2, la, lb):
    rows = 16
    width = la.shape[1]
    even = lax.rem(lax.axis_index("lat"), 2) == 0
    sub = iota(8, 0)

    def work(tile, cols):
        far_e, far_o = e2[:rows, cols], o2[:rows, cols]
        first = jnp.where(sub < 1, far_e[:8], down(far_o[:8], 1))
        last = jnp.where(sub >= 7, far_e[rows - 8 :], down(far_o[rows - 8 :], 7))
        la[:, cols] = jnp.where(even, last, first)
        lb[:, cols] = jnp.where(even, first, last)

    each_tile(width, work)


def last_kernel(counts, forward, u, a3, q, part, rr, e2, o2, *refs):
    tm_count, lat_count = counts
    if forward:
        passed, la, lb, noise, far, near, edge = refs
    else:
        la, lb, noise, far, near, edge = refs
    _, odd, open_side = places(tm_count)
    rows, width = part.shape[1:]
    tiles = width // LANES
    mask = lat_mask(lat_count)
    even = lax.rem(lax.axis_index("lat"), 2) == 0
    sub = iota(8, 0)

    def gather(tile, cols):
        below = jnp.where(even, la[:, cols], lb[:, cols])
        above = jnp.where(even, lb[:, cols], la[:, cols])

        def joined(body, below, above):
            return jnp.concatenate([body, jnp.where(sub < 4, below, above) * mask[rows:]], axis=0)

        far_o = joined(o2[:rows, cols], down(below, 7), down(above, 1)) * open_side
        far_e = joined(e2[:rows, cols], below, above)
        for i, cells, near_at, edge_at in ((0, far_o, 0, 0), (1, far_e, SLICES + 1, SLICES - 1)):
            far[i, :, cols] = cells
            near[i, :, cols] = a3[near_at, :, cols] + W3 * cells
            edge[i, :, cols] = q[edge_at, :, cols] + (W2 * W3) * cells

    each_tile(width, gather)

    def work(tile, cols):
        field = rr[:, cols]
        beyond = []
        for i in range(2):
            if forward:
                ends = passed[i, :, cols]
            else:
                ends = (o2, e2)[i][rows : 2 * rows, cols]
            c, s = around(far, i, tile, tiles)
            s = s[:rows] + u[(SLICES + 1) * i, :rows, cols] + ends
            third = (1.0 - W3 * field[:rows]) * c[:rows] + W3 * s
            c, s = around(near, i, tile, tiles)
            s = s[:rows] + third + a3[1 + (SLICES - 1) * i, :rows, cols]
            second = (1.0 - W2 * field[:rows]) * c[:rows] + W2 * s
            beyond.append(second * open_side if i == 0 else second)
        keep = 1.0 - W1 * field[:rows]
        cells, sums = [], []
        for j in range(SLICES):
            if j in (0, SLICES - 1):
                c, s = around(edge, min(j, 1), tile, tiles)
            else:
                c, s = around(q, j, tile, tiles)
            cells.append(c[:rows])
            sums.append(s[:rows])
        cells = [beyond[0], *cells, beyond[1]]
        for j in range(SLICES):
            s = sums[j] + cells[j] + cells[j + 2]
            first = keep * cells[j + 1] + W1 * s
            out = part[j, :, cols] + W0 * first
            if j in (0, SLICES - 1):
                out = out + (W1 * W2 * W3) * far[min(j, 1), :rows, cols]
            noise[pl.ds(mirrored(odd, j), 1), :, cols] = out[None]

    each_tile(width, work)


def body(counts, cotangent, iterates, range_field):
    tm_count, lat_count = counts
    forward = tm_count == 4
    slices, rows, width = cotangent.shape
    chunk = range_field.shape[1]
    assert slices == SLICES and rows == HELD - 8
    even, odd = even_pairs(tm_count), odd_pairs(tm_count)
    lat_even, lat_odd = even_pairs(lat_count), odd_pairs(lat_count)
    y_pairs = [(i, i ^ 2) for i in range(tm_count)]

    message = (width // chunk + 1) * rows
    deep = rows if forward else 2 * rows
    own, e1, o1, e2, o2 = call(
        functools.partial(first_kernel, forward),
        [shape_of(slices, rows, width)]
        + [shape_of(message, chunk)] * 2
        + [shape_of(deep, width)] * 2,
        cotangent,
        range_field,
    )
    e1 = lax.ppermute(e1, "tm", even)
    o1 = lax.ppermute(o1, "tm", odd)
    if forward:
        field = (range_field, lax.ppermute(range_field, "tm", y_pairs))
    else:
        field = (lax.all_gather(range_field, "tm", axis=1, tiled=True),)
    e2 = lax.ppermute(e2, "tm", even)
    o2 = lax.ppermute(o2, "tm", odd)

    la, lb, full = call(
        functools.partial(rows_kernel, forward),
        [shape_of(24, width)] * 2 + [shape_of(rows, width)],
        own,
        e1,
        o1,
        *field,
    )
    la = lax.ppermute(la, "lat", lat_even)
    lb = lax.ppermute(lb, "lat", lat_odd)

    held = shape_of(SLICES + 2, HELD, width)
    u, a3, q, part, grad, rr = call(
        functools.partial(main_kernel, counts),
        [
            held,
            held,
            shape_of(SLICES, HELD, width),
            shape_of(SLICES, rows, width),
            shape_of(rows, width),
            shape_of(HELD, width),
        ],
        own,
        e1,
        o1,
        full,
        la,
        lb,
        iterates,
    )
    if forward:
        mine, g1, g2, g3, passed = call(
            functools.partial(late_kernel, tm_count, True),
            [shape_of(rows, chunk)] * 4 + [shape_of(2, rows, width)],
            grad,
            e2,
            o2,
            iterates,
            scratch=[pltpu.VMEM((rows, width), F32)],
        )
        g1 = lax.ppermute(g1, "tm", even)
        g2 = lax.ppermute(g2, "tm", y_pairs)
        g3 = lax.ppermute(g3, "tm", odd)
        gradient = (mine + g1) + (g2 + g3)
        extra = (lax.ppermute(passed, "tm", y_pairs),)
    else:
        total = call(
            functools.partial(late_kernel, tm_count, False),
            shape_of(rows, width),
            grad,
            e2,
            o2,
            iterates,
        )
        gradient = lax.psum_scatter(total, "tm", scatter_dimension=1, tiled=True)
        extra = ()
    la, lb = call(corner_kernel, [shape_of(8, width)] * 2, e2, o2)
    la = lax.ppermute(la, "lat", lat_even)
    lb = lax.ppermute(lb, "lat", lat_odd)
    noise = call(
        functools.partial(last_kernel, counts, forward),
        shape_of(SLICES, rows, width),
        u,
        a3,
        q,
        part,
        rr,
        e2,
        o2,
        *extra,
        la,
        lb,
        scratch=[pltpu.VMEM((2, HELD, width), F32)] * 3,
    )
    return noise, gradient


def solution(mesh):
    counts = (mesh.shape["tm"], mesh.shape["lat"])
    return jax.shard_map(
        functools.partial(body, counts),
        mesh=mesh,
        in_specs=(P("tm", "lat", None), P(None, "tm", "lat", None), P("lat", "tm")),
        out_specs=(P("tm", "lat", None), P("lat", "tm")),
        check_vma=False,
    )
```

time: 91.7 us -> 42 us (0.46)
  waiting for transfers between devices: 30.9 us -> 14.8 us
  between operations: 14.3 us -> 0.73 us
  starting transfers between devices: 28.5 us -> 15.2 us
  blocking collectives: 10.5 us -> 0 us
  Pallas kernels: 0 us -> 7.3 us
  other arithmetic: 2.77 us -> 0.63 us
  local copies, waits for them, and re-layouts: 4.31 us -> 3.2 us
    reduce_scatter x1 -> x0, waiting for transfers between devices: 17.8 us -> none  [body(): lax.psum_scatter(product_sum, 'tm', scatter_dimension=1, tiled=True)]
    ppermute x12 -> x13, starting transfers between devices: 28.5 us -> 15.2 us  [the longest x2 4.46 us: body(): lb = lax.ppermute(lb, 'lat', lat_odd)]
    all_gather x1 -> x0, blocking collectives: 10.5 us -> none  [body(): range_rows = lax.all_gather(range_field, 'tm', axis=1, tiled=True)]
    pallas_call x0 -> x6, Pallas kernels: none -> 7.3 us  [call(): pl.pallas_call(kernel, out_shape=outs, in_specs=[spec] * len(args), out_s...]
    slice x12 -> x0, local copies, waits for them, and re-layouts: 4.29 us -> none  [the longest x6 2.04 us: stencil(): longitude = jnp.roll(field, 1, 2) + jnp.roll(field, -1, 2)]
    unnamed x6 -> x8, local copies, waits for them, and re-layouts: 0.02 us -> 3.2 us
    ppermute x12 -> x13, waiting for transfers between devices: 13.1 us -> 14.8 us  [the longest x1 4.21 us: body(): field = (range_field, lax.ppermute(range_field, 'tm', y_pairs))]
    add x3 -> x1, other arithmetic: 1.93 us -> 0.63 us  [body(): gradient = mine + g1 + (g2 + g3)]
  transfers between devices with their start and end apart: 13 -> 13, of which waited for: 5 -> 6; matrix products, arithmetic and copies ran while one was open for 5% -> 1% of each run, Pallas kernels for 0% -> 9%
where the time goes in v1:
time: 42 us; the launch traced here: 41.8 us
  starting transfers between devices  15.2 us (36%)
  waiting for transfers between devices  14.8 us (35%)
  Pallas kernels  7.3 us (17%)
  local copies, waits for them, and re-layouts  3.2 us (8%)
  between operations  0.73 us (2%)
  other arithmetic  0.63 us (2%)
    pallas_call x6, Pallas kernels, call(): pl.pallas_call(kernel, out_shape=outs, in_specs=[spec] * len(args), out_s...  7.3 us
    ppermute x2, starting transfers between devices, body(): lb = lax.ppermute(lb, 'lat', lat_odd)  4.46 us
    ppermute x1, waiting for transfers between devices, body(): field = (range_field, lax.ppermute(range_field, 'tm', y_pairs))  4.21 us
    ppermute x2, waiting for transfers between devices, body(): lb = lax.ppermute(lb, 'lat', lat_odd)  3.75 us
    unnamed x8, local copies, waits for them, and re-layouts  3.2 us
    ppermute x1, waiting for transfers between devices, body(): o1 = lax.ppermute(o1, 'tm', odd)  3.16 us
    ppermute x1, waiting for transfers between devices, body(): g2 = lax.ppermute(g2, 'tm', y_pairs)  3.14 us
    ppermute x1, starting transfers between devices, body(): e1 = lax.ppermute(e1, 'tm', even)  3 us
  transfers between devices with their start and end apart: 13, of which 6 were waited for; matrix products, arithmetic and copies ran while one was open for 1% of the time, Pallas kernels for 9%

profile of v1, /device:TPU:0, one launch (start us, length us, event | category | flops | bytes accessed | tf_op | source)
XLA Modules:
  0.0 41.8 jit_solution(13420504110393727820)
XLA Ops:
  0.6 1.0 %copy-done.2 = f32[4,16,2048]{2,1,0:T(8,128)S(1)} copy-done((f32[4,16,2048]{2,1,0:T(8,128)S(1)}, f32[4,16,2048]{2,1,0:T(8,128)}, u32[]{:S(2)}) %copy-start.2) | copy-done | bytes 524312
  1.7 0.8 %copy-done.3 = f32[16,512]{1,0:T(8,128)S(1)} copy-done((f32[16,512]{1,0:T(8,128)S(1)}, f32[16,512]{1,0:T(8,128)}, u32[]{:S(2)}) %copy-start.3) | copy-done | bytes 32792
  2.4 0.1 shard_map.50
  2.5 3.0 %collective-permute-start = (f32[80,512]{1,0:T(8,128)S(1)}, f32[80,512]{1,0:T(8,128)S(1)}, u32[]{:S(2)}, u32[]{:S(2)}) collective-permute-start(f32[80,512]{1,0:T(8,128)S(1)} %get-tuple-element.24), channel_id=1, source_target_pairs={{0,8},{8,0},{16,24},{24,16},{1,9},{9,1},{17,25},{25,17},{2,10},{10... | collective-permute-start | bytes 491528 | tf_op jit(solution)/shard_map/ppermute | solution.py:368
  5.5 1.5 %collective-permute-start.1 = (f32[80,512]{1,0:T(8,128)S(1)}, f32[80,512]{1,0:T(8,128)S(1)}, u32[]{:S(2)}, u32[]{:S(2)}) collective-permute-start(f32[80,512]{1,0:T(8,128)S(1)} %get-tuple-element.25), channel_id=1, source_target_pairs={{0,24},{8,16},{16,8},{24,0},{1,25},{9,17},{17,9},{25,1},{2,26},{10... | collective-permute-start | bytes 491528 | tf_op jit(solution)/shard_map/ppermute | solution.py:369
  7.0 0.1 collective-permute-start.2
  7.1 4.2 %collective-permute-done.2.refs_1_ = f32[16,512]{1,0:T(8,128)S(1)} collective-permute-done((f32[16,512]{1,0:T(8,128)S(1)}, f32[16,512]{1,0:T(8,128)S(1)}, u32[]{:S(2)}, u32[]{:S(2)}) %collective-permute-start.2) | collective-permute-done | bytes 32800 | tf_op jit(solution)/shard_map/ppermute | solution.py:371
  11.3 0.0 collective-permute-done.e1
  11.3 3.2 %collective-permute-done.1.o1 = f32[80,512]{1,0:T(8,128)S(1)} collective-permute-done((f32[80,512]{1,0:T(8,128)S(1)}, f32[80,512]{1,0:T(8,128)S(1)}, u32[]{:S(2)}, u32[]{:S(2)}) %collective-permute-start.1) | collective-permute-done | bytes 163872 | tf_op jit(solution)/shard_map/ppermute | solution.py:369
  14.4 0.2 shard_map.51
  14.6 0.1 collective-permute-start.3
  14.7 3.7 %collective-permute-start.4 = (f32[24,2048]{1,0:T(8,128)S(1)}, f32[24,2048]{1,0:T(8,128)S(1)}, u32[]{:S(2)}, u32[]{:S(2)}) collective-permute-start(f32[24,2048]{1,0:T(8,128)S(1)} %get-tuple-element.28), channel_id=1, source_target_pairs={{0,7},{1,2},{2,1},{3,4},{4,3},{5,6},{6,5},{7,0},{8,15},{9,10},{10,... | collective-permute-start | bytes 589832 | tf_op jit(solution)/shard_map/ppermute | solution.py:386
  18.4 1.5 %collective-permute-start.5 = (f32[16,2048]{1,0:T(8,128)S(1)}, f32[16,2048]{1,0:T(8,128)S(1)}, u32[]{:S(2)}, u32[]{:S(2)}) collective-permute-start(f32[16,2048]{1,0:T(8,128)S(1)} %get-tuple-element.34), channel_id=1, source_target_pairs={{0,8},{8,0},{16,24},{24,16},{1,9},{9,1},{17,25},{25,17},{2,10},{10... | collective-permute-start | bytes 393224 | tf_op jit(solution)/shard_map/ppermute | solution.py:374
  19.9 0.5 %collective-permute-start.6 = (f32[16,2048]{1,0:T(8,128)S(1)}, f32[16,2048]{1,0:T(8,128)S(1)}, u32[]{:S(2)}, u32[]{:S(2)}) collective-permute-start(f32[16,2048]{1,0:T(8,128)S(1)} %get-tuple-element.35), channel_id=1, source_target_pairs={{0,24},{8,16},{16,8},{24,0},{1,25},{9,17},{17,9},{25,1},{2,26},{10... | collective-permute-start | bytes 393224 | tf_op jit(solution)/shard_map/ppermute | solution.py:375
  20.4 0.0 collective-permute-done.3.la
  20.4 2.8 %collective-permute-done.4.lb = f32[24,2048]{1,0:T(8,128)S(1)} collective-permute-done((f32[24,2048]{1,0:T(8,128)S(1)}, f32[24,2048]{1,0:T(8,128)S(1)}, u32[]{:S(2)}, u32[]{:S(2)}) %collective-permute-start.4) | collective-permute-done | bytes 196640 | tf_op jit(solution)/shard_map/ppermute | solution.py:386
  23.2 1.4 %copy-done = f32[3,4,16,2048]{3,2,1,0:T(8,128)S(1)} copy-done((f32[3,4,16,2048]{3,2,1,0:T(8,128)S(1)}, f32[3,4,16,2048]{3,2,1,0:T(8,128)}, u32[]{:S(2)}) %copy-start) | copy-done | bytes 1572888
  24.6 3.8 %shard_map.52 = (f32[6,24,2048]{2,1,0:T(8,128)S(1)}, f32[6,24,2048]{2,1,0:T(8,128)S(1)}, f32[4,24,2048]{2,1,0:T(8,128)S(1)}, f32[4,16,2048]{2,1,0:T(8,128)S(1)},...) custom-call(f32[4,16,2048]{2,1,0:T(8,128)S(1)} %get-tuple-element.23.own, f32[80,512]{1,0:T(8,128)S(1)} %collective-permute-done.e1, ...), custom_call_target="tpu_custom_call" | custom-call | tf_op jit(solution)/shard_map/pallas_call | solution.py:45
  28.4 0.0 collective-permute-done.5.e2
  28.4 0.2 shard_map.53
  28.7 0.6 %collective-permute-start.7 = (f32[2,16,2048]{2,1,0:T(8,128)S(1)}, f32[2,16,2048]{2,1,0:T(8,128)S(1)}, u32[]{:S(2)}, u32[]{:S(2)}) collective-permute-start(f32[2,16,2048]{2,1,0:T(8,128)S(1)} %get-tuple-element.37), channel_id=1, source_target_pairs={{0,16},{8,24},{16,0},{24,8},{1,17},{9,25},{17,1},{25,9},{2,18},{10... | collective-permute-start | bytes 786440 | tf_op jit(solution)/shard_map/ppermute | solution.py:421
  29.2 1.5 %collective-permute-start.10 = (f32[16,512]{1,0:T(8,128)S(1)}, f32[16,512]{1,0:T(8,128)S(1)}, u32[]{:S(2)}, u32[]{:S(2)}) collective-permute-start(f32[16,512]{1,0:T(8,128)S(1)} %get-tuple-element.41), channel_id=1, source_target_pairs={{0,8},{8,0},{16,24},{24,16},{1,9},{9,1},{17,25},{25,17},{2,10},{10... | collective-permute-start | bytes 98312 | tf_op jit(solution)/shard_map/ppermute | solution.py:417
  30.7 1.5 %collective-permute-start.11 = (f32[16,512]{1,0:T(8,128)S(1)}, f32[16,512]{1,0:T(8,128)S(1)}, u32[]{:S(2)}, u32[]{:S(2)}) collective-permute-start(f32[16,512]{1,0:T(8,128)S(1)} %get-tuple-element.42), channel_id=1, source_target_pairs={{0,16},{8,24},{16,0},{24,8},{1,17},{9,25},{17,1},{25,9},{2,18},{10... | collective-permute-start | bytes 98312 | tf_op jit(solution)/shard_map/ppermute | solution.py:418
  32.3 0.5 %collective-permute-start.12 = (f32[16,512]{1,0:T(8,128)S(1)}, f32[16,512]{1,0:T(8,128)S(1)}, u32[]{:S(2)}, u32[]{:S(2)}) collective-permute-start(f32[16,512]{1,0:T(8,128)S(1)} %get-tuple-element.43), channel_id=1, source_target_pairs={{0,24},{8,16},{16,8},{24,0},{1,25},{9,17},{17,9},{25,1},{2,26},{10... | collective-permute-start | bytes 98312 | tf_op jit(solution)/shard_map/ppermute | solution.py:419
  32.7 0.1 shard_map.54
  32.8 0.1 collective-permute-start.8
  32.9 0.5 %collective-permute-done.10 = f32[16,512]{1,0:T(8,128)S(1)} collective-permute-done((f32[16,512]{1,0:T(8,128)S(1)}, f32[16,512]{1,0:T(8,128)S(1)}, u32[]{:S(2)}, u32[]{:S(2)}) %collective-permute-start.10) | collective-permute-done | bytes 32800 | tf_op jit(solution)/shard_map/ppermute | solution.py:417
  33.4 0.8 %collective-permute-start.9 = (f32[8,2048]{1,0:T(8,128)S(1)}, f32[8,2048]{1,0:T(8,128)S(1)}, u32[]{:S(2)}, u32[]{:S(2)}) collective-permute-start(f32[8,2048]{1,0:T(8,128)S(1)} %get-tuple-element.39), channel_id=1, source_target_pairs={{0,7},{1,2},{2,1},{3,4},{4,3},{5,6},{6,5},{7,0},{8,15},{9,10},{10,... | collective-permute-start | bytes 196616 | tf_op jit(solution)/shard_map/ppermute | solution.py:435
  34.2 3.1 %collective-permute-done.11 = f32[16,512]{1,0:T(8,128)S(1)} collective-permute-done((f32[16,512]{1,0:T(8,128)S(1)}, f32[16,512]{1,0:T(8,128)S(1)}, u32[]{:S(2)}, u32[]{:S(2)}) %collective-permute-start.11) | collective-permute-done | bytes 32800 | tf_op jit(solution)/shard_map/ppermute | solution.py:418
  37.3 0.6 %add_add_fusion = f32[16,512]{1,0:T(8,128)} fusion(f32[16,512]{1,0:T(8,128)S(1)} %collective-permute-done.11, f32[16,512]{1,0:T(8,128)S(1)} %collective-permute-done.12, f32[16,512]{1,0:T(8,128)S(1)} %get-tuple-element.40, f32[16,512]{1,0:T(8,128)S(1)} %collective-permute-done.10), kind=kLoop, calls=%fused_computation | loop fusion | flops 24576 | bytes 163840 | tf_op jit(solution)/shard_map/add | solution.py:420
  37.9 1.0 %collective-permute-done.9.refs_2_ = f32[8,2048]{1,0:T(8,128)S(1)} collective-permute-done((f32[8,2048]{1,0:T(8,128)S(1)}, f32[8,2048]{1,0:T(8,128)S(1)}, u32[]{:S(2)}, u32[]{:S(2)}) %collective-permute-start.9) | collective-permute-done | bytes 65568 | tf_op jit(solution)/shard_map/ppermute | solution.py:435
  38.9 2.9 %shard_map.55 = f32[4,16,2048]{2,1,0:T(8,128)} custom-call(f32[6,24,2048]{2,1,0:T(8,128)S(1)} %get-tuple-element.29.u, f32[6,24,2048]{2,1,0:T(8,128)S(1)} %get-tuple-element.30.a3, f32[4,24,2048]{2,1,0:T(8,128)S(1)} %get-tuple-element.31.q, f32[4,16,2048]{2,1,0:T(8,128)S(1)} %get-tuple-element.32.part, f32[24,2048]{1,0:T(8,128)S(1)} %get-tuple-element.33.rr, ...), custom_call_target="tpu_custom_call" | custom-call | tf_op jit(solution)/shard_map/pallas_call | solution.py:45
  (9 shorter events, 0.0 us)
Async XLA Ops:
  0.6 1.0 %copy-start.2 = (f32[4,16,2048]{2,1,0:T(8,128)S(1)}, f32[4,16,2048]{2,1,0:T(8,128)}, u32[]{:S(2)}) copy-start(f32[4,16,2048]{2,1,0:T(8,128)} %cot.1) | copy-start | bytes 1572868
  1.7 0.8 %copy-start.3 = (f32[16,512]{1,0:T(8,128)S(1)}, f32[16,512]{1,0:T(8,128)}, u32[]{:S(2)}) copy-start(f32[16,512]{1,0:T(8,128)} %refs_0_.1) | copy-start | bytes 98308
  2.5 8.8 %collective-permute-start = (f32[80,512]{1,0:T(8,128)S(1)}, f32[80,512]{1,0:T(8,128)S(1)}, u32[]{:S(2)}, u32[]{:S(2)}) collective-permute-start(f32[80,512]{1,0:T(8,128)S(1)} %get-tuple-element.24), channel_id=1, source_target_pairs={{0,8},{8,0},{16,24},{24,16},{1,9},{9,1},{17,25},{25,17},{2,10},{10... | collective-permute-start | bytes 491528 | tf_op jit(solution)/shard_map/ppermute | solution.py:368
  5.5 8.9 %collective-permute-start.1 = (f32[80,512]{1,0:T(8,128)S(1)}, f32[80,512]{1,0:T(8,128)S(1)}, u32[]{:S(2)}, u32[]{:S(2)}) collective-permute-start(f32[80,512]{1,0:T(8,128)S(1)} %get-tuple-element.25), channel_id=1, source_target_pairs={{0,24},{8,16},{16,8},{24,0},{1,25},{9,17},{17,9},{25,1},{2,26},{10... | collective-permute-start | bytes 491528 | tf_op jit(solution)/shard_map/ppermute | solution.py:369
  7.0 4.3 %collective-permute-start.2 = (f32[16,512]{1,0:T(8,128)S(1)}, f32[16,512]{1,0:T(8,128)S(1)}, u32[]{:S(2)}, u32[]{:S(2)}) collective-permute-start(f32[16,512]{1,0:T(8,128)S(1)} %copy-done.3), channel_id=1, source_target_pairs={{0,16},{8,24},{16,0},{24,8},{1,17},{9,25},{17,1},{25,9},{2,18},{10... | collective-permute-start | bytes 98312 | tf_op jit(solution)/shard_map/ppermute | solution.py:371
  14.6 5.8 %collective-permute-start.3 = (f32[24,2048]{1,0:T(8,128)S(1)}, f32[24,2048]{1,0:T(8,128)S(1)}, u32[]{:S(2)}, u32[]{:S(2)}) collective-permute-start(f32[24,2048]{1,0:T(8,128)S(1)} %get-tuple-element.27), channel_id=1, source_target_pairs={{0,1},{1,0},{2,3},{3,2},{4,5},{5,4},{6,7},{7,6},{8,9},{9,8},{10,11... | collective-permute-start | bytes 589832 | tf_op jit(solution)/shard_map/ppermute | solution.py:385
  14.7 8.5 %collective-permute-start.4 = (f32[24,2048]{1,0:T(8,128)S(1)}, f32[24,2048]{1,0:T(8,128)S(1)}, u32[]{:S(2)}, u32[]{:S(2)}) collective-permute-start(f32[24,2048]{1,0:T(8,128)S(1)} %get-tuple-element.28), channel_id=1, source_target_pairs={{0,7},{1,2},{2,1},{3,4},{4,3},{5,6},{6,5},{7,0},{8,15},{9,10},{10,... | collective-permute-start | bytes 589832 | tf_op jit(solution)/shard_map/ppermute | solution.py:386
  18.4 10.0 %collective-permute-start.5 = (f32[16,2048]{1,0:T(8,128)S(1)}, f32[16,2048]{1,0:T(8,128)S(1)}, u32[]{:S(2)}, u32[]{:S(2)}) collective-permute-start(f32[16,2048]{1,0:T(8,128)S(1)} %get-tuple-element.34), channel_id=1, source_target_pairs={{0,8},{8,0},{16,24},{24,16},{1,9},{9,1},{17,25},{25,17},{2,10},{10... | collective-permute-start | bytes 393224 | tf_op jit(solution)/shard_map/ppermute | solution.py:374
  19.9 8.5 %collective-permute-start.6 = (f32[16,2048]{1,0:T(8,128)S(1)}, f32[16,2048]{1,0:T(8,128)S(1)}, u32[]{:S(2)}, u32[]{:S(2)}) collective-permute-start(f32[16,2048]{1,0:T(8,128)S(1)} %get-tuple-element.35), channel_id=1, source_target_pairs={{0,24},{8,16},{16,8},{24,0},{1,25},{9,17},{17,9},{25,1},{2,26},{10... | collective-permute-start | bytes 393224 | tf_op jit(solution)/shard_map/ppermute | solution.py:375
  23.2 1.4 %copy-start = (f32[3,4,16,2048]{3,2,1,0:T(8,128)S(1)}, f32[3,4,16,2048]{3,2,1,0:T(8,128)}, u32[]{:S(2)}) copy-start(f32[3,4,16,2048]{3,2,1,0:T(8,128)} %its.3) | copy-start | bytes 4718596
  24.6 3.8 %copy-start.1 = (f32[3,4,16,2048]{3,2,1,0:T(8,128)S(1)}, f32[3,4,16,2048]{3,2,1,0:T(8,128)}, u32[]{:S(2)}) copy-start(f32[3,4,16,2048]{3,2,1,0:T(8,128)} %its.3) | copy-start | bytes 4718596
  28.7 10.2 %collective-permute-start.7 = (f32[2,16,2048]{2,1,0:T(8,128)S(1)}, f32[2,16,2048]{2,1,0:T(8,128)S(1)}, u32[]{:S(2)}, u32[]{:S(2)}) collective-permute-start(f32[2,16,2048]{2,1,0:T(8,128)S(1)} %get-tuple-element.37), channel_id=1, source_target_pairs={{0,16},{8,24},{16,0},{24,8},{1,17},{9,25},{17,1},{25,9},{2,18},{10... | collective-permute-start | bytes 786440 | tf_op jit(solution)/shard_map/ppermute | solution.py:421
  29.2 4.2 %collective-permute-start.10 = (f32[16,512]{1,0:T(8,128)S(1)}, f32[16,512]{1,0:T(8,128)S(1)}, u32[]{:S(2)}, u32[]{:S(2)}) collective-permute-start(f32[16,512]{1,0:T(8,128)S(1)} %get-tuple-element.41), channel_id=1, source_target_pairs={{0,8},{8,0},{16,24},{24,16},{1,9},{9,1},{17,25},{25,17},{2,10},{10... | collective-permute-start | bytes 98312 | tf_op jit(solution)/shard_map/ppermute | solution.py:417
  30.7 6.6 %collective-permute-start.11 = (f32[16,512]{1,0:T(8,128)S(1)}, f32[16,512]{1,0:T(8,128)S(1)}, u32[]{:S(2)}, u32[]{:S(2)}) collective-permute-start(f32[16,512]{1,0:T(8,128)S(1)} %get-tuple-element.42), channel_id=1, source_target_pairs={{0,16},{8,24},{16,0},{24,8},{1,17},{9,25},{17,1},{25,9},{2,18},{10... | collective-permute-start | bytes 98312 | tf_op jit(solution)/shard_map/ppermute | solution.py:418
  32.3 5.0 %collective-permute-start.12 = (f32[16,512]{1,0:T(8,128)S(1)}, f32[16,512]{1,0:T(8,128)S(1)}, u32[]{:S(2)}, u32[]{:S(2)}) collective-permute-start(f32[16,512]{1,0:T(8,128)S(1)} %get-tuple-element.43), channel_id=1, source_target_pairs={{0,24},{8,16},{16,8},{24,0},{1,25},{9,17},{17,9},{25,1},{2,26},{10... | collective-permute-start | bytes 98312 | tf_op jit(solution)/shard_map/ppermute | solution.py:419
  32.8 5.1 %collective-permute-start.8 = (f32[8,2048]{1,0:T(8,128)S(1)}, f32[8,2048]{1,0:T(8,128)S(1)}, u32[]{:S(2)}, u32[]{:S(2)}) collective-permute-start(f32[8,2048]{1,0:T(8,128)S(1)} %get-tuple-element.38), channel_id=1, source_target_pairs={{0,1},{1,0},{2,3},{3,2},{4,5},{5,4},{6,7},{7,6},{8,9},{9,8},{10,11... | collective-permute-start | bytes 196616 | tf_op jit(solution)/shard_map/ppermute | solution.py:434
  33.4 5.5 %collective-permute-start.9 = (f32[8,2048]{1,0:T(8,128)S(1)}, f32[8,2048]{1,0:T(8,128)S(1)}, u32[]{:S(2)}, u32[]{:S(2)}) collective-permute-start(f32[8,2048]{1,0:T(8,128)S(1)} %get-tuple-element.39), channel_id=1, source_target_pairs={{0,7},{1,2},{2,1},{3,4},{4,3},{5,6},{6,5},{7,0},{8,15},{9,10},{10,... | collective-permute-start | bytes 196616 | tf_op jit(solution)/shard_map/ppermute | solution.py:435

commit v2 on v0

v2 whole, which is shorter than its diff:
```python
import functools
import math

import jax
import jax.numpy as jnp
from jax import lax
from jax.experimental import pallas as pl
from jax.experimental.pallas import tpu as pltpu
from jax.sharding import PartitionSpec as P

F32 = jnp.float32
LANES = 128
SLICES = 4
ROWS = 16
HELD = 24


def step_weights():
    centre_value = 6.525
    spread_value = 6.475
    root_order = (3, 0, 2, 1)
    return [
        1.0 / (centre_value + spread_value * math.cos(math.pi * (2 * section + 1) / 8.0))
        for section in root_order
    ]


W0, W1, W2, W3 = step_weights()
SUM2 = W2 + W3
PROD2 = W2 * W3
COEFFS = (
    W0 + W1 + W2 + W3,
    W0 * (W1 + W2 + W3) + W1 * SUM2 + W2 * W3,
    W0 * (W1 * W2 + W1 * W3 + W2 * W3) + W1 * PROD2,
    W0 * W1 * W2 * W3,
)


def even_pairs(count):
    return [(i, i ^ 1) for i in range(count)]


def odd_pairs(count):
    return [(i, (i + 1) % count if i % 2 else (i - 1) % count) for i in range(count)]


def shape_of(*dims):
    return jax.ShapeDtypeStruct(dims, F32)


IN_PLACE = pl.BlockSpec(memory_space=pltpu.VMEM)
ANYWHERE = pl.BlockSpec(memory_space=pltpu.HBM)


def call(kernel, outs, *args, in_specs=None, out_specs=None, scratch=(), aliases=None, cost=0):
    many = isinstance(outs, (list, tuple))
    return pl.pallas_call(
        kernel,
        out_shape=outs,
        in_specs=in_specs or [IN_PLACE] * len(args),
        out_specs=out_specs or ([IN_PLACE] * len(outs) if many else IN_PLACE),
        scratch_shapes=scratch,
        input_output_aliases=aliases or {},
        cost_estimate=pl.CostEstimate(flops=cost, bytes_accessed=cost, transcendentals=0),
        compiler_params=pltpu.CompilerParams(vmem_limit_bytes=12 << 20),
    )(*args)


def tile_at(tile):
    return pl.ds(pl.multiple_of(tile * LANES, LANES), LANES)


def each_tile(width, work, unroll=4):
    def step(tile, carry):
        work(tile, tile_at(tile))
        return carry

    tiles = width // LANES
    lax.fori_loop(0, tiles, step, 0, unroll=min(unroll, tiles))


def iota(rows, dim):
    return lax.broadcasted_iota(jnp.int32, (rows, LANES), dim)


def down(cells, by):
    return pltpu.roll(cells, by, 0)


def around(ref, index, tile, tiles, circular=True):
    cells = ref[index, :, tile_at(tile)]
    before = ref[index, :, tile_at(lax.rem(tile + tiles - 1, tiles))]
    after = ref[index, :, tile_at(lax.rem(tile + 1, tiles))]
    lane = iota(cells.shape[0], 1)
    west = pltpu.roll(jnp.where(lane == LANES - 1, before, cells), 1, 1)
    east = pltpu.roll(jnp.where(lane == 0, after, cells), LANES - 1, 1)
    return cells, west + east + (down(cells, 1) + down(cells, cells.shape[0] - 1))


def places(tm_count):
    t = lax.axis_index("tm")
    odd = lax.rem(t, 2)
    return odd, jnp.where(odd == 1, t < tm_count - 1, t > 0).astype(F32)


def lat_places(lat_count):
    l = lax.axis_index("lat")
    return lax.rem(l, 2) == 0, (l < lat_count - 1).astype(F32), (l > 0).astype(F32)


def mirrored(odd, j):
    return jnp.where(odd == 1, SLICES - 1 - j, j)


def first_kernel(cot, _, own, la, lb, e3, *o3):
    odd, _ = places(2)
    even_lat, _, _ = lat_places(2)
    for j in range(SLICES):
        own[j] = cot[pl.ds(mirrored(odd, j), 1)][0]
    e3[...] = own[1]
    if o3:
        o3[0][...] = own[2]
    sub = iota(8, 0)

    def work(tile, cols):
        for i in range(0, SLICES, 2):
            first = jnp.where(sub < 4, own[i, :8, cols], down(own[i + 1, :8, cols], 5))
            last = jnp.where(sub >= 4, own[i, ROWS - 8 :, cols], down(own[i + 1, ROWS - 8 :, cols], 3))
            at = pl.ds(4 * i, 8)
            la[at, cols] = jnp.where(even_lat, last, first)
            lb[at, cols] = jnp.where(even_lat, first, last)

    each_tile(own.shape[2], work)


def in_blocks(out, cells):
    chunk = out.shape[1]
    blocks = cells.shape[1] // chunk
    for b in range(blocks):
        out[b * ROWS : (b + 1) * ROWS] = cells[:, b * chunk : (b + 1) * chunk]
    return blocks * ROWS


def near_kernel(near_e, near_o, rng, e1, o1):
    for out, cells in ((e1, near_e), (o1, near_o)):
        out[in_blocks(out, cells) :] = rng[...]


def below_above(lat_count, la, lb, at, cols):
    even_lat, has_below, has_above = lat_places(lat_count)
    a, b = la[pl.ds(at, 8), cols], lb[pl.ds(at, 8), cols]
    return jnp.where(even_lat, a, b) * has_below, jnp.where(even_lat, b, a) * has_above


def edge_rows(blocks):
    return (2 * blocks + 7) // 8 * 8


def far_kernel(lat_count, own, la, lb, *refs):
    e2, o2 = refs[-2:]
    chunk = e2.shape[1]
    blocks = own.shape[2] // chunk
    sub = iota(8, 0)
    for out, j, at, shifts in ((o2, 1, 0, (3, 5)), (e2, 2, 8, (0, 0))):
        start = in_blocks(out, own.at[j])
        for tile in range(chunk // LANES):
            for v in range(0, edge_rows(blocks), 8):
                rows = jnp.zeros((8, LANES), F32)
                for k in range(4):
                    b = v // 2 + k
                    if b < blocks:
                        cols = pl.ds(b * chunk + tile * LANES, LANES)
                        below, above = below_above(lat_count, la, lb, at, cols)
                        below = down(below, (shifts[0] + 2 * k + 1) % 8)
                        above = down(above, (shifts[1] + 2 * k + 1) % 8)
                        rows = jnp.where(sub == 2 * k, above, jnp.where(sub == 2 * k + 1, below, rows))
                out[start + v : start + v + 8, tile * LANES : (tile + 1) * LANES] = rows


def slab(ref, tile):
    per = ref.shape[1] // LANES
    at = pl.multiple_of(lax.div(tile, per) * ROWS, ROWS)
    return ref[pl.ds(at, ROWS), tile_at(lax.rem(tile, per))]


def rows_kernel(forward, e1, o1, *refs):
    chunk = e1.shape[1]
    even_lat, _, _ = lat_places(2)
    if forward:
        rng, far, la, lb, full = refs
        t = lax.axis_index("tm")
        for piece, owner in (
            (rng[...], t),
            (e1[pl.ds(e1.shape[0] - ROWS, ROWS)], t ^ 1),
            (far[...], t ^ 2),
            (o1[pl.ds(e1.shape[0] - ROWS, ROWS)], t ^ 3),
        ):
            full[:, pl.ds(pl.multiple_of(owner * chunk, chunk), chunk)] = piece
    else:
        gathered, la, lb, full = refs
        full[...] = gathered[...]
    sub = iota(8, 0)

    def work(tile, cols):
        near_e, near_o, field = slab(e1, tile), slab(o1, tile), full[:, cols]
        first = jnp.where(sub < 2, near_e[:8], jnp.where(sub < 4, down(near_o[:8], 2), down(field[:8], 4)))
        last = jnp.where(sub >= 6, near_e[8:], jnp.where(sub >= 4, down(near_o[8:], 6), down(field[8:], 4)))
        la[:, cols] = jnp.where(even_lat, last, first)
        lb[:, cols] = jnp.where(even_lat, first, last)

    each_tile(full.shape[1], work)


def main_kernel(counts, forward, own, e1, o1, e2, o2, full, la1, lb1, la2, lb2, its, u, y1, y2, rr, *grads):
    tm_count, lat_count = counts
    odd, has_before = places(tm_count)
    _, has_below, has_above = lat_places(lat_count)
    width = own.shape[2]
    chunk = e2.shape[1]
    tiles = width // LANES
    sub = iota(8, 0)
    row = iota(HELD, 0)
    mask = jnp.where(row < ROWS, 1.0, jnp.where(row < ROWS + 4, has_below, has_above))
    grad = grads[-1]

    def gather(tile, cols):
        def joined(cells, below, above):
            return jnp.concatenate([cells, jnp.where(sub < 4, below, above)], axis=0)

        for i in range(0, SLICES, 2):
            below, above = below_above(lat_count, la1, lb1, 4 * i, cols)
            u[1 + i, :, cols] = joined(own[i, :, cols], below, above)
            u[2 + i, :, cols] = joined(own[i + 1, :, cols], down(below, 3), down(above, 5))
        below, above = below_above(lat_count, la2, lb2, 0, cols)
        u[0, :, cols] = joined(slab(o1, tile), down(below, 6), down(above, 2)) * has_before
        u[SLICES + 1, :, cols] = joined(slab(e1, tile), below, above)
        rr[:, cols] = joined(full[:, cols], down(below, 4), down(above, 4)) + 6.0

    each_tile(width, gather)

    def once(tile, cols):
        field = rr[:, cols]
        for i in range(SLICES + 2):
            cells, beside = around(u, i, tile, tiles)
            y1[i, :, cols] = (beside - field * cells) * mask

    each_tile(width, once)

    def twice(tile, cols):
        field = rr[:, cols]
        c0 = [u[i, :ROWS, cols] for i in range(SLICES + 2)]
        c1 = [y1[i, :ROWS, cols] for i in range(SLICES + 2)]
        total = jnp.zeros((ROWS, LANES), F32)
        for j in range(SLICES):
            cells, beside = around(y1, j + 1, tile, tiles)
            out = (beside - field * cells) * mask
            y2[j, :, cols] = out
            at = mirrored(odd, j)
            x1, x2, x3 = (its[k, pl.ds(at, 1), :, cols][0] for k in range(3))
            one = c1[j + 1] + (c0[j] + c0[j + 2])
            two = out[:ROWS] + 2.0 * (c1[j] + c1[j + 2])
            two = two + (1.0 + (has_before if j == 0 else 1.0)) * c0[j + 1]
            two = two + (c0[j - 1] if j > 0 else slab(o2, tile) * has_before)
            two = two + (c0[j + 3] if j < SLICES - 1 else slab(e2, tile))
            total = total + c0[j + 1] * (W3 * x3 + W2 * x2 + W1 * x1)
            total = total + one * ((W2 * W3) * x2 + (W1 * SUM2) * x1) + two * ((W1 * PROD2) * x1)
        grad[:, cols] = -total

    each_tile(width, twice)
    if forward:
        t = lax.axis_index("tm")
        passed = width // chunk * ROWS
        for i, out in enumerate(grads[:4]):
            at = passed if i == 2 else 0
            out[at:] = grad[:, pl.ds(pl.multiple_of((t ^ i) * chunk, chunk), chunk)]
        grads[2][:passed] = e2[:passed]


def noise_kernel(tm_count, u, y1, y2, rr, e2, o2, e3, noise, ends, part, beside_far, sems):
    odd, has_before = places(tm_count)
    width = part.shape[2]
    tiles = width // LANES
    K0, K1, K2, K3 = COEFFS
    chunk = e2.shape[1]
    blocks = width // chunk
    row = iota(ROWS, 0)
    sub = iota(8, 0)
    for i, ref in enumerate((o2, e2)):
        for b in range(blocks):
            for tile in range(chunk // LANES):
                at = blocks * ROWS + b // 4 * 8
                rows = ref[at : at + 8, tile * LANES : (tile + 1) * LANES]
                k = b % 4
                rows = jnp.where(sub < 4, down(rows, (8 - 2 * k) % 8), down(rows, 6 - 2 * k))
                beside_far[i, :, b * chunk + tile * LANES : b * chunk + (tile + 1) * LANES] = rows

    def work(tile, cols):
        field = rr[:ROWS, cols]
        c0 = [u[i, :ROWS, cols] for i in range(SLICES + 2)]
        c1, c2, c3 = [], [], []
        for i in range(SLICES + 2):
            if i in (0, SLICES + 1):
                cells, beside = around(y1, i, tile, tiles)
                c1.append(cells[:ROWS])
                c2.append(beside[:ROWS] - field * cells[:ROWS])
                c3.append(None)
            else:
                cells, beside = around(y2, i - 1, tile, tiles)
                c1.append(y1[i, :ROWS, cols])
                c2.append(cells[:ROWS])
                c3.append(beside[:ROWS] - field * cells[:ROWS])
        far = []
        lane = iota(ROWS, 1)
        for i, ref in enumerate((o2, e2)):
            cells = slab(ref, tile)
            before = slab(ref, lax.rem(tile + tiles - 1, tiles))
            after = slab(ref, lax.rem(tile + 1, tiles))
            west = pltpu.roll(jnp.where(lane == LANES - 1, before, cells), 1, 1)
            east = pltpu.roll(jnp.where(lane == 0, after, cells), LANES - 1, 1)
            edge = jnp.concatenate([beside_far[i, :, cols]] * 2, axis=0)
            above = jnp.where(row == 0, edge, down(cells, 1))
            below = jnp.where(row == ROWS - 1, edge, down(cells, ROWS - 1))
            once = west + east + (above + below) - field * cells
            scale = has_before if i == 0 else 1.0
            far.append((cells * scale, once * scale))
        c0 = [far[0][0], *c0, far[1][0]]
        c1 = [far[0][1], *c1, far[1][1]]
        back = (1.0 + has_before, 2.0 + has_before)
        for j in range(SLICES):
            a, b = j + 2, j + 1
            one = c1[a] + (c0[a - 1] + c0[a + 1])
            twofold = back[0] if j == 0 else 2.0
            two = c2[b] + 2.0 * (c1[a - 1] + c1[a + 1]) + (c0[a - 2] + twofold * c0[a] + c0[a + 2])
            three = c3[b] + 3.0 * (c2[b - 1] + c2[b + 1] + (c1[a - 2] + twofold * c1[a] + c1[a + 2]))
            left = back[1] if j == 1 else 3.0
            right = back[1] if j == 0 else 3.0
            three = three + left * c0[a - 1] + right * c0[a + 1]
            if j > 0:
                three = three + c0[a - 3]
            three = three + (c0[a + 3] if j < SLICES - 1 else e3[:, cols])
            out = K0 * c0[a] + K1 * one + K2 * two + K3 * three
            if j == 0:
                ends[:, cols] = out
            else:
                part[j - 1, :, cols] = out

    each_tile(width, work)
    copies = [
        pltpu.make_async_copy(part.at[j - 1], noise.at[mirrored(odd, j)], sems.at[j])
        for j in range(1, SLICES)
    ]
    for copy in copies:
        copy.start()
    for copy in copies:
        copy.wait()


def last_kernel(tm_count, forward, noise_in, ends, o3, *refs):
    *parts, noise, gradient, part, sems = refs
    odd, has_before = places(tm_count)

    def work(tile, cols):
        part[:, cols] = ends[:, cols] + (COEFFS[3] * has_before) * (slab(o3, tile) if forward else o3[:, cols])

    each_tile(part.shape[1], work)
    copy = pltpu.make_async_copy(part, noise.at[mirrored(odd, 0)], sems.at[0])
    copy.start()
    total = parts[0][...]
    for more in parts[1:]:
        total = total + more[...]
    if forward:
        total = total + o3[pl.ds(o3.shape[0] - ROWS, ROWS)]
    gradient[...] = total
    copy.wait()


def body(counts, cotangent, iterates, range_field):
    tm_count, lat_count = counts
    forward = tm_count == 4
    slices, rows, width = cotangent.shape
    chunk = range_field.shape[1]
    assert slices == SLICES and rows == ROWS
    even, odd = even_pairs(tm_count), odd_pairs(tm_count)
    lat_even, lat_odd = even_pairs(lat_count), odd_pairs(lat_count)
    y_pairs = [(i, i ^ 2) for i in range(tm_count)]
    one = shape_of(ROWS, width)
    dma = pltpu.SemaphoreType.DMA

    blocks = width // chunk
    message = shape_of((blocks + 1) * ROWS, chunk)
    flip = lax.rem(lax.axis_index("tm"), 2) == 1
    near_e, near_o = (
        lax.dynamic_index_in_dim(cotangent, jnp.where(flip, SLICES - 1 - j, j), 0, False)
        for j in (SLICES - 1, 0)
    )
    e1, o1 = call(near_kernel, [message, message], near_e, near_o, range_field)
    e1 = lax.ppermute(e1, "tm", even)
    o1 = lax.ppermute(o1, "tm", odd)
    if forward:
        field = (range_field, lax.ppermute(range_field, "tm", y_pairs))
    else:
        field = (lax.all_gather(range_field, "tm", axis=1, tiled=True),)
    own, la1, lb1, e3, *o3 = call(
        first_kernel, [shape_of(SLICES, ROWS, width)] + [one] * (3 if forward else 4), cotangent, field[-1]
    )
    la1 = lax.ppermute(la1, "lat", lat_even)
    lb1 = lax.ppermute(lb1, "lat", lat_odd)
    far = shape_of(blocks * ROWS + edge_rows(blocks), chunk)
    e2, o2 = call(functools.partial(far_kernel, lat_count), [far, far], own, la1, lb1, e1)
    e2 = lax.ppermute(e2, "tm", even)
    o2 = lax.ppermute(o2, "tm", odd)
    e3 = lax.ppermute(e3, "tm", even)

    edge = shape_of(8, width)
    la2, lb2, full = call(functools.partial(rows_kernel, forward), [edge, edge, one], e1, o1, *field)
    la2 = lax.ppermute(la2, "lat", lat_even)
    lb2 = lax.ppermute(lb2, "lat", lat_odd)
    held = shape_of(SLICES + 2, HELD, width)
    outs = [held, held, shape_of(SLICES, HELD, width), shape_of(HELD, width)]
    piece = shape_of(ROWS, chunk)
    u, y1, y2, rr, *parts = call(
        functools.partial(main_kernel, counts, forward),
        outs + ([piece, piece, message, piece] if forward else [one]),
        own,
        e1,
        o1,
        e2,
        o2,
        full,
        la1,
        lb1,
        la2,
        lb2,
        iterates,
        scratch=[pltpu.VMEM((ROWS, width), F32)] if forward else (),
    )
    if forward:
        g0, g1, g2, g3 = parts
        o3 = lax.ppermute(g2, "tm", y_pairs)
        g1 = lax.ppermute(g1, "tm", even)
        g3 = lax.ppermute(g3, "tm", odd)
        parts = (g0, g1, g3)
    else:
        o3 = lax.ppermute(o3[0], "tm", odd)
        parts = (lax.psum_scatter(parts[0], "tm", scatter_dimension=1, tiled=True),)

    noise, ends = call(
        functools.partial(noise_kernel, tm_count),
        [shape_of(SLICES, ROWS, width), one],
        u,
        y1,
        y2,
        rr,
        e2,
        o2,
        e3,
        out_specs=[ANYWHERE, IN_PLACE],
        scratch=[pltpu.VMEM((SLICES - 1, ROWS, width), F32), pltpu.VMEM((2, 8, width), F32), dma((SLICES,))],
    )
    return call(
        functools.partial(last_kernel, tm_count, forward),
        [shape_of(SLICES, ROWS, width), shape_of(ROWS, chunk)],
        noise,
        ends,
        o3,
        *parts,
        in_specs=[ANYWHERE] + [IN_PLACE] * (2 + len(parts)),
        out_specs=[ANYWHERE, IN_PLACE],
        scratch=[pltpu.VMEM((ROWS, width), F32), dma((1,))],
        aliases={0: 0},
    )


def solution(mesh):
    counts = (mesh.shape["tm"], mesh.shape["lat"])
    return jax.shard_map(
        functools.partial(body, counts),
        mesh=mesh,
        in_specs=(P("tm", "lat", None), P(None, "tm", "lat", None), P("lat", "tm")),
        out_specs=(P("tm", "lat", None), P("lat", "tm")),
        check_vma=False,
    )
```

time: 91.7 us -> 36.5 us (0.40)
  waiting for transfers between devices: 30.9 us -> 11.4 us
  between operations: 14.3 us -> 0.76 us
  starting transfers between devices: 28.5 us -> 16 us
  blocking collectives: 10.5 us -> 0 us
  Pallas kernels: 0 us -> 6.34 us
  other arithmetic: 2.77 us -> 0 us
  local copies, waits for them, and re-layouts: 4.31 us -> 1.87 us
    reduce_scatter x1 -> x0, waiting for transfers between devices: 17.8 us -> none  [body(): lax.psum_scatter(product_sum, 'tm', scatter_dimension=1, tiled=True)]
    ppermute x12 -> x13, starting transfers between devices: 28.5 us -> 16 us  [the longest x1 3.7 us: body(): lb1 = lax.ppermute(lb1, 'lat', lat_odd)]
    all_gather x1 -> x0, blocking collectives: 10.5 us -> none  [body(): range_rows = lax.all_gather(range_field, 'tm', axis=1, tiled=True)]
    pallas_call x0 -> x7, Pallas kernels: none -> 6.34 us  [call(): pl.pallas_call(kernel, out_shape=outs, in_specs=in_specs or [IN_PLACE] *...]
    slice x12 -> x0, local copies, waits for them, and re-layouts: 4.29 us -> none  [the longest x6 2.04 us: stencil(): longitude = jnp.roll(field, 1, 2) + jnp.roll(field, -1, 2)]
    add x3 -> x0, other arithmetic: 1.93 us -> none  [the longest x1 1.24 us: body(): noise_cot = noise_cot + weights[section - 1] * adjoint]
    ppermute x12 -> x13, waiting for transfers between devices: 13.1 us -> 11.4 us  [the longest x1 4.31 us: body(): lb2 = lax.ppermute(lb2, 'lat', lat_odd)]
    squeeze x0 -> x1, local copies, waits for them, and re-layouts: none -> 0.99 us  [body(): lax.dynamic_index_in_dim(cotangent, jnp.where(flip, SLICES - 1 - j, j), 0...]
  transfers between devices with their start and end apart: 13 -> 13, of which waited for: 5 -> 5; matrix products, arithmetic and copies ran while one was open for 5% -> 3% of each run, Pallas kernels for 0% -> 7%
where the time goes in v2:
time: 36.5 us; the launch traced here: 36.4 us
  starting transfers between devices  16 us (44%)
  waiting for transfers between devices  11.4 us (31%)
  Pallas kernels  6.34 us (17%)
  local copies, waits for them, and re-layouts  1.87 us (5%)
  between operations  0.76 us (2%)
    pallas_call x7, Pallas kernels, call(): pl.pallas_call(kernel, out_shape=outs, in_specs=in_specs or [IN_PLACE] *...  6.34 us
    ppermute x1, waiting for transfers between devices, body(): lb2 = lax.ppermute(lb2, 'lat', lat_odd)  4.31 us
    ppermute x1, starting transfers between devices, body(): lb1 = lax.ppermute(lb1, 'lat', lat_odd)  3.7 us
    ppermute x1, starting transfers between devices, body(): field = (range_field, lax.ppermute(range_field, 'tm', y_pairs))  3.03 us
    ppermute x1, waiting for transfers between devices, body(): o1 = lax.ppermute(o1, 'tm', odd)  2.38 us
    ppermute x1, starting transfers between devices, body(): e3 = lax.ppermute(e3, 'tm', even)  2.14 us
    ppermute x1, waiting for transfers between devices, body(): lb1 = lax.ppermute(lb1, 'lat', lat_odd)  1.76 us
    ppermute x1, waiting for transfers between devices, body(): e3 = lax.ppermute(e3, 'tm', even)  1.75 us
  transfers between devices with their start and end apart: 13, of which 5 were waited for; matrix products, arithmetic and copies ran while one was open for 3% of the time, Pallas kernels for 7%

profile of v2, /device:TPU:0, one launch (start us, length us, event | category | flops | bytes accessed | tf_op | source)
XLA Modules:
  0.0 36.4 jit_solution(7229467525989017938)
XLA Ops:
  0.6 3.0 %collective-permute-start = (f32[16,512]{1,0:T(8,128)}, f32[16,512]{1,0:T(8,128)S(1)}, u32[]{:S(2)}, u32[]{:S(2)}) collective-permute-start(f32[16,512]{1,0:T(8,128)} %refs_0_.1), channel_id=1, source_target_pairs={{0,16},{8,24},{16,0},{24,8},{1,17},{9,25},{17,1},{25,9},{2,18},{10... | collective-permute-start | bytes 98312 | tf_op jit(solution)/shard_map/ppermute | solution.py:400
  3.7 1.0 %dynamic-slice_bitcast_fusion = (f32[16,2048]{1,0:T(8,128)S(1)}, f32[16,2048]{1,0:T(8,128)S(1)}) fusion(f32[4,16,2048]{2,1,0:T(8,128)} %cot.1, s32[]{:T(128)S(6)} %select_n.11, s32[]{:T(128)S(6)} %select_n.10), kind=kLoop, calls=%fused_computation | loop fusion | bytes 524296 | tf_op jit(solution)/shard_map/jit(dynamic_index_in_dim)/squeeze | solution.py:393
  4.7 0.0 copy-start
  4.7 0.0 copy-start.2
  4.7 0.9 %copy-done.2 = f32[16,512]{1,0:T(8,128)S(1)} copy-done((f32[16,512]{1,0:T(8,128)S(1)}, f32[16,512]{1,0:T(8,128)}, u32[]{:S(2)}) %copy-start.2) | copy-done | bytes 32792
  5.6 1.6 %collective-permute-start.1 = (f32[80,512]{1,0:T(8,128)S(1)}, f32[80,512]{1,0:T(8,128)S(1)}, u32[]{:S(2)}, u32[]{:S(2)}) collective-permute-start(f32[80,512]{1,0:T(8,128)S(1)} %get-tuple-element.24), channel_id=1, source_target_pairs={{0,8},{8,0},{16,24},{24,16},{1,9},{9,1},{17,25},{25,17},{2,10},{10... | collective-permute-start | bytes 491528 | tf_op jit(solution)/shard_map/ppermute | solution.py:397
  7.1 0.0 collective-permute-done._.refs_1_
  7.1 0.1 shard_map.50
  7.3 0.1 collective-permute-start.3
  7.4 3.7 %collective-permute-start.4 = (f32[16,2048]{1,0:T(8,128)S(1)}, f32[16,2048]{1,0:T(8,128)S(1)}, u32[]{:S(2)}, u32[]{:S(2)}) collective-permute-start(f32[16,2048]{1,0:T(8,128)S(1)} %get-tuple-element.27), channel_id=1, source_target_pairs={{0,7},{1,2},{2,1},{3,4},{4,3},{5,6},{6,5},{7,0},{8,15},{9,10},{10,... | collective-permute-start | bytes 393224 | tf_op jit(solution)/shard_map/ppermute | solution.py:407
  11.1 1.6 %collective-permute-start.2 = (f32[80,512]{1,0:T(8,128)S(1)}, f32[80,512]{1,0:T(8,128)S(1)}, u32[]{:S(2)}, u32[]{:S(2)}) collective-permute-start(f32[80,512]{1,0:T(8,128)S(1)} %get-tuple-element.25), channel_id=1, source_target_pairs={{0,24},{8,16},{16,8},{24,0},{1,25},{9,17},{17,9},{25,1},{2,26},{10... | collective-permute-start | bytes 491528 | tf_op jit(solution)/shard_map/ppermute | solution.py:398
  12.7 0.0 collective-permute-done.3.la.la1
  12.7 1.8 %collective-permute-done.4.lb.lb1 = f32[16,2048]{1,0:T(8,128)S(1)} collective-permute-done((f32[16,2048]{1,0:T(8,128)S(1)}, f32[16,2048]{1,0:T(8,128)S(1)}, u32[]{:S(2)}, u32[]{:S(2)}) %collective-permute-start.4) | collective-permute-done | bytes 131104 | tf_op jit(solution)/shard_map/ppermute | solution.py:407
  14.5 0.7 %collective-permute-start.5 = (f32[72,512]{1,0:T(8,128)S(1)}, f32[72,512]{1,0:T(8,128)S(1)}, u32[]{:S(2)}, u32[]{:S(2)}) collective-permute-start(f32[72,512]{1,0:T(8,128)S(1)} %get-tuple-element.28), channel_id=1, source_target_pairs={{0,8},{8,0},{16,24},{24,16},{1,9},{9,1},{17,25},{25,17},{2,10},{10... | collective-permute-start | bytes 442376 | tf_op jit(solution)/shard_map/ppermute | solution.py:410
  15.2 1.5 %collective-permute-start.6 = (f32[72,512]{1,0:T(8,128)S(1)}, f32[72,512]{1,0:T(8,128)S(1)}, u32[]{:S(2)}, u32[]{:S(2)}) collective-permute-start(f32[72,512]{1,0:T(8,128)S(1)} %get-tuple-element.29), channel_id=1, source_target_pairs={{0,24},{8,16},{16,8},{24,0},{1,25},{9,17},{17,9},{25,1},{2,26},{10... | collective-permute-start | bytes 442376 | tf_op jit(solution)/shard_map/ppermute | solution.py:411
  16.7 2.4 %collective-permute-done.2.o1 = f32[80,512]{1,0:T(8,128)S(1)} collective-permute-done((f32[80,512]{1,0:T(8,128)S(1)}, f32[80,512]{1,0:T(8,128)S(1)}, u32[]{:S(2)}, u32[]{:S(2)}) %collective-permute-start.2) | collective-permute-done | bytes 163872 | tf_op jit(solution)/shard_map/ppermute | solution.py:398
  19.0 0.1 shard_map.53
  19.2 0.1 collective-permute-start.7
  19.3 0.1 collective-permute-start.8
  19.3 1.2 %collective-permute-done.7.la2 = f32[8,2048]{1,0:T(8,128)S(1)} collective-permute-done((f32[8,2048]{1,0:T(8,128)S(1)}, f32[8,2048]{1,0:T(8,128)S(1)}, u32[]{:S(2)}, u32[]{:S(2)}) %collective-permute-start.7) | collective-permute-done | bytes 65568 | tf_op jit(solution)/shard_map/ppermute | solution.py:416
  20.5 4.3 %collective-permute-done.8.lb2 = f32[8,2048]{1,0:T(8,128)S(1)} collective-permute-done((f32[8,2048]{1,0:T(8,128)S(1)}, f32[8,2048]{1,0:T(8,128)S(1)}, u32[]{:S(2)}, u32[]{:S(2)}) %collective-permute-start.8) | collective-permute-done | bytes 65568 | tf_op jit(solution)/shard_map/ppermute | solution.py:417
  24.8 0.0 collective-permute-done.5.e2
  24.8 0.0 collective-permute-done.6.o2
  24.8 2.5 %shard_map.54 = (f32[6,24,2048]{2,1,0:T(8,128)S(1)}, f32[6,24,2048]{2,1,0:T(8,128)S(1)}, f32[4,24,2048]{2,1,0:T(8,128)S(1)}, f32[24,2048]{1,0:T(8,128)S(1)}, f32...) custom-call(f32[4,16,2048]{2,1,0:T(8,128)S(1)} %get-tuple-element.23.own, ...), custom_call_target="tpu_custom_call" | custom-call | tf_op jit(solution)/shard_map/pallas_call | solution.py:57
  27.3 0.1 collective-permute-start.10
  27.4 2.1 %collective-permute-start.9 = (f32[16,2048]{1,0:T(8,128)S(1)}, f32[16,2048]{1,0:T(8,128)S(1)}, u32[]{:S(2)}, u32[]{:S(2)}) collective-permute-start(f32[16,2048]{1,0:T(8,128)S(1)} %get-tuple-element.37), channel_id=1, source_target_pairs={{0,8},{8,0},{16,24},{24,16},{1,9},{9,1},{17,25},{25,17},{2,10},{10... | collective-permute-start | bytes 393224 | tf_op jit(solution)/shard_map/ppermute | solution.py:412
  29.5 0.0 collective-permute-start.11
  29.6 1.5 %collective-permute-start.12 = (f32[16,512]{1,0:T(8,128)S(1)}, f32[16,512]{1,0:T(8,128)S(1)}, u32[]{:S(2)}, u32[]{:S(2)}) collective-permute-start(f32[16,512]{1,0:T(8,128)S(1)} %get-tuple-element.43), channel_id=1, source_target_pairs={{0,24},{8,16},{16,8},{24,0},{1,25},{9,17},{17,9},{25,1},{2,26},{10... | collective-permute-start | bytes 98312 | tf_op jit(solution)/shard_map/ppermute | solution.py:441
  31.1 1.8 %collective-permute-done.9.e3 = f32[16,2048]{1,0:T(8,128)S(1)} collective-permute-done((f32[16,2048]{1,0:T(8,128)S(1)}, f32[16,2048]{1,0:T(8,128)S(1)}, u32[]{:S(2)}, u32[]{:S(2)}) %collective-permute-start.9) | collective-permute-done | bytes 131104 | tf_op jit(solution)/shard_map/ppermute | solution.py:412
  32.8 2.1 %shard_map.55 = (f32[4,16,2048]{2,1,0:T(8,128)}, f32[16,2048]{1,0:T(8,128)S(1)}) custom-call(f32[6,24,2048]{2,1,0:T(8,128)S(1)} %get-tuple-element.33.u, f32[6,24,2048]{2,1,0:T(8,128)S(1)} %get-tuple-element.34.y1, f32[4,24,2048]{2,1,0:T(8,128)S(1)} %get-tuple-element.35.y2, f32[24,2048]{1,0:T(8,128)S(1)} %get-tuple-element.36.rr, ...), custom_call_target="tpu_custom_call" | custom-call | tf_op jit(solution)/shard_map/pallas_call | solution.py:57
  34.9 0.0 collective-permute-done.12.refs_2_
  35.0 1.4 %shard_map.56 = (f32[4,16,2048]{2,1,0:T(8,128)}, f32[16,512]{1,0:T(8,128)}) custom-call(f32[4,16,2048]{2,1,0:T(8,128)} %get-tuple-element.38.noise_in, f32[16,2048]{1,0:T(8,128)S(1)} %get-tuple-element.39.ends, f32[80,512]{1,0:T(8,128)S(1)} %collective-permute-done.10.o3, f32[16,512]{1,0:T(8,128)S(1)} %get-tuple-element.41.refs_0_, ...), custom_call_target="tpu_custom_call", output_to_operand_aliasing={{0}: (0, {})} | custom-call | tf_op jit(solution)/shard_map/pallas_call | solution.py:57
  (10 shorter events, 0.1 us)
Async XLA Ops:
  0.6 6.5 %copy-start.1 = (f32[4,16,2048]{2,1,0:T(8,128)S(1)}, f32[4,16,2048]{2,1,0:T(8,128)}, u32[]{:S(2)}) copy-start(f32[4,16,2048]{2,1,0:T(8,128)} %cot.1) | copy-start | bytes 1572868
  0.6 6.5 %collective-permute-start = (f32[16,512]{1,0:T(8,128)}, f32[16,512]{1,0:T(8,128)S(1)}, u32[]{:S(2)}, u32[]{:S(2)}) collective-permute-start(f32[16,512]{1,0:T(8,128)} %refs_0_.1), channel_id=1, source_target_pairs={{0,16},{8,24},{16,0},{24,8},{1,17},{9,25},{17,1},{25,9},{2,18},{10... | collective-permute-start | bytes 98312 | tf_op jit(solution)/shard_map/ppermute | solution.py:400
  4.7 20.2 %copy-start = (f32[3,4,16,2048]{3,2,1,0:T(8,128)S(1)}, f32[3,4,16,2048]{3,2,1,0:T(8,128)}, u32[]{:S(2)}) copy-start(f32[3,4,16,2048]{3,2,1,0:T(8,128)} %its.1) | copy-start | bytes 4718596
  4.7 0.9 %copy-start.2 = (f32[16,512]{1,0:T(8,128)S(1)}, f32[16,512]{1,0:T(8,128)}, u32[]{:S(2)}) copy-start(f32[16,512]{1,0:T(8,128)} %refs_0_.1) | copy-start | bytes 98308
  5.6 13.5 %copy-start.3 = (f32[16,512]{1,0:T(8,128)S(1)}, f32[16,512]{1,0:T(8,128)}, u32[]{:S(2)}) copy-start(f32[16,512]{1,0:T(8,128)} %refs_0_.1) | copy-start | bytes 98308
  5.6 7.1 %collective-permute-start.1 = (f32[80,512]{1,0:T(8,128)S(1)}, f32[80,512]{1,0:T(8,128)S(1)}, u32[]{:S(2)}, u32[]{:S(2)}) collective-permute-start(f32[80,512]{1,0:T(8,128)S(1)} %get-tuple-element.24), channel_id=1, source_target_pairs={{0,8},{8,0},{16,24},{24,16},{1,9},{9,1},{17,25},{25,17},{2,10},{10... | collective-permute-start | bytes 491528 | tf_op jit(solution)/shard_map/ppermute | solution.py:397
  7.3 5.4 %collective-permute-start.3 = (f32[16,2048]{1,0:T(8,128)S(1)}, f32[16,2048]{1,0:T(8,128)S(1)}, u32[]{:S(2)}, u32[]{:S(2)}) collective-permute-start(f32[16,2048]{1,0:T(8,128)S(1)} %get-tuple-element.26), channel_id=1, source_target_pairs={{0,1},{1,0},{2,3},{3,2},{4,5},{5,4},{6,7},{7,6},{8,9},{9,8},{10,11... | collective-permute-start | bytes 393224 | tf_op jit(solution)/shard_map/ppermute | solution.py:406
  7.4 7.1 %collective-permute-start.4 = (f32[16,2048]{1,0:T(8,128)S(1)}, f32[16,2048]{1,0:T(8,128)S(1)}, u32[]{:S(2)}, u32[]{:S(2)}) collective-permute-start(f32[16,2048]{1,0:T(8,128)S(1)} %get-tuple-element.27), channel_id=1, source_target_pairs={{0,7},{1,2},{2,1},{3,4},{4,3},{5,6},{6,5},{7,0},{8,15},{9,10},{10,... | collective-permute-start | bytes 393224 | tf_op jit(solution)/shard_map/ppermute | solution.py:407
  11.1 8.0 %collective-permute-start.2 = (f32[80,512]{1,0:T(8,128)S(1)}, f32[80,512]{1,0:T(8,128)S(1)}, u32[]{:S(2)}, u32[]{:S(2)}) collective-permute-start(f32[80,512]{1,0:T(8,128)S(1)} %get-tuple-element.25), channel_id=1, source_target_pairs={{0,24},{8,16},{16,8},{24,0},{1,25},{9,17},{17,9},{25,1},{2,26},{10... | collective-permute-start | bytes 491528 | tf_op jit(solution)/shard_map/ppermute | solution.py:398
  14.5 10.4 %collective-permute-start.5 = (f32[72,512]{1,0:T(8,128)S(1)}, f32[72,512]{1,0:T(8,128)S(1)}, u32[]{:S(2)}, u32[]{:S(2)}) collective-permute-start(f32[72,512]{1,0:T(8,128)S(1)} %get-tuple-element.28), channel_id=1, source_target_pairs={{0,8},{8,0},{16,24},{24,16},{1,9},{9,1},{17,25},{25,17},{2,10},{10... | collective-permute-start | bytes 442376 | tf_op jit(solution)/shard_map/ppermute | solution.py:410
  15.2 9.7 %collective-permute-start.6 = (f32[72,512]{1,0:T(8,128)S(1)}, f32[72,512]{1,0:T(8,128)S(1)}, u32[]{:S(2)}, u32[]{:S(2)}) collective-permute-start(f32[72,512]{1,0:T(8,128)S(1)} %get-tuple-element.29), channel_id=1, source_target_pairs={{0,24},{8,16},{16,8},{24,0},{1,25},{9,17},{17,9},{25,1},{2,26},{10... | collective-permute-start | bytes 442376 | tf_op jit(solution)/shard_map/ppermute | solution.py:411
  19.2 1.3 %collective-permute-start.7 = (f32[8,2048]{1,0:T(8,128)S(1)}, f32[8,2048]{1,0:T(8,128)S(1)}, u32[]{:S(2)}, u32[]{:S(2)}) collective-permute-start(f32[8,2048]{1,0:T(8,128)S(1)} %get-tuple-element.31), channel_id=1, source_target_pairs={{0,1},{1,0},{2,3},{3,2},{4,5},{5,4},{6,7},{7,6},{8,9},{9,8},{10,11... | collective-permute-start | bytes 196616 | tf_op jit(solution)/shard_map/ppermute | solution.py:416
  19.3 5.6 %collective-permute-start.8 = (f32[8,2048]{1,0:T(8,128)S(1)}, f32[8,2048]{1,0:T(8,128)S(1)}, u32[]{:S(2)}, u32[]{:S(2)}) collective-permute-start(f32[8,2048]{1,0:T(8,128)S(1)} %get-tuple-element.32), channel_id=1, source_target_pairs={{0,7},{1,2},{2,1},{3,4},{4,3},{5,6},{6,5},{7,0},{8,15},{9,10},{10,... | collective-permute-start | bytes 196616 | tf_op jit(solution)/shard_map/ppermute | solution.py:417
  27.3 7.6 %collective-permute-start.10 = (f32[80,512]{1,0:T(8,128)S(1)}, f32[80,512]{1,0:T(8,128)S(1)}, u32[]{:S(2)}, u32[]{:S(2)}) collective-permute-start(f32[80,512]{1,0:T(8,128)S(1)} %get-tuple-element.40), channel_id=1, source_target_pairs={{0,16},{8,24},{16,0},{24,8},{1,17},{9,25},{17,1},{25,9},{2,18},{10... | collective-permute-start | bytes 491528 | tf_op jit(solution)/shard_map/ppermute | solution.py:439
  27.4 5.4 %collective-permute-start.9 = (f32[16,2048]{1,0:T(8,128)S(1)}, f32[16,2048]{1,0:T(8,128)S(1)}, u32[]{:S(2)}, u32[]{:S(2)}) collective-permute-start(f32[16,2048]{1,0:T(8,128)S(1)} %get-tuple-element.37), channel_id=1, source_target_pairs={{0,8},{8,0},{16,24},{24,16},{1,9},{9,1},{17,25},{25,17},{2,10},{10... | collective-permute-start | bytes 393224 | tf_op jit(solution)/shard_map/ppermute | solution.py:412
  29.5 5.4 %collective-permute-start.11 = (f32[16,512]{1,0:T(8,128)S(1)}, f32[16,512]{1,0:T(8,128)S(1)}, u32[]{:S(2)}, u32[]{:S(2)}) collective-permute-start(f32[16,512]{1,0:T(8,128)S(1)} %get-tuple-element.42), channel_id=1, source_target_pairs={{0,8},{8,0},{16,24},{24,16},{1,9},{9,1},{17,25},{25,17},{2,10},{10... | collective-permute-start | bytes 98312 | tf_op jit(solution)/shard_map/ppermute | solution.py:440
  29.6 5.4 %collective-permute-start.12 = (f32[16,512]{1,0:T(8,128)S(1)}, f32[16,512]{1,0:T(8,128)S(1)}, u32[]{:S(2)}, u32[]{:S(2)}) collective-permute-start(f32[16,512]{1,0:T(8,128)S(1)} %get-tuple-element.43), channel_id=1, source_target_pairs={{0,24},{8,16},{16,8},{24,0},{1,25},{9,17},{17,9},{25,1},{2,26},{10... | collective-permute-start | bytes 98312 | tf_op jit(solution)/shard_map/ppermute | solution.py:441

commit v3 on v0

v3 whole, which is shorter than its diff:
```python
import functools
import math

import jax
import jax.numpy as jnp
from jax import lax
from jax.experimental import pallas as pl
from jax.experimental.pallas import tpu as pltpu
from jax.sharding import PartitionSpec as P

F32 = jnp.float32
LANES = 128
SLICES = 4
ROWS = 16
HELD = 24


def step_weights():
    centre_value = 6.525
    spread_value = 6.475
    root_order = (3, 0, 2, 1)
    return [
        1.0 / (centre_value + spread_value * math.cos(math.pi * (2 * section + 1) / 8.0))
        for section in root_order
    ]


W0, W1, W2, W3 = step_weights()
SUM2 = W2 + W3
PROD2 = W2 * W3
COEFFS = (
    W0 + W1 + W2 + W3,
    W0 * (W1 + W2 + W3) + W1 * SUM2 + W2 * W3,
    W0 * (W1 * W2 + W1 * W3 + W2 * W3) + W1 * PROD2,
    W0 * W1 * W2 * W3,
)


def even_pairs(count):
    return [(i, i ^ 1) for i in range(count)]


def odd_pairs(count):
    return [(i, (i + 1) % count if i % 2 else (i - 1) % count) for i in range(count)]


def lat_odd_pairs(count):
    return [(i, i if i in (0, count - 1) else other) for i, other in odd_pairs(count)]


def shape_of(*dims):
    return jax.ShapeDtypeStruct(dims, F32)


IN_PLACE = pl.BlockSpec(memory_space=pltpu.VMEM)
ANYWHERE = pl.BlockSpec(memory_space=pltpu.HBM)


def call(kernel, outs, *args, in_specs=None, out_specs=None, scratch=(), aliases=None, cost=0):
    many = isinstance(outs, (list, tuple))
    return pl.pallas_call(
        kernel,
        out_shape=outs,
        in_specs=in_specs or [IN_PLACE] * len(args),
        out_specs=out_specs or ([IN_PLACE] * len(outs) if many else IN_PLACE),
        scratch_shapes=scratch,
        input_output_aliases=aliases or {},
        cost_estimate=pl.CostEstimate(flops=cost, bytes_accessed=cost, transcendentals=0),
        compiler_params=pltpu.CompilerParams(vmem_limit_bytes=12 << 20),
    )(*args)


def tile_at(tile):
    return pl.ds(pl.multiple_of(tile * LANES, LANES), LANES)


def each_tile(width, work, unroll=8):
    def step(tile, carry):
        work(tile, tile_at(tile))
        return carry

    tiles = width // LANES
    lax.fori_loop(0, tiles, step, 0, unroll=min(unroll, tiles))


def iota(rows, dim):
    return lax.broadcasted_iota(jnp.int32, (rows, LANES), dim)


def down(cells, by):
    return pltpu.roll(cells, by, 0)


def around(ref, index, tile, tiles, circular=True):
    cells = ref[index, :, tile_at(tile)]
    before = ref[index, :, tile_at(lax.rem(tile + tiles - 1, tiles))]
    after = ref[index, :, tile_at(lax.rem(tile + 1, tiles))]
    lane = iota(cells.shape[0], 1)
    west = pltpu.roll(jnp.where(lane == LANES - 1, before, cells), 1, 1)
    east = pltpu.roll(jnp.where(lane == 0, after, cells), LANES - 1, 1)
    return cells, west + east + (down(cells, 1) + down(cells, cells.shape[0] - 1))


def places(tm_count):
    t = lax.axis_index("tm")
    odd = lax.rem(t, 2)
    return odd, jnp.where(odd == 1, t < tm_count - 1, t > 0).astype(F32)


def lat_places(lat_count):
    l = lax.axis_index("lat")
    return lax.rem(l, 2) == 0, (l < lat_count - 1).astype(F32), (l > 0).astype(F32)


def mirrored(odd, j):
    return jnp.where(odd == 1, SLICES - 1 - j, j)


def first_kernel(cot, *slabs):
    odd, _ = places(2)
    for j in range(SLICES):
        slabs[j][...] = cot[pl.ds(mirrored(odd, j), 1)][0]


def scale_kernel(s2, rng, its, far_e, held, scales):
    far_e[...] = s2[...]
    held[...] = rng[...]
    odd, _ = places(2)

    def work(tile, cols):
        for j in range(SLICES):
            x1, x2, x3 = (its[k, pl.ds(mirrored(odd, j), 1), :, cols][0] for k in range(3))
            scales[0, j, :, cols] = W3 * x3 + W2 * x2 + W1 * x1
            scales[1, j, :, cols] = (W2 * W3) * x2 + (W1 * SUM2) * x1
            scales[2, j, :, cols] = (W1 * PROD2) * x1

    each_tile(s2.shape[1], work)


def rows_kernel(forward, *refs):
    slabs, (near_e, near_o), refs = refs[:SLICES], refs[SLICES : SLICES + 2], refs[SLICES + 2 :]
    even_lat, _, _ = lat_places(2)
    *field, full, la, lb = refs
    if forward:
        t = lax.axis_index("tm")
        chunk = field[0].shape[1]
        for i, piece in enumerate(field):
            full[:, pl.ds(pl.multiple_of((t ^ i) * chunk, chunk), chunk)] = piece[...]
    else:
        full[...] = field[0][...]
    sub = iota(8, 0)

    def work(tile, cols):
        for i in range(SLICES // 2):
            one, two, field = slabs[2 * i], slabs[2 * i + 1], full
            first = jnp.where(sub == 3, down(field[:8, cols], 3 - i), down(two[:8, cols], 5))
            first = jnp.where(sub < 3, one[:8, cols], first)
            last = jnp.where(sub == 4, down(field[8:, cols], 6 - i), down(two[8:, cols], 3))
            last = jnp.where(sub > 4, one[8:, cols], last)
            la[8 * i : 8 * i + 8, cols] = jnp.where(even_lat, last, first)
            lb[8 * i : 8 * i + 8, cols] = jnp.where(even_lat, first, last)
        first = jnp.where(sub < 2, near_e[:8, cols], down(near_o[:8, cols], 2))
        last = jnp.where(sub >= 6, near_e[8:, cols], down(near_o[8:, cols], 6))
        la[16:, cols] = jnp.where(even_lat, last, first)
        lb[16:, cols] = jnp.where(even_lat, first, last)

    each_tile(full.shape[1], work)


def below_above(lat_count, la, lb, at, cols):
    even_lat, has_below, has_above = lat_places(lat_count)
    a, b = la[pl.ds(at, 8), cols], lb[pl.ds(at, 8), cols]
    return jnp.where(even_lat, a, b) * has_below, jnp.where(even_lat, b, a) * has_above


def joined(cells, below, above):
    return jnp.concatenate([cells, jnp.where(iota(8, 0) < 4, below, above)], axis=0)


def lat_mask(lat_count):
    _, has_below, has_above = lat_places(lat_count)
    row = iota(HELD, 0)
    return jnp.where(row < ROWS, 1.0, jnp.where(row < ROWS + 4, has_below, has_above))


def at(cells, j):
    return cells[j] if 0 <= j < SLICES else 0.0


def own_kernel(counts, s0, s1, s2, s3, full, la, lb, scales, grad, noise, rr, edge_e, edge_o, u, y1, y2):
    tm_count, lat_count = counts
    K0, K1, K2, _ = COEFFS
    odd, has_before = places(tm_count)
    width = full.shape[1]
    tiles = width // LANES
    mask = lat_mask(lat_count)
    back = 1.0 + has_before

    def gather(tile, cols):
        first, last = below_above(lat_count, la, lb, 0, cols)
        second, ahead = below_above(lat_count, la, lb, 8, cols)
        u[0, :, cols] = joined(s0[:, cols], first, last)
        u[1, :, cols] = joined(s1[:, cols], down(first, 3), down(last, 5))
        u[2, :, cols] = joined(s2[:, cols], second, ahead)
        u[3, :, cols] = joined(s3[:, cols], down(second, 3), down(ahead, 5))
        sub = iota(8, 0)
        below = jnp.where(sub == 0, down(first, 5), down(second, 6))
        above = jnp.where(sub == 7, down(ahead, 3), down(last, 2))
        rr[:, cols] = joined(full[:, cols], below, above) + 6.0

    each_tile(width, gather)

    def once(tile, cols):
        field = rr[:, cols]
        for j in range(SLICES):
            cells, beside = around(u, j, tile, tiles)
            y1[j, :, cols] = (beside - field * cells) * mask

    each_tile(width, once)

    def twice(tile, cols):
        field = rr[:, cols]
        c0 = [u[j, :ROWS, cols] for j in range(SLICES)]
        c1 = [y1[j, :ROWS, cols] for j in range(SLICES)]
        total = jnp.zeros((ROWS, LANES), F32)
        for j in range(SLICES):
            cells, beside = around(y1, j, tile, tiles)
            c2 = (beside - field * cells) * mask
            y2[j, :, cols] = c2
            one = c1[j] + (at(c0, j - 1) + at(c0, j + 1))
            two = c2[:ROWS] + 2.0 * (at(c1, j - 1) + at(c1, j + 1))
            two = two + (back if j == 0 else 2.0) * c0[j] + (at(c0, j - 2) + at(c0, j + 2))
            total = total + c0[j] * scales[0, j, :, cols] + one * scales[1, j, :, cols] + two * scales[2, j, :, cols]
            noise[j, :, cols] = K0 * c0[j] + K1 * one + K2 * two
        grad[:, cols] = -total

    each_tile(width, twice)
    chunk = edge_e.shape[1]
    blocks = width // chunk
    sub = iota(8, 0)
    for out, start, shifts in ((edge_o, 0, (3, 5)), (edge_e, 8, (0, 0))):
        for tile in range(chunk // LANES):
            for v in range(0, edge_rows(blocks), 8):
                rows = jnp.zeros((8, LANES), F32)
                for k in range(min(4, blocks - v // 2)):
                    cols = pl.ds((v // 2 + k) * chunk + tile * LANES, LANES)
                    below, above = below_above(lat_count, la, lb, start, cols)
                    below = down(below, (shifts[0] + 2 * k + 1) % 8)
                    above = down(above, (shifts[1] + 2 * k + 1) % 8)
                    rows = jnp.where(sub == 2 * k, above, jnp.where(sub == 2 * k + 1, below, rows))
                out[v : v + 8, tile * LANES : (tile + 1) * LANES] = rows


def third_kernel(tm_count, noise, u, y1, y2, rr, _, out):
    _, has_before = places(tm_count)
    width = noise.shape[2]
    tiles = width // LANES
    K3 = COEFFS[3]
    back = 1.0 + has_before

    def thrice(tile, cols):
        field = rr[:ROWS, cols]
        c0 = [u[j, :ROWS, cols] for j in range(SLICES)]
        c1 = [y1[j, :ROWS, cols] for j in range(SLICES)]
        c2 = [y2[j, :ROWS, cols] for j in range(SLICES)]
        for j in range(SLICES):
            cells, beside = around(y2, j, tile, tiles)
            three = beside[:ROWS] - field * cells[:ROWS]
            three = three + 3.0 * (at(c2, j - 1) + at(c2, j + 1) + at(c1, j - 2) + at(c1, j + 2))
            three = three + (3.0 * back if j == 0 else 6.0) * c1[j]
            left, right = (1.0 + back if j == i else 3.0 for i in (1, 0))
            three = three + (left * at(c0, j - 1) + right * at(c0, j + 1) + at(c0, j - 3) + at(c0, j + 3))
            out[j, :, cols] = noise[j, :, cols] + K3 * three

    each_tile(width, thrice)


def edge_rows(blocks):
    return (2 * blocks + 7) // 8 * 8


def near_kernel(counts, forward, grad, near_e, near_o, far_e, far_o, la, lb, rr, edge_e, edge_o, scales, *refs):
    tm_count, lat_count = counts
    odd, has_before = places(tm_count)
    width = grad.shape[1]
    tiles = width // LANES
    mask = lat_mask(lat_count)
    u, y1 = refs[:2]
    total = refs[-1] if forward else refs[2]

    def gather(tile, cols):
        below, above = below_above(lat_count, la, lb, 16, cols)
        u[0, :, cols] = joined(near_o[:, cols], down(below, 6), down(above, 2)) * has_before
        u[1, :, cols] = joined(near_e[:, cols], below, above)

    each_tile(width, gather)

    def once(tile, cols):
        field = rr[:, cols]
        out = grad[:, cols]
        for i, far in enumerate((far_o, far_e)):
            cells, beside = around(u, i, tile, tiles)
            c1 = (beside - field * cells) * mask
            y1[i, :, cols] = c1
            beyond = far[:, cols] * has_before if i == 0 else far[:, cols]
            j, inner = (0, 1) if i == 0 else (SLICES - 1, SLICES - 2)
            add = cells[:ROWS] * (scales[1, j, :, cols] + scales[2, inner, :, cols])
            out = out - (add + (2.0 * c1[:ROWS] + beyond) * scales[2, j, :, cols])
        total[:, cols] = out

    each_tile(width, once, unroll=2)
    if forward:
        t = lax.axis_index("tm")
        chunk = refs[2].shape[1]
        for i, out in enumerate(refs[2:6]):
            out[:ROWS] = total[:, pl.ds(pl.multiple_of((t ^ i) * chunk, chunk), chunk)]
        refs[3][ROWS:] = edge_e[...]
        refs[5][ROWS:] = edge_o[...]
def last_kernel(tm_count, own, u, y1, rr, far_e, far_o, end_e, end_o, edge_e, edge_o, *refs):
    *parts, noise, gradient, out, total, beside_far, sems = refs
    odd, has_before = places(tm_count)
    width = own.shape[2]
    tiles = width // LANES
    K0, K1, K2, K3 = COEFFS
    chunk = total.shape[1]
    for i, more in enumerate(parts):
        total[...] = more[:ROWS] if i == 0 else total[...] + more[:ROWS]
    copies = [pltpu.make_async_copy(total, gradient, sems.at[0])]
    copies[0].start()
    blocks = width // chunk
    start = edge_e.shape[0] - edge_rows(blocks)
    sub = iota(8, 0)
    for i, ref in enumerate((edge_o, edge_e)):
        for b in range(blocks):
            for tile in range(chunk // LANES):
                k, at = b % 4, start + b // 4 * 8
                rows = ref[at : at + 8, tile * LANES : (tile + 1) * LANES]
                rows = jnp.where(sub < 4, down(rows, (8 - 2 * k) % 8), down(rows, 6 - 2 * k))
                beside_far[i, :, b * chunk + tile * LANES : b * chunk + (tile + 1) * LANES] = rows
    row, lane = iota(ROWS, 0), iota(ROWS, 1)

    def work(tile, cols):
        field = rr[:ROWS, cols]
        result = [own[j, :, cols] for j in range(SLICES)]
        for i, (far, end) in enumerate(((far_o, end_o), (far_e, end_e))):
            cells, beside = around(y1, i, tile, tiles)
            n0, n1 = u[i, :ROWS, cols], cells[:ROWS]
            n2 = beside[:ROWS] - field * n1
            f0 = far[:, cols]
            before = far[:, tile_at(lax.rem(tile + tiles - 1, tiles))]
            after = far[:, tile_at(lax.rem(tile + 1, tiles))]
            west = pltpu.roll(jnp.where(lane == LANES - 1, before, f0), 1, 1)
            east = pltpu.roll(jnp.where(lane == 0, after, f0), LANES - 1, 1)
            edge = jnp.concatenate([beside_far[i, :, cols]] * 2, axis=0)
            above = jnp.where(row == 0, edge, down(f0, 1))
            below = jnp.where(row == ROWS - 1, edge, down(f0, ROWS - 1))
            f1 = west + east + (above + below) - field * f0
            beyond = 3.0 * f1 + end[:, cols]
            if i == 0:
                f0, beyond = f0 * has_before, beyond * has_before
            a, b, c = (0, 1, 2) if i == 0 else (3, 2, 1)
            result[a] = result[a] + (K1 + 3.0 * K3) * n0 + K2 * (2.0 * n1 + f0) + K3 * (3.0 * n2 + beyond)
            result[b] = result[b] + K2 * n0 + K3 * (3.0 * n1 + f0)
            result[c] = result[c] + K3 * n0
        for j in range(SLICES):
            out[j, :, cols] = result[j]

    per = min(4, tiles)
    for q in range(0, tiles, per):

        def step(tile, carry):
            work(tile, tile_at(tile))
            return carry

        lax.fori_loop(q, q + per, step, 0, unroll=per)
        cols = pl.ds(q * LANES, per * LANES)
        for j in range(SLICES):
            copy = pltpu.make_async_copy(
                out.at[j, :, cols], noise.at[mirrored(odd, j), :, cols], sems.at[1 + q // per * SLICES + j]
            )
            copy.start()
            copies.append(copy)
    for copy in copies:
        copy.wait()


def body(counts, cotangent, iterates, range_field):
    tm_count, lat_count = counts
    forward = tm_count == 4
    slices, rows, width = cotangent.shape
    chunk = range_field.shape[1]
    assert slices == SLICES and rows == ROWS
    even, odd = even_pairs(tm_count), odd_pairs(tm_count)
    lat_even, lat_odd = even_pairs(lat_count), lat_odd_pairs(lat_count)
    y_pairs = [(i, i ^ 2) for i in range(tm_count)]
    one = shape_of(ROWS, width)
    extra = edge_rows(width // chunk)

    if forward:
        field = [range_field] + [lax.ppermute(range_field, "tm", pairs) for pairs in (even, y_pairs, odd)]
    else:
        field = [lax.all_gather(range_field, "tm", axis=1, tiled=True)]
    s0, s1, s2, s3 = slabs = call(first_kernel, [one] * SLICES, cotangent)
    near_e, near_o = lax.ppermute(s3, "tm", even), lax.ppermute(s0, "tm", odd)
    far_e, held, scales = call(
        scale_kernel, [one, shape_of(ROWS, chunk), shape_of(3, SLICES, ROWS, width)], s2, range_field, iterates
    )
    if forward:
        field[0] = held
    pair = shape_of(24, width)
    full, la1, lb1 = call(functools.partial(rows_kernel, forward), [one, pair, pair], *slabs, near_e, near_o, *field)
    la1, lb1 = lax.ppermute(la1, "lat", lat_even), lax.ppermute(lb1, "lat", lat_odd)
    far_e, far_o = lax.ppermute(far_e, "tm", even), lax.ppermute(s1, "tm", odd)
    end_e = lax.ppermute(s1, "tm", even)
    end_o = lax.ppermute(far_e, "tm", y_pairs) if forward else lax.ppermute(s2, "tm", odd)

    deep = shape_of(SLICES, HELD, width)
    own = shape_of(SLICES, ROWS, width)
    edge = shape_of(extra, chunk)
    grad, own, rr, edge_e, edge_o, *powers = call(
        functools.partial(own_kernel, counts),
        [one, own, shape_of(HELD, width), edge, edge, deep, deep, deep],
        *slabs,
        full,
        la1,
        lb1,
        scales,
    )
    two = shape_of(2, HELD, width)
    if forward:
        outs = [shape_of(ROWS + more, chunk) for more in (0, extra, 0, extra)]
    else:
        outs = [one]
    u, y1, *outs = call(
        functools.partial(near_kernel, counts, forward),
        [two, two] + outs,
        grad,
        near_e,
        near_o,
        far_e,
        far_o,
        la1,
        lb1,
        rr,
        edge_e,
        edge_o,
        scales,
        scratch=[pltpu.VMEM((ROWS, width), F32)] if forward else (),
    )
    own = call(
        functools.partial(third_kernel, tm_count), shape_of(SLICES, ROWS, width), own, *powers, rr, u
    )
    if forward:
        g1, g2, g3 = (lax.ppermute(g, "tm", p) for g, p in zip(outs[1:], (even, y_pairs, odd)))
        edge_e, edge_o = g1, g3
        parts = (outs[0], g1, g2, g3)
    else:
        parts = (lax.psum_scatter(outs[0], "tm", scatter_dimension=1, tiled=True),)
        edge_e, edge_o = lax.ppermute(edge_e, "tm", even), lax.ppermute(edge_o, "tm", odd)
    tiles = width // LANES
    return call(
        functools.partial(last_kernel, tm_count),
        [shape_of(SLICES, ROWS, width), shape_of(ROWS, chunk)],
        own,
        u,
        y1,
        rr,
        far_e,
        far_o,
        end_e,
        end_o,
        edge_e,
        edge_o,
        *parts,
        out_specs=[ANYWHERE, ANYWHERE],
        scratch=[
            pltpu.VMEM((SLICES, ROWS, width), F32),
            pltpu.VMEM((ROWS, chunk), F32),
            pltpu.VMEM((2, 8, width), F32),
            pltpu.SemaphoreType.DMA((1 + tiles // min(4, tiles) * SLICES,)),
        ],
    )


def solution(mesh):
    counts = (mesh.shape["tm"], mesh.shape["lat"])
    return jax.shard_map(
        functools.partial(body, counts),
        mesh=mesh,
        in_specs=(P("tm", "lat", None), P(None, "tm", "lat", None), P("lat", "tm")),
        out_specs=(P("tm", "lat", None), P("lat", "tm")),
        check_vma=False,
    )
```

time: 91.7 us -> 31.7 us (0.35)
  the two profiles are of different devices: /device:TPU:0 before, /device:TPU:8 now
where the time goes in v3:
time: 31.7 us; the launch traced here: 31.5 us
  starting transfers between devices  17.7 us (56%)
  Pallas kernels  5.24 us (17%)
  waiting for transfers between devices  4.6 us (15%)
  local copies, waits for them, and re-layouts  3.2 us (10%)
  between operations  0.73 us (2%)
    pallas_call x7, Pallas kernels, call(): pl.pallas_call(kernel, out_shape=outs, in_specs=in_specs or [IN_PLACE] *...  5.24 us
    ppermute x3, starting transfers between devices, body(): lax.ppermute(g, 'tm', p)  3.55 us
    ppermute x3, starting transfers between devices, body(): lax.ppermute(range_field, 'tm', pairs)  3.49 us
    unnamed x6, local copies, waits for them, and re-layouts  3.2 us
    ppermute x2, starting transfers between devices, body(): near_e, near_o = (lax.ppermute(s3, 'tm', even), lax.ppermute(s0, 'tm', odd))  3.05 us
    ppermute x3, waiting for transfers between devices, body(): lax.ppermute(g, 'tm', p)  2.63 us
    ppermute x1, starting transfers between devices, body(): lax.ppermute(lb1, 'lat', lat_odd)  2.45 us
    ppermute x1, starting transfers between devices, body(): lax.ppermute(s1, 'tm', odd)  1.55 us
  transfers between devices with their start and end apart: 14, of which 3 were waited for; matrix products, arithmetic and copies ran while one was open for 0% of the time, Pallas kernels for 13%

profile of v3, /device:TPU:8, one launch (start us, length us, event | category | flops | bytes accessed | tf_op | source)
XLA Modules:
  0.0 31.5 jit_solution(16672262971266381568)
XLA Ops:
  0.6 1.0 %copy-done.1 = f32[4,16,2048]{2,1,0:T(8,128)S(1)} copy-done((f32[4,16,2048]{2,1,0:T(8,128)S(1)}, f32[4,16,2048]{2,1,0:T(8,128)}, u32[]{:S(2)}) %copy-start.1) | copy-done | bytes 524312
  1.7 1.6 %collective-permute-start = (f32[16,2048]{1,0:T(8,128)S(1)}, f32[16,2048]{1,0:T(8,128)S(1)}, u32[]{:S(2)}, u32[]{:S(2)}) collective-permute-start(f32[16,2048]{1,0:T(8,128)S(1)} %get-tuple-element.29.refs_3_.s3), channel_id=1, source_target_pairs={{0,8},{8,0},{16,24},{24,16},{1,9},{9,1},{17,25},{25,17},{2,10},{10... | collective-permute-start | bytes 393224 | tf_op jit(solution)/shard_map/ppermute | solution.py:404
  3.3 1.5 %collective-permute-start.1 = (f32[16,2048]{1,0:T(8,128)S(1)}, f32[16,2048]{1,0:T(8,128)S(1)}, u32[]{:S(2)}, u32[]{:S(2)}) collective-permute-start(f32[16,2048]{1,0:T(8,128)S(1)} %get-tuple-element.26.refs_0_.s0), channel_id=1, source_target_pairs={{0,24},{8,16},{16,8},{24,0},{1,25},{9,17},{17,9},{25,1},{2,26},{10... | collective-permute-start | bytes 393224 | tf_op jit(solution)/shard_map/ppermute | solution.py:404
  4.8 1.5 %collective-permute-start.2 = (f32[16,512]{1,0:T(8,128)}, f32[16,512]{1,0:T(8,128)S(1)}, u32[]{:S(2)}, u32[]{:S(2)}) collective-permute-start(f32[16,512]{1,0:T(8,128)} %rng.1), channel_id=1, source_target_pairs={{0,8},{8,0},{16,24},{24,16},{1,9},{9,1},{17,25},{25,17},{2,10},{10... | collective-permute-start | bytes 98312 | tf_op jit(solution)/shard_map/ppermute | solution.py:400
  6.2 0.5 %collective-permute-start.3 = (f32[16,512]{1,0:T(8,128)}, f32[16,512]{1,0:T(8,128)S(1)}, u32[]{:S(2)}, u32[]{:S(2)}) collective-permute-start(f32[16,512]{1,0:T(8,128)} %rng.1), channel_id=1, source_target_pairs={{0,16},{8,24},{16,0},{24,8},{1,17},{9,25},{17,1},{25,9},{2,18},{10... | collective-permute-start | bytes 98312 | tf_op jit(solution)/shard_map/ppermute | solution.py:400
  6.8 1.5 %collective-permute-start.4 = (f32[16,512]{1,0:T(8,128)}, f32[16,512]{1,0:T(8,128)S(1)}, u32[]{:S(2)}, u32[]{:S(2)}) collective-permute-start(f32[16,512]{1,0:T(8,128)} %rng.1), channel_id=1, source_target_pairs={{0,24},{8,16},{16,8},{24,0},{1,25},{9,17},{17,9},{25,1},{2,26},{10... | collective-permute-start | bytes 98312 | tf_op jit(solution)/shard_map/ppermute | solution.py:400
  8.2 1.4 %copy-done = f32[3,4,16,2048]{3,2,1,0:T(8,128)S(1)} copy-done((f32[3,4,16,2048]{3,2,1,0:T(8,128)S(1)}, f32[3,4,16,2048]{3,2,1,0:T(8,128)}, u32[]{:S(2)}) %copy-start) | copy-done | bytes 1572888
  9.7 0.8 %copy-done.2 = f32[16,512]{1,0:T(8,128)S(1)} copy-done((f32[16,512]{1,0:T(8,128)S(1)}, f32[16,512]{1,0:T(8,128)}, u32[]{:S(2)}) %copy-start.2) | copy-done | bytes 32792
  10.4 0.4 %shard_map.51 = (f32[16,2048]{1,0:T(8,128)S(1)}, f32[16,512]{1,0:T(8,128)S(1)}, f32[3,4,16,2048]{3,2,1,0:T(8,128)S(1)}) custom-call(f32[16,2048]{1,0:T(8,128)S(1)} %get-tuple-element.28.s2.refs_2_, f32[16,512]{1,0:T(8,128)S(1)} %copy-done.2, f32[3,4,16,2048]{3,2,1,0:T(8,128)S(1)} %copy-done), custom_call_target="tpu_custom_call" | custom-call | tf_op jit(solution)/shard_map/pallas_call | solution.py:61
  10.8 0.0 collective-permute-done.2.refs_7_
  10.9 1.5 %collective-permute-start.7 = (f32[16,2048]{1,0:T(8,128)S(1)}, f32[16,2048]{1,0:T(8,128)S(1)}, u32[]{:S(2)}, u32[]{:S(2)}) collective-permute-start(f32[16,2048]{1,0:T(8,128)S(1)} %get-tuple-element.41), channel_id=1, source_target_pairs={{0,8},{8,0},{16,24},{24,16},{1,9},{9,1},{17,25},{25,17},{2,10},{10... | collective-permute-start | bytes 393224 | tf_op jit(solution)/shard_map/ppermute | solution.py:413
  12.4 0.0 collective-permute-done.3.refs_8_
  12.4 0.0 collective-permute-done.4.refs_9_
  12.4 0.0 collective-permute-done.1.refs_5_.near_o
  12.4 0.2 shard_map.52
  12.6 0.1 collective-permute-start.5
  12.7 2.4 %collective-permute-start.6 = (f32[24,2048]{1,0:T(8,128)S(1)}, f32[24,2048]{1,0:T(8,128)S(1)}, u32[]{:S(2)}, u32[]{:S(2)}) collective-permute-start(f32[24,2048]{1,0:T(8,128)S(1)} %get-tuple-element.33), channel_id=1, source_target_pairs={{0,0},{1,2},{2,1},{3,4},{4,3},{5,6},{6,5},{7,7},{8,8},{9,10},{10,9... | collective-permute-start | bytes 589832 | tf_op jit(solution)/shard_map/ppermute | solution.py:412
  15.1 1.6 %collective-permute-start.8 = (f32[16,2048]{1,0:T(8,128)S(1)}, f32[16,2048]{1,0:T(8,128)S(1)}, u32[]{:S(2)}, u32[]{:S(2)}) collective-permute-start(f32[16,2048]{1,0:T(8,128)S(1)} %get-tuple-element.27.refs_1_.s1), channel_id=1, source_target_pairs={{0,24},{8,16},{16,8},{24,0},{1,25},{9,17},{17,9},{25,1},{2,26},{10... | collective-permute-start | bytes 393224 | tf_op jit(solution)/shard_map/ppermute | solution.py:413
  16.7 1.4 %collective-permute-start.9 = (f32[16,2048]{1,0:T(8,128)S(1)}, f32[16,2048]{1,0:T(8,128)S(1)}, u32[]{:S(2)}, u32[]{:S(2)}) collective-permute-start(f32[16,2048]{1,0:T(8,128)S(1)} %get-tuple-element.27.refs_1_.s1), channel_id=1, source_target_pairs={{0,8},{8,0},{16,24},{24,16},{1,9},{9,1},{17,25},{25,17},{2,10},{10... | collective-permute-start | bytes 393224 | tf_op jit(solution)/shard_map/ppermute | solution.py:414
  18.1 0.0 collective-permute-done.7.far_e
  18.1 0.6 %collective-permute-start.10 = (f32[16,2048]{1,0:T(8,128)S(1)}, f32[16,2048]{1,0:T(8,128)S(1)}, u32[]{:S(2)}, u32[]{:S(2)}) collective-permute-start(f32[16,2048]{1,0:T(8,128)S(1)} %collective-permute-done.7.far_e), channel_id=1, source_target_pairs={{0,16},{8,24},{16,0},{24,8},{1,17},{9,25},{17,1},{25,9},{2,18},{10... | collective-permute-start | bytes 393224 | tf_op jit(solution)/shard_map/ppermute | solution.py:415
  18.7 0.0 collective-permute-done.5.la
  18.7 1.0 %collective-permute-done.6.lb = f32[24,2048]{1,0:T(8,128)S(1)} collective-permute-done((f32[24,2048]{1,0:T(8,128)S(1)}, f32[24,2048]{1,0:T(8,128)S(1)}, u32[]{:S(2)}, u32[]{:S(2)}) %collective-permute-start.6) | collective-permute-done | bytes 196640 | tf_op jit(solution)/shard_map/ppermute | solution.py:412
  19.7 1.8 %shard_map.53 = (f32[16,2048]{1,0:T(8,128)S(1)}, f32[4,16,2048]{2,1,0:T(8,128)S(1)}, f32[24,2048]{1,0:T(8,128)S(1)}, f32[8,512]{1,0:T(8,128)S(1)}, f32[8,512]{1,...) custom-call(f32[16,2048]{1,0:T(8,128)S(1)} %get-tuple-element.26.refs_0_.s0, ...), custom_call_target="tpu_custom_call" | custom-call | tf_op jit(solution)/shard_map/pallas_call | solution.py:61
  21.5 0.9 %collective-permute-done.8.far_o = f32[16,2048]{1,0:T(8,128)S(1)} collective-permute-done((f32[16,2048]{1,0:T(8,128)S(1)}, f32[16,2048]{1,0:T(8,128)S(1)}, u32[]{:S(2)}, u32[]{:S(2)}) %collective-permute-start.8) | collective-permute-done | bytes 131104 | tf_op jit(solution)/shard_map/ppermute | solution.py:413
  22.4 0.9 %shard_map.54 = (f32[2,24,2048]{2,1,0:T(8,128)S(1)}, f32[2,24,2048]{2,1,0:T(8,128)S(1)}, f32[16,512]{1,0:T(8,128)S(1)}, f32[24,512]{1,0:T(8,128)S(1)}, f32[16,512]{1,0:T(8,128)S(1)}, /*index=5*/f32[24,512]{1,0:T(8,128)S(1)}) custom-call(f32[16,2048]{1,0:T(8,128)S(1)} %get-tuple-element.40.grad, f32[16,2048]{1,0:T(8,128)S(1)} %collective-permute-done.refs_4_.near_e, ...), custom_call_target="tpu_custom_call" | custom-call | tf_op jit(solution)/shard_map/pallas_call | solution.py:61
  23.3 1.3 %collective-permute-start.11 = (f32[24,512]{1,0:T(8,128)S(1)}, f32[24,512]{1,0:T(8,128)S(1)}, u32[]{:S(2)}, u32[]{:S(2)}) collective-permute-start(f32[24,512]{1,0:T(8,128)S(1)} %get-tuple-element.46), channel_id=1, source_target_pairs={{0,8},{8,0},{16,24},{24,16},{1,9},{9,1},{17,25},{25,17},{2,10},{10... | collective-permute-start | bytes 147464 | tf_op jit(solution)/shard_map/ppermute | solution.py:454
  24.6 1.7 %collective-permute-start.12 = (f32[24,512]{1,0:T(8,128)S(1)}, f32[24,512]{1,0:T(8,128)S(1)}, u32[]{:S(2)}, u32[]{:S(2)}) collective-permute-start(f32[24,512]{1,0:T(8,128)S(1)} %get-tuple-element.47), channel_id=1, source_target_pairs={{0,24},{8,16},{16,8},{24,0},{1,25},{9,17},{17,9},{25,1},{2,26},{10... | collective-permute-start | bytes 147464 | tf_op jit(solution)/shard_map/ppermute | solution.py:454
  26.3 0.6 %collective-permute-start.13 = (f32[16,512]{1,0:T(8,128)S(1)}, f32[16,512]{1,0:T(8,128)S(1)}, u32[]{:S(2)}, u32[]{:S(2)}) collective-permute-start(f32[16,512]{1,0:T(8,128)S(1)} %get-tuple-element.49), channel_id=1, source_target_pairs={{0,16},{8,24},{16,0},{24,8},{1,17},{9,25},{17,1},{25,9},{2,18},{10... | collective-permute-start | bytes 98312 | tf_op jit(solution)/shard_map/ppermute | solution.py:454
  26.9 0.7 %shard_map.55.own = f32[4,16,2048]{2,1,0:T(8,128)S(1)} custom-call(f32[4,16,2048]{2,1,0:T(8,128)S(1)} %get-tuple-element.35.noise, f32[4,24,2048]{2,1,0:T(8,128)S(1)} %get-tuple-element.36.u, f32[4,24,2048]{2,1,0:T(8,128)S(1)} %get-tuple-element.37.y1, f32[4,24,2048]{2,1,0:T(8,128)S(1)} %get-tuple-element.38.y2, f32[24,2048]{1,0:T(8,128)S(1)} %get-tuple-element.39.rr, ...), custom_call_target="tpu_custom_call" | custom-call | tf_op jit(solution)/shard_map/pallas_call | solution.py:61
  27.6 2.6 %collective-permute-done.13.refs_2_ = f32[16,512]{1,0:T(8,128)S(1)} collective-permute-done((f32[16,512]{1,0:T(8,128)S(1)}, f32[16,512]{1,0:T(8,128)S(1)}, u32[]{:S(2)}, u32[]{:S(2)}) %collective-permute-start.13) | collective-permute-done | bytes 32800 | tf_op jit(solution)/shard_map/ppermute | solution.py:454
  30.2 1.2 %shard_map.56 = (f32[4,16,2048]{2,1,0:T(8,128)}, f32[16,512]{1,0:T(8,128)}) custom-call(f32[4,16,2048]{2,1,0:T(8,128)S(1)} %shard_map.55.own, f32[2,24,2048]{2,1,0:T(8,128)S(1)} %get-tuple-element.44._.u, f32[2,24,2048]{2,1,0:T(8,128)S(1)} %get-tuple-element.45.y1, f32[24,2048]{1,0:T(8,128)S(1)} %get-tuple-element.39.rr, ...), custom_call_target="tpu_custom_call" | custom-call | tf_op jit(solution)/shard_map/pallas_call | solution.py:61
  (9 shorter events, 0.1 us)
Async XLA Ops:
  0.6 1.0 %copy-start.1 = (f32[4,16,2048]{2,1,0:T(8,128)S(1)}, f32[4,16,2048]{2,1,0:T(8,128)}, u32[]{:S(2)}) copy-start(f32[4,16,2048]{2,1,0:T(8,128)} %cot.1) | copy-start | bytes 1572868
  1.7 10.7 %collective-permute-start = (f32[16,2048]{1,0:T(8,128)S(1)}, f32[16,2048]{1,0:T(8,128)S(1)}, u32[]{:S(2)}, u32[]{:S(2)}) collective-permute-start(f32[16,2048]{1,0:T(8,128)S(1)} %get-tuple-element.29.refs_3_.s3), channel_id=1, source_target_pairs={{0,8},{8,0},{16,24},{24,16},{1,9},{9,1},{17,25},{25,17},{2,10},{10... | collective-permute-start | bytes 393224 | tf_op jit(solution)/shard_map/ppermute | solution.py:404
  3.3 9.2 %collective-permute-start.1 = (f32[16,2048]{1,0:T(8,128)S(1)}, f32[16,2048]{1,0:T(8,128)S(1)}, u32[]{:S(2)}, u32[]{:S(2)}) collective-permute-start(f32[16,2048]{1,0:T(8,128)S(1)} %get-tuple-element.26.refs_0_.s0), channel_id=1, source_target_pairs={{0,24},{8,16},{16,8},{24,0},{1,25},{9,17},{17,9},{25,1},{2,26},{10... | collective-permute-start | bytes 393224 | tf_op jit(solution)/shard_map/ppermute | solution.py:404
  4.8 6.1 %collective-permute-start.2 = (f32[16,512]{1,0:T(8,128)}, f32[16,512]{1,0:T(8,128)S(1)}, u32[]{:S(2)}, u32[]{:S(2)}) collective-permute-start(f32[16,512]{1,0:T(8,128)} %rng.1), channel_id=1, source_target_pairs={{0,8},{8,0},{16,24},{24,16},{1,9},{9,1},{17,25},{25,17},{2,10},{10... | collective-permute-start | bytes 98312 | tf_op jit(solution)/shard_map/ppermute | solution.py:400
  6.2 6.2 %collective-permute-start.3 = (f32[16,512]{1,0:T(8,128)}, f32[16,512]{1,0:T(8,128)S(1)}, u32[]{:S(2)}, u32[]{:S(2)}) collective-permute-start(f32[16,512]{1,0:T(8,128)} %rng.1), channel_id=1, source_target_pairs={{0,16},{8,24},{16,0},{24,8},{1,17},{9,25},{17,1},{25,9},{2,18},{10... | collective-permute-start | bytes 98312 | tf_op jit(solution)/shard_map/ppermute | solution.py:400
  6.8 5.7 %collective-permute-start.4 = (f32[16,512]{1,0:T(8,128)}, f32[16,512]{1,0:T(8,128)S(1)}, u32[]{:S(2)}, u32[]{:S(2)}) collective-permute-start(f32[16,512]{1,0:T(8,128)} %rng.1), channel_id=1, source_target_pairs={{0,24},{8,16},{16,8},{24,0},{1,25},{9,17},{17,9},{25,1},{2,26},{10... | collective-permute-start | bytes 98312 | tf_op jit(solution)/shard_map/ppermute | solution.py:400
  8.2 1.4 %copy-start = (f32[3,4,16,2048]{3,2,1,0:T(8,128)S(1)}, f32[3,4,16,2048]{3,2,1,0:T(8,128)}, u32[]{:S(2)}) copy-start(f32[3,4,16,2048]{3,2,1,0:T(8,128)} %its.1) | copy-start | bytes 4718596
  9.7 0.8 %copy-start.2 = (f32[16,512]{1,0:T(8,128)S(1)}, f32[16,512]{1,0:T(8,128)}, u32[]{:S(2)}) copy-start(f32[16,512]{1,0:T(8,128)} %rng.1) | copy-start | bytes 98308
  10.9 7.3 %collective-permute-start.7 = (f32[16,2048]{1,0:T(8,128)S(1)}, f32[16,2048]{1,0:T(8,128)S(1)}, u32[]{:S(2)}, u32[]{:S(2)}) collective-permute-start(f32[16,2048]{1,0:T(8,128)S(1)} %get-tuple-element.41), channel_id=1, source_target_pairs={{0,8},{8,0},{16,24},{24,16},{1,9},{9,1},{17,25},{25,17},{2,10},{10... | collective-permute-start | bytes 393224 | tf_op jit(solution)/shard_map/ppermute | solution.py:413
  12.6 6.1 %collective-permute-start.5 = (f32[24,2048]{1,0:T(8,128)S(1)}, f32[24,2048]{1,0:T(8,128)S(1)}, u32[]{:S(2)}, u32[]{:S(2)}) collective-permute-start(f32[24,2048]{1,0:T(8,128)S(1)} %get-tuple-element.32), channel_id=1, source_target_pairs={{0,1},{1,0},{2,3},{3,2},{4,5},{5,4},{6,7},{7,6},{8,9},{9,8},{10,11... | collective-permute-start | bytes 589832 | tf_op jit(solution)/shard_map/ppermute | solution.py:412
  12.7 7.0 %collective-permute-start.6 = (f32[24,2048]{1,0:T(8,128)S(1)}, f32[24,2048]{1,0:T(8,128)S(1)}, u32[]{:S(2)}, u32[]{:S(2)}) collective-permute-start(f32[24,2048]{1,0:T(8,128)S(1)} %get-tuple-element.33), channel_id=1, source_target_pairs={{0,0},{1,2},{2,1},{3,4},{4,3},{5,6},{6,5},{7,7},{8,8},{9,10},{10,9... | collective-permute-start | bytes 589832 | tf_op jit(solution)/shard_map/ppermute | solution.py:412
  15.1 7.2 %collective-permute-start.8 = (f32[16,2048]{1,0:T(8,128)S(1)}, f32[16,2048]{1,0:T(8,128)S(1)}, u32[]{:S(2)}, u32[]{:S(2)}) collective-permute-start(f32[16,2048]{1,0:T(8,128)S(1)} %get-tuple-element.27.refs_1_.s1), channel_id=1, source_target_pairs={{0,24},{8,16},{16,8},{24,0},{1,25},{9,17},{17,9},{25,1},{2,26},{10... | collective-permute-start | bytes 393224 | tf_op jit(solution)/shard_map/ppermute | solution.py:413
  16.7 10.9 %collective-permute-start.9 = (f32[16,2048]{1,0:T(8,128)S(1)}, f32[16,2048]{1,0:T(8,128)S(1)}, u32[]{:S(2)}, u32[]{:S(2)}) collective-permute-start(f32[16,2048]{1,0:T(8,128)S(1)} %get-tuple-element.27.refs_1_.s1), channel_id=1, source_target_pairs={{0,8},{8,0},{16,24},{24,16},{1,9},{9,1},{17,25},{25,17},{2,10},{10... | collective-permute-start | bytes 393224 | tf_op jit(solution)/shard_map/ppermute | solution.py:414
  18.1 9.5 %collective-permute-start.10 = (f32[16,2048]{1,0:T(8,128)S(1)}, f32[16,2048]{1,0:T(8,128)S(1)}, u32[]{:S(2)}, u32[]{:S(2)}) collective-permute-start(f32[16,2048]{1,0:T(8,128)S(1)} %collective-permute-done.7.far_e), channel_id=1, source_target_pairs={{0,16},{8,24},{16,0},{24,8},{1,17},{9,25},{17,1},{25,9},{2,18},{10... | collective-permute-start | bytes 393224 | tf_op jit(solution)/shard_map/ppermute | solution.py:415
  23.3 6.9 %collective-permute-start.11 = (f32[24,512]{1,0:T(8,128)S(1)}, f32[24,512]{1,0:T(8,128)S(1)}, u32[]{:S(2)}, u32[]{:S(2)}) collective-permute-start(f32[24,512]{1,0:T(8,128)S(1)} %get-tuple-element.46), channel_id=1, source_target_pairs={{0,8},{8,0},{16,24},{24,16},{1,9},{9,1},{17,25},{25,17},{2,10},{10... | collective-permute-start | bytes 147464 | tf_op jit(solution)/shard_map/ppermute | solution.py:454
  24.6 5.6 %collective-permute-start.12 = (f32[24,512]{1,0:T(8,128)S(1)}, f32[24,512]{1,0:T(8,128)S(1)}, u32[]{:S(2)}, u32[]{:S(2)}) collective-permute-start(f32[24,512]{1,0:T(8,128)S(1)} %get-tuple-element.47), channel_id=1, source_target_pairs={{0,24},{8,16},{16,8},{24,0},{1,25},{9,17},{17,9},{25,1},{2,26},{10... | collective-permute-start | bytes 147464 | tf_op jit(solution)/shard_map/ppermute | solution.py:454
  26.3 3.9 %collective-permute-start.13 = (f32[16,512]{1,0:T(8,128)S(1)}, f32[16,512]{1,0:T(8,128)S(1)}, u32[]{:S(2)}, u32[]{:S(2)}) collective-permute-start(f32[16,512]{1,0:T(8,128)S(1)} %get-tuple-element.49), channel_id=1, source_target_pairs={{0,16},{8,24},{16,0},{24,8},{1,17},{9,25},{17,1},{25,9},{2,18},{10... | collective-permute-start | bytes 98312 | tf_op jit(solution)/shard_map/ppermute | solution.py:454

commit v4 on v3

--- a/solution.py
+++ b/solution.py
@@ -44,8 +44,23 @@
     return [(i, (i + 1) % count if i % 2 else (i - 1) % count) for i in range(count)]
 
 
-def lat_odd_pairs(count):
-    return [(i, i if i in (0, count - 1) else other) for i, other in odd_pairs(count)]
+def lat_odd_pairs(tm_count, lat_count):
+    ring = {0: 1, 1: 3, 3: 2, 2: 0} if tm_count == 4 else dict(even_pairs(tm_count))
+    pairs = []
+    for t in range(tm_count):
+        for l, (_, other) in enumerate(odd_pairs(lat_count)):
+            end = l in (0, lat_count - 1)
+            pairs.append((t * lat_count + l, ring[t] * lat_count + l if end else t * lat_count + other))
+    return pairs
+
+
+def inner_odd_pairs(tm_count, lat_count):
+    pairs = []
+    for t, (_, other) in enumerate(odd_pairs(tm_count)):
+        for l in range(lat_count):
+            end = t in (0, tm_count - 1)
+            pairs.append((t * lat_count + l, t * lat_count + (l ^ 1) if end else other * lat_count + l))
+    return pairs
 
 
 def shape_of(*dims):
@@ -116,36 +131,49 @@
     return jnp.where(odd == 1, SLICES - 1 - j, j)
 
 
-def first_kernel(cot, *slabs):
-    odd, _ = places(2)
-    for j in range(SLICES):
-        slabs[j][...] = cot[pl.ds(mirrored(odd, j), 1)][0]
-
-
-def scale_kernel(s2, rng, its, far_e, held, scales):
-    far_e[...] = s2[...]
+def corner_rows(blocks):
+    return 8 * (blocks // 2)
+
+
+def corner_kernel(s0, s1, s2, s3, rng, even_out, odd_out, held, even_two, odd_two):
     held[...] = rng[...]
-    odd, _ = places(2)
-
-    def work(tile, cols):
-        for j in range(SLICES):
-            x1, x2, x3 = (its[k, pl.ds(mirrored(odd, j), 1), :, cols][0] for k in range(3))
-            scales[0, j, :, cols] = W3 * x3 + W2 * x2 + W1 * x1
-            scales[1, j, :, cols] = (W2 * W3) * x2 + (W1 * SUM2) * x1
-            scales[2, j, :, cols] = (W1 * PROD2) * x1
-
-    each_tile(s2.shape[1], work)
+    for out, cells in ((even_two, (s3, s2)), (odd_two, (s0, s1))):
+        for i in range(2):
+            out[i * ROWS : (i + 1) * ROWS] = cells[i][...]
+    chunk = rng.shape[1]
+    per = chunk // LANES
+    half = s0.shape[1] // 2
+    sub = iota(8, 0)
+    for cells, out in ((s3, even_out), (s0, odd_out)):
+        out[:ROWS] = rng[...]
+        for tile in range(half // LANES):
+            left, right = (
+                jnp.where(sub < 4, cells[:8, cols], cells[ROWS - 8 :, cols])
+                for cols in (pl.ds(at + tile * LANES, LANES) for at in (0, half))
+            )
+            at = ROWS + tile // per * 8
+            inner = (sub >= 2) & (sub < 6)
+            out[at : at + 8, tile % per * LANES : (tile % per + 1) * LANES] = jnp.where(inner, down(right, 4), left)
+
+
+def corners(message, tile, tiles):
+    half, per = tiles // 2, message.shape[1] // LANES
+    place = lax.rem(tile, half)
+    at = pl.multiple_of(ROWS + lax.div(place, per) * 8, 8)
+    rows = message[pl.ds(at, 8), tile_at(lax.rem(place, per))]
+    return jnp.where(tile < half, rows, down(rows, 4))
 
 
 def rows_kernel(forward, *refs):
     slabs, (near_e, near_o), refs = refs[:SLICES], refs[SLICES : SLICES + 2], refs[SLICES + 2 :]
+    tiles = slabs[0].shape[1] // LANES
     even_lat, _, _ = lat_places(2)
     *field, full, la, lb = refs
     if forward:
         t = lax.axis_index("tm")
         chunk = field[0].shape[1]
-        for i, piece in enumerate(field):
-            full[:, pl.ds(pl.multiple_of((t ^ i) * chunk, chunk), chunk)] = piece[...]
+        for i, piece in enumerate((field[0], near_e, field[1], near_o)):
+            full[:, pl.ds(pl.multiple_of((t ^ i) * chunk, chunk), chunk)] = piece[:ROWS]
     else:
         full[...] = field[0][...]
     sub = iota(8, 0)
@@ -159,8 +187,9 @@
             last = jnp.where(sub > 4, one[8:, cols], last)
             la[8 * i : 8 * i + 8, cols] = jnp.where(even_lat, last, first)
             lb[8 * i : 8 * i + 8, cols] = jnp.where(even_lat, first, last)
-        first = jnp.where(sub < 2, near_e[:8, cols], down(near_o[:8, cols], 2))
-        last = jnp.where(sub >= 6, near_e[8:, cols], down(near_o[8:, cols], 6))
+        from_e, from_o = (corners(ref, tile, tiles) for ref in (near_e, near_o))
+        first = jnp.where(sub < 2, from_e, down(from_o, 2))
+        last = jnp.where(sub >= 6, from_e, down(from_o, 6))
         la[16:, cols] = jnp.where(even_lat, last, first)
         lb[16:, cols] = jnp.where(even_lat, first, last)
 
@@ -187,7 +216,7 @@
     return cells[j] if 0 <= j < SLICES else 0.0
 
 
-def own_kernel(counts, s0, s1, s2, s3, full, la, lb, scales, grad, noise, rr, edge_e, edge_o, u, y1, y2):
+def own_kernel(counts, s0, s1, s2, s3, full, la, lb, by0, by1, by2, grad, noise, rr, edge_e, edge_o, u, y1, y2, end_e, end_o):
     tm_count, lat_count = counts
     K0, K1, K2, _ = COEFFS
     odd, has_before = places(tm_count)
@@ -195,6 +224,9 @@
     tiles = width // LANES
     mask = lat_mask(lat_count)
     back = 1.0 + has_before
+
+    end_e[...] = s1[...]
+    end_o[...] = s2[...]
 
     def gather(tile, cols):
         first, last = below_above(lat_count, la, lb, 0, cols)
@@ -230,7 +262,8 @@
             one = c1[j] + (at(c0, j - 1) + at(c0, j + 1))
             two = c2[:ROWS] + 2.0 * (at(c1, j - 1) + at(c1, j + 1))
             two = two + (back if j == 0 else 2.0) * c0[j] + (at(c0, j - 2) + at(c0, j + 2))
-            total = total + c0[j] * scales[0, j, :, cols] + one * scales[1, j, :, cols] + two * scales[2, j, :, cols]
+            place = pl.ds(mirrored(odd, j), 1)
+            total = total + c0[j] * by0[place, :, cols][0] + one * by1[place, :, cols][0] + two * by2[place, :, cols][0]
             noise[j, :, cols] = K0 * c0[j] + K1 * one + K2 * two
         grad[:, cols] = -total
 
@@ -279,7 +312,7 @@
     return (2 * blocks + 7) // 8 * 8
 
 
-def near_kernel(counts, forward, grad, near_e, near_o, far_e, far_o, la, lb, rr, edge_e, edge_o, scales, *refs):
+def near_kernel(counts, forward, grad, near_e, near_o, la, lb, rr, edge_e, edge_o, by1, by2, *refs):
     tm_count, lat_count = counts
     odd, has_before = places(tm_count)
     width = grad.shape[1]
@@ -290,22 +323,23 @@
 
     def gather(tile, cols):
         below, above = below_above(lat_count, la, lb, 16, cols)
-        u[0, :, cols] = joined(near_o[:, cols], down(below, 6), down(above, 2)) * has_before
-        u[1, :, cols] = joined(near_e[:, cols], below, above)
+        u[0, :, cols] = joined(near_o[:ROWS, cols], down(below, 6), down(above, 2)) * has_before
+        u[1, :, cols] = joined(near_e[:ROWS, cols], below, above)
 
     each_tile(width, gather)
 
     def once(tile, cols):
         field = rr[:, cols]
         out = grad[:, cols]
-        for i, far in enumerate((far_o, far_e)):
+        for i, two in enumerate((near_o, near_e)):
             cells, beside = around(u, i, tile, tiles)
             c1 = (beside - field * cells) * mask
             y1[i, :, cols] = c1
-            beyond = far[:, cols] * has_before if i == 0 else far[:, cols]
+            beyond = two[ROWS:, cols] * has_before if i == 0 else two[ROWS:, cols]
             j, inner = (0, 1) if i == 0 else (SLICES - 1, SLICES - 2)
-            add = cells[:ROWS] * (scales[1, j, :, cols] + scales[2, inner, :, cols])
-            out = out - (add + (2.0 * c1[:ROWS] + beyond) * scales[2, j, :, cols])
+            j, inner = pl.ds(mirrored(odd, j), 1), pl.ds(mirrored(odd, inner), 1)
+            add = cells[:ROWS] * (by1[j, :, cols][0] + by2[inner, :, cols][0])
+            out = out - (add + (2.0 * c1[:ROWS] + beyond) * by2[j, :, cols][0])
         total[:, cols] = out
 
     each_tile(width, once, unroll=2)
@@ -316,7 +350,7 @@
             out[:ROWS] = total[:, pl.ds(pl.multiple_of((t ^ i) * chunk, chunk), chunk)]
         refs[3][ROWS:] = edge_e[...]
         refs[5][ROWS:] = edge_o[...]
-def last_kernel(tm_count, own, u, y1, rr, far_e, far_o, end_e, end_o, edge_e, edge_o, *refs):
+def last_kernel(tm_count, own, u, y1, rr, near_e, near_o, end_e, end_o, edge_e, edge_o, *refs):
     *parts, noise, gradient, out, total, beside_far, sems = refs
     odd, has_before = places(tm_count)
     width = own.shape[2]
@@ -342,13 +376,13 @@
     def work(tile, cols):
         field = rr[:ROWS, cols]
         result = [own[j, :, cols] for j in range(SLICES)]
-        for i, (far, end) in enumerate(((far_o, end_o), (far_e, end_e))):
+        for i, (far, end) in enumerate(((near_o, end_o), (near_e, end_e))):
             cells, beside = around(y1, i, tile, tiles)
             n0, n1 = u[i, :ROWS, cols], cells[:ROWS]
             n2 = beside[:ROWS] - field * n1
-            f0 = far[:, cols]
-            before = far[:, tile_at(lax.rem(tile + tiles - 1, tiles))]
-            after = far[:, tile_at(lax.rem(tile + 1, tiles))]
+            f0 = far[ROWS:, cols]
+            before = far[ROWS:, tile_at(lax.rem(tile + tiles - 1, tiles))]
+            after = far[ROWS:, tile_at(lax.rem(tile + 1, tiles))]
             west = pltpu.roll(jnp.where(lane == LANES - 1, before, f0), 1, 1)
             east = pltpu.roll(jnp.where(lane == 0, after, f0), LANES - 1, 1)
             edge = jnp.concatenate([beside_far[i, :, cols]] * 2, axis=0)
@@ -391,60 +425,62 @@
     chunk = range_field.shape[1]
     assert slices == SLICES and rows == ROWS
     even, odd = even_pairs(tm_count), odd_pairs(tm_count)
-    lat_even, lat_odd = even_pairs(lat_count), lat_odd_pairs(lat_count)
+    lat_even, lat_odd = even_pairs(lat_count), lat_odd_pairs(tm_count, lat_count)
+    inner = inner_odd_pairs(tm_count, lat_count)
     y_pairs = [(i, i ^ 2) for i in range(tm_count)]
     one = shape_of(ROWS, width)
     extra = edge_rows(width // chunk)
 
+    flip = lax.rem(lax.axis_index("tm"), 2) == 1
+    slabs = [
+        lax.dynamic_index_in_dim(cotangent, jnp.where(flip, SLICES - 1 - j, j), 0, False) for j in range(SLICES)
+    ]
+    message = shape_of(ROWS + corner_rows(width // chunk), chunk)
+    two = shape_of(2 * ROWS, width)
+    corner_e, corner_o, held, near_e, near_o = call(
+        corner_kernel, [message, message, shape_of(ROWS, chunk), two, two], *slabs, range_field
+    )
+    corner_e, corner_o = lax.ppermute(corner_e, "tm", even), lax.ppermute(corner_o, "tm", odd)
     if forward:
-        field = [range_field] + [lax.ppermute(range_field, "tm", pairs) for pairs in (even, y_pairs, odd)]
+        field = [held, lax.ppermute(range_field, "tm", y_pairs)]
     else:
         field = [lax.all_gather(range_field, "tm", axis=1, tiled=True)]
-    s0, s1, s2, s3 = slabs = call(first_kernel, [one] * SLICES, cotangent)
-    near_e, near_o = lax.ppermute(s3, "tm", even), lax.ppermute(s0, "tm", odd)
-    far_e, held, scales = call(
-        scale_kernel, [one, shape_of(ROWS, chunk), shape_of(3, SLICES, ROWS, width)], s2, range_field, iterates
-    )
-    if forward:
-        field[0] = held
+    near_e, near_o = lax.ppermute(near_e, "tm", even), lax.ppermute(near_o, ("tm", "lat"), inner)
+    x1, x2, x3 = iterates[0], iterates[1], iterates[2]
+    scales = (W3 * x3 + W2 * x2 + W1 * x1, (W2 * W3) * x2 + (W1 * SUM2) * x1, (W1 * PROD2) * x1)
     pair = shape_of(24, width)
-    full, la1, lb1 = call(functools.partial(rows_kernel, forward), [one, pair, pair], *slabs, near_e, near_o, *field)
-    la1, lb1 = lax.ppermute(la1, "lat", lat_even), lax.ppermute(lb1, "lat", lat_odd)
-    far_e, far_o = lax.ppermute(far_e, "tm", even), lax.ppermute(s1, "tm", odd)
-    end_e = lax.ppermute(s1, "tm", even)
-    end_o = lax.ppermute(far_e, "tm", y_pairs) if forward else lax.ppermute(s2, "tm", odd)
-
+    full, la1, lb1 = call(functools.partial(rows_kernel, forward), [one, pair, pair], *slabs, corner_e, corner_o, *field)
+    la1, lb1 = lax.ppermute(la1, "lat", lat_even), lax.ppermute(lb1, ("tm", "lat"), lat_odd)
     deep = shape_of(SLICES, HELD, width)
     own = shape_of(SLICES, ROWS, width)
     edge = shape_of(extra, chunk)
-    grad, own, rr, edge_e, edge_o, *powers = call(
+    grad, own, rr, edge_e, edge_o, *powers, end_e, end_o = call(
         functools.partial(own_kernel, counts),
-        [one, own, shape_of(HELD, width), edge, edge, deep, deep, deep],
+        [one, own, shape_of(HELD, width), edge, edge, deep, deep, deep, one, one],
         *slabs,
         full,
         la1,
         lb1,
-        scales,
+        *scales,
     )
-    two = shape_of(2, HELD, width)
+    end_e, end_o = lax.ppermute(end_e, "tm", even), lax.ppermute(end_o, ("tm", "lat"), inner)
+    pair = shape_of(2, HELD, width)
     if forward:
         outs = [shape_of(ROWS + more, chunk) for more in (0, extra, 0, extra)]
     else:
         outs = [one]
     u, y1, *outs = call(
         functools.partial(near_kernel, counts, forward),
-        [two, two] + outs,
+        [pair, pair] + outs,
         grad,
         near_e,
         near_o,
-        far_e,
-        far_o,
         la1,
         lb1,
         rr,
         edge_e,
         edge_o,
-        scales,
+        *scales[1:],
         scratch=[pltpu.VMEM((ROWS, width), F32)] if forward else (),
     )
     own = call(
@@ -465,8 +501,8 @@
         u,
         y1,
         rr,
-        far_e,
-        far_o,
+        near_e,
+        near_o,
         end_e,
         end_o,
         edge_e,

time: 31.7 us -> 30.8 us (0.972)
  the two profiles are of different devices: /device:TPU:8 before, /device:TPU:0 now
where the time goes in v4:
time: 30.8 us; the launch traced here: 30.6 us
  starting transfers between devices  13.1 us (43%)
  waiting for transfers between devices  8.31 us (27%)
  Pallas kernels  4.95 us (16%)
  local copies, waits for them, and re-layouts  1.89 us (6%)
  other arithmetic  1.61 us (5%)
  between operations  0.73 us (2%)
    pallas_call x6, Pallas kernels, call(): pl.pallas_call(kernel, out_shape=outs, in_specs=in_specs or [IN_PLACE] *...  4.95 us
    ppermute x3, starting transfers between devices, body(): lax.ppermute(g, 'tm', p)  3.64 us
    ppermute x3, waiting for transfers between devices, body(): lax.ppermute(g, 'tm', p)  3.09 us
    ppermute x1, starting transfers between devices, body(): lax.ppermute(corner_e, 'tm', even)  3 us
    ppermute x1, waiting for transfers between devices, body(): lax.ppermute(lb1, ('tm', 'lat'), lat_odd)  2.91 us
    ppermute x1, waiting for transfers between devices, body(): field = [held, lax.ppermute(range_field, 'tm', y_pairs)]  2.26 us
    ppermute x1, starting transfers between devices, body(): lax.ppermute(near_e, 'tm', even)  1.95 us
    ppermute x1, starting transfers between devices, body(): lax.ppermute(end_e, 'tm', even)  1.72 us
  transfers between devices with their start and end apart: 12, of which 3 were waited for; matrix products, arithmetic and copies ran while one was open for 5% of the time, Pallas kernels for 12%

profile of v4, /device:TPU:0, one launch (start us, length us, event | category | flops | bytes accessed | tf_op | source)
XLA Modules:
  0.0 30.6 jit_solution(17571318517773884469)
XLA Ops:
  0.6 1.1 %dynamic-slice_bitcast_fusion = (f32[16,2048]{1,0:T(8,128)S(1)}, f32[16,2048]{1,0:T(8,128)S(1)}, f32[16,2048]{1,0:T(8,128)S(1)}, f32[16,2048]{1,0:T(8,128)S(1)}) fusion(f32[4,16,2048]{2,1,0:T(8,128)} %param.3, s32[]{:T(128)S(6)} %select_n.21, s32[]{:T(128)S(6)} %select_n.19, s32[]{:T(128)S(6)} %select_n.18, s32[]{:T(128)S(6)} %select_n.20), kind=kLoop, calls=%fused_computation.3 | loop fusion | bytes 1048592 | tf_op jit(solution)/shard_map/jit(dynamic_index_in_dim)/squeeze | solution.py:436
  1.8 0.0 copy-start
  1.8 0.7 %copy-done = f32[16,512]{1,0:T(8,128)S(1)} copy-done((f32[16,512]{1,0:T(8,128)S(1)}, f32[16,512]{1,0:T(8,128)}, u32[]{:S(2)}) %copy-start) | copy-done | bytes 32792
  2.6 3.0 %collective-permute-start = (f32[32,512]{1,0:T(8,128)S(1)}, f32[32,512]{1,0:T(8,128)S(1)}, u32[]{:S(2)}, u32[]{:S(2)}) collective-permute-start(f32[32,512]{1,0:T(8,128)S(1)} %get-tuple-element.26), channel_id=1, source_target_pairs={{0,8},{8,0},{16,24},{24,16},{1,9},{9,1},{17,25},{25,17},{2,10},{10... | collective-permute-start | bytes 196616 | tf_op jit(solution)/shard_map/ppermute | solution.py:443
  5.6 1.5 %collective-permute-start.1 = (f32[32,512]{1,0:T(8,128)S(1)}, f32[32,512]{1,0:T(8,128)S(1)}, u32[]{:S(2)}, u32[]{:S(2)}) collective-permute-start(f32[32,512]{1,0:T(8,128)S(1)} %get-tuple-element.27), channel_id=1, source_target_pairs={{0,24},{8,16},{16,8},{24,0},{1,25},{9,17},{17,9},{25,1},{2,26},{10... | collective-permute-start | bytes 196616 | tf_op jit(solution)/shard_map/ppermute | solution.py:443
  7.1 0.1 collective-permute-start.2
  7.1 1.9 %collective-permute-start.5 = (f32[32,2048]{1,0:T(8,128)S(1)}, f32[32,2048]{1,0:T(8,128)S(1)}, u32[]{:S(2)}, u32[]{:S(2)}) collective-permute-start(f32[32,2048]{1,0:T(8,128)S(1)} %get-tuple-element.38), channel_id=1, source_target_pairs={{0,8},{8,0},{16,24},{24,16},{1,9},{9,1},{17,25},{25,17},{2,10},{10... | collective-permute-start | bytes 786440 | tf_op jit(solution)/shard_map/ppermute | solution.py:448
  9.1 0.0 collective-permute-start.6
  9.1 2.3 %collective-permute-done.2.refs_7_ = f32[16,512]{1,0:T(8,128)S(1)} collective-permute-done((f32[16,512]{1,0:T(8,128)S(1)}, f32[16,512]{1,0:T(8,128)S(1)}, u32[]{:S(2)}, u32[]{:S(2)}) %collective-permute-start.2) | collective-permute-done | bytes 32800 | tf_op jit(solution)/shard_map/ppermute | solution.py:445
  11.4 0.0 collective-permute-done.refs_4_
  11.4 0.0 collective-permute-done.1.refs_5_
  11.4 0.2 shard_map.51
  11.6 0.1 collective-permute-start.3
  11.7 1.2 %collective-permute-start.4 = (f32[24,2048]{1,0:T(8,128)S(1)}, f32[24,2048]{1,0:T(8,128)S(1)}, u32[]{:S(2)}, u32[]{:S(2)}) collective-permute-start(f32[24,2048]{1,0:T(8,128)S(1)} %get-tuple-element.31), channel_id=1, source_target_pairs={{0,8},{1,2},{2,1},{3,4},{4,3},{5,6},{6,5},{7,15},{8,24},{9,10},{10... | collective-permute-start | bytes 589832 | tf_op jit(solution)/shard_map/ppermute | solution.py:453
  12.9 1.6 %multiply_bitcast_fusion = (f32[4,16,2048]{2,1,0:T(8,128)S(1)}, f32[4,16,2048]{2,1,0:T(8,128)S(1)}, f32[4,16,2048]{2,1,0:T(8,128)S(1)}) fusion(f32[3,4,16,2048]{3,2,1,0:T(8,128)} %param.4), kind=kLoop, calls=%fused_computation | loop fusion | flops 1179648 | bytes 3145728 | tf_op jit(solution)/shard_map/mul | solution.py:450
  14.5 0.0 collective-permute-done.3.la
  14.5 2.9 %collective-permute-done.4.lb = f32[24,2048]{1,0:T(8,128)S(1)} collective-permute-done((f32[24,2048]{1,0:T(8,128)S(1)}, f32[24,2048]{1,0:T(8,128)S(1)}, u32[]{:S(2)}, u32[]{:S(2)}) %collective-permute-start.4) | collective-permute-done | bytes 196640 | tf_op jit(solution)/shard_map/ppermute | solution.py:453
  17.4 1.8 %shard_map.52 = (f32[16,2048]{1,0:T(8,128)S(1)}, f32[4,16,2048]{2,1,0:T(8,128)S(1)}, f32[24,2048]{1,0:T(8,128)S(1)}, f32[8,512]{1,0:T(8,128)S(1)}, f32[8,512]{1,...) custom-call(f32[16,2048]{1,0:T(8,128)S(1)} %get-tuple-element.55.s0., ...), custom_call_target="tpu_custom_call" | custom-call | tf_op jit(solution)/shard_map/pallas_call | solution.py:76
  19.2 1.7 %collective-permute-start.7 = (f32[16,2048]{1,0:T(8,128)S(1)}, f32[16,2048]{1,0:T(8,128)S(1)}, u32[]{:S(2)}, u32[]{:S(2)}) collective-permute-start(f32[16,2048]{1,0:T(8,128)S(1)} %get-tuple-element.44), channel_id=1, source_target_pairs={{0,8},{8,0},{16,24},{24,16},{1,9},{9,1},{17,25},{25,17},{2,10},{10... | collective-permute-start | bytes 393224 | tf_op jit(solution)/shard_map/ppermute | solution.py:466
  21.0 0.0 collective-permute-start.8
  21.0 0.0 collective-permute-done.5.near_e
  21.0 0.0 collective-permute-done.6.near_o
  21.0 0.9 %shard_map.53 = (f32[2,24,2048]{2,1,0:T(8,128)S(1)}, f32[2,24,2048]{2,1,0:T(8,128)S(1)}, f32[16,512]{1,0:T(8,128)S(1)}, f32[24,512]{1,0:T(8,128)S(1)}, f32[16,512]{1,0:T(8,128)S(1)}, /*index=5*/f32[24,512]{1,0:T(8,128)S(1)}) custom-call(f32[16,2048]{1,0:T(8,128)S(1)} %get-tuple-element.37.grad, f32[32,2048]{1,0:T(8,128)S(1)} %collective-permute-done.5.near_e, ...), custom_call_target="tpu_custom_call" | custom-call | tf_op jit(solution)/shard_map/pallas_call | solution.py:76
  21.9 2.1 %collective-permute-start.9 = (f32[24,512]{1,0:T(8,128)S(1)}, f32[24,512]{1,0:T(8,128)S(1)}, u32[]{:S(2)}, u32[]{:S(2)}) collective-permute-start(f32[24,512]{1,0:T(8,128)S(1)} %get-tuple-element.46), channel_id=1, source_target_pairs={{0,8},{8,0},{16,24},{24,16},{1,9},{9,1},{17,25},{25,17},{2,10},{10... | collective-permute-start | bytes 147464 | tf_op jit(solution)/shard_map/ppermute | solution.py:490
  24.0 1.2 %collective-permute-start.10 = (f32[24,512]{1,0:T(8,128)S(1)}, f32[24,512]{1,0:T(8,128)S(1)}, u32[]{:S(2)}, u32[]{:S(2)}) collective-permute-start(f32[24,512]{1,0:T(8,128)S(1)} %get-tuple-element.47), channel_id=1, source_target_pairs={{0,24},{8,16},{16,8},{24,0},{1,25},{9,17},{17,9},{25,1},{2,26},{10... | collective-permute-start | bytes 147464 | tf_op jit(solution)/shard_map/ppermute | solution.py:490
  25.3 0.3 collective-permute-start.11
  25.6 0.7 %shard_map.54.own = f32[4,16,2048]{2,1,0:T(8,128)S(1)} custom-call(f32[4,16,2048]{2,1,0:T(8,128)S(1)} %get-tuple-element.32.noise, f32[4,24,2048]{2,1,0:T(8,128)S(1)} %get-tuple-element.33.u, f32[4,24,2048]{2,1,0:T(8,128)S(1)} %get-tuple-element.34.y1, f32[4,24,2048]{2,1,0:T(8,128)S(1)} %get-tuple-element.35.y2, f32[24,2048]{1,0:T(8,128)S(1)} %get-tuple-element.36.rr, ...), custom_call_target="tpu_custom_call" | custom-call | tf_op jit(solution)/shard_map/pallas_call | solution.py:76
  26.3 3.1 %collective-permute-done.11.refs_2_ = f32[16,512]{1,0:T(8,128)S(1)} collective-permute-done((f32[16,512]{1,0:T(8,128)S(1)}, f32[16,512]{1,0:T(8,128)S(1)}, u32[]{:S(2)}, u32[]{:S(2)}) %collective-permute-start.11) | collective-permute-done | bytes 32800 | tf_op jit(solution)/shard_map/ppermute | solution.py:490
  29.4 0.0 collective-permute-done.9.edge_e.refs_1_
  29.4 0.0 collective-permute-done.10.edge_o.refs_3_
  29.4 0.0 collective-permute-done.7.end_e
  29.4 1.2 %shard_map.55 = (f32[4,16,2048]{2,1,0:T(8,128)}, f32[16,512]{1,0:T(8,128)}) custom-call(f32[4,16,2048]{2,1,0:T(8,128)S(1)} %shard_map.54.own, f32[2,24,2048]{2,1,0:T(8,128)S(1)} %get-tuple-element.42._.u, f32[2,24,2048]{2,1,0:T(8,128)S(1)} %get-tuple-element.43.y1, f32[24,2048]{1,0:T(8,128)S(1)} %get-tuple-element.36.rr, ...), custom_call_target="tpu_custom_call" | custom-call | tf_op jit(solution)/shard_map/pallas_call | solution.py:76
  (2 shorter events, 0.0 us)
Async XLA Ops:
  1.8 0.8 %copy-start = (f32[16,512]{1,0:T(8,128)S(1)}, f32[16,512]{1,0:T(8,128)}, u32[]{:S(2)}) copy-start(f32[16,512]{1,0:T(8,128)} %rng.1) | copy-start | bytes 98308
  2.6 8.8 %collective-permute-start = (f32[32,512]{1,0:T(8,128)S(1)}, f32[32,512]{1,0:T(8,128)S(1)}, u32[]{:S(2)}, u32[]{:S(2)}) collective-permute-start(f32[32,512]{1,0:T(8,128)S(1)} %get-tuple-element.26), channel_id=1, source_target_pairs={{0,8},{8,0},{16,24},{24,16},{1,9},{9,1},{17,25},{25,17},{2,10},{10... | collective-permute-start | bytes 196616 | tf_op jit(solution)/shard_map/ppermute | solution.py:443
  5.6 5.8 %collective-permute-start.1 = (f32[32,512]{1,0:T(8,128)S(1)}, f32[32,512]{1,0:T(8,128)S(1)}, u32[]{:S(2)}, u32[]{:S(2)}) collective-permute-start(f32[32,512]{1,0:T(8,128)S(1)} %get-tuple-element.27), channel_id=1, source_target_pairs={{0,24},{8,16},{16,8},{24,0},{1,25},{9,17},{17,9},{25,1},{2,26},{10... | collective-permute-start | bytes 196616 | tf_op jit(solution)/shard_map/ppermute | solution.py:443
  7.1 4.3 %collective-permute-start.2 = (f32[16,512]{1,0:T(8,128)S(1)}, f32[16,512]{1,0:T(8,128)S(1)}, u32[]{:S(2)}, u32[]{:S(2)}) collective-permute-start(f32[16,512]{1,0:T(8,128)S(1)} %copy-done), channel_id=1, source_target_pairs={{0,16},{8,24},{16,0},{24,8},{1,17},{9,25},{17,1},{25,9},{2,18},{10... | collective-permute-start | bytes 98312 | tf_op jit(solution)/shard_map/ppermute | solution.py:445
  7.1 13.8 %collective-permute-start.5 = (f32[32,2048]{1,0:T(8,128)S(1)}, f32[32,2048]{1,0:T(8,128)S(1)}, u32[]{:S(2)}, u32[]{:S(2)}) collective-permute-start(f32[32,2048]{1,0:T(8,128)S(1)} %get-tuple-element.38), channel_id=1, source_target_pairs={{0,8},{8,0},{16,24},{24,16},{1,9},{9,1},{17,25},{25,17},{2,10},{10... | collective-permute-start | bytes 786440 | tf_op jit(solution)/shard_map/ppermute | solution.py:448
  9.1 11.9 %collective-permute-start.6 = (f32[32,2048]{1,0:T(8,128)S(1)}, f32[32,2048]{1,0:T(8,128)S(1)}, u32[]{:S(2)}, u32[]{:S(2)}) collective-permute-start(f32[32,2048]{1,0:T(8,128)S(1)} %get-tuple-element.39), channel_id=1, source_target_pairs={{0,1},{1,0},{2,3},{3,2},{4,5},{5,4},{6,7},{7,6},{8,16},{9,17},{10,... | collective-permute-start | bytes 786440 | tf_op jit(solution)/shard_map/ppermute | solution.py:448
  11.6 2.9 %collective-permute-start.3 = (f32[24,2048]{1,0:T(8,128)S(1)}, f32[24,2048]{1,0:T(8,128)S(1)}, u32[]{:S(2)}, u32[]{:S(2)}) collective-permute-start(f32[24,2048]{1,0:T(8,128)S(1)} %get-tuple-element.30), channel_id=1, source_target_pairs={{0,1},{1,0},{2,3},{3,2},{4,5},{5,4},{6,7},{7,6},{8,9},{9,8},{10,11... | collective-permute-start | bytes 589832 | tf_op jit(solution)/shard_map/ppermute | solution.py:453
  11.7 5.7 %collective-permute-start.4 = (f32[24,2048]{1,0:T(8,128)S(1)}, f32[24,2048]{1,0:T(8,128)S(1)}, u32[]{:S(2)}, u32[]{:S(2)}) collective-permute-start(f32[24,2048]{1,0:T(8,128)S(1)} %get-tuple-element.31), channel_id=1, source_target_pairs={{0,8},{1,2},{2,1},{3,4},{4,3},{5,6},{6,5},{7,15},{8,24},{9,10},{10... | collective-permute-start | bytes 589832 | tf_op jit(solution)/shard_map/ppermute | solution.py:453
  19.2 10.1 %collective-permute-start.7 = (f32[16,2048]{1,0:T(8,128)S(1)}, f32[16,2048]{1,0:T(8,128)S(1)}, u32[]{:S(2)}, u32[]{:S(2)}) collective-permute-start(f32[16,2048]{1,0:T(8,128)S(1)} %get-tuple-element.44), channel_id=1, source_target_pairs={{0,8},{8,0},{16,24},{24,16},{1,9},{9,1},{17,25},{25,17},{2,10},{10... | collective-permute-start | bytes 393224 | tf_op jit(solution)/shard_map/ppermute | solution.py:466
  21.0 8.4 %collective-permute-start.8 = (f32[16,2048]{1,0:T(8,128)S(1)}, f32[16,2048]{1,0:T(8,128)S(1)}, u32[]{:S(2)}, u32[]{:S(2)}) collective-permute-start(f32[16,2048]{1,0:T(8,128)S(1)} %get-tuple-element.45), channel_id=1, source_target_pairs={{0,1},{1,0},{2,3},{3,2},{4,5},{5,4},{6,7},{7,6},{8,16},{9,17},{10,... | collective-permute-start | bytes 393224 | tf_op jit(solution)/shard_map/ppermute | solution.py:466
  21.9 7.4 %collective-permute-start.9 = (f32[24,512]{1,0:T(8,128)S(1)}, f32[24,512]{1,0:T(8,128)S(1)}, u32[]{:S(2)}, u32[]{:S(2)}) collective-permute-start(f32[24,512]{1,0:T(8,128)S(1)} %get-tuple-element.46), channel_id=1, source_target_pairs={{0,8},{8,0},{16,24},{24,16},{1,9},{9,1},{17,25},{25,17},{2,10},{10... | collective-permute-start | bytes 147464 | tf_op jit(solution)/shard_map/ppermute | solution.py:490
  24.0 5.3 %collective-permute-start.10 = (f32[24,512]{1,0:T(8,128)S(1)}, f32[24,512]{1,0:T(8,128)S(1)}, u32[]{:S(2)}, u32[]{:S(2)}) collective-permute-start(f32[24,512]{1,0:T(8,128)S(1)} %get-tuple-element.47), channel_id=1, source_target_pairs={{0,24},{8,16},{16,8},{24,0},{1,25},{9,17},{17,9},{25,1},{2,26},{10... | collective-permute-start | bytes 147464 | tf_op jit(solution)/shard_map/ppermute | solution.py:490
  25.3 4.1 %collective-permute-start.11 = (f32[16,512]{1,0:T(8,128)S(1)}, f32[16,512]{1,0:T(8,128)S(1)}, u32[]{:S(2)}, u32[]{:S(2)}) collective-permute-start(f32[16,512]{1,0:T(8,128)S(1)} %get-tuple-element.49), channel_id=1, source_target_pairs={{0,16},{8,24},{16,0},{24,8},{1,17},{9,25},{17,1},{25,9},{2,18},{10... | collective-permute-start | bytes 98312 | tf_op jit(solution)/shard_map/ppermute | solution.py:490

commit v5 on v4

--- a/solution.py
+++ b/solution.py
@@ -89,7 +89,7 @@
     return pl.ds(pl.multiple_of(tile * LANES, LANES), LANES)
 
 
-def each_tile(width, work, unroll=8):
+def each_tile(width, work, unroll=16):
     def step(tile, carry):
         work(tile, tile_at(tile))
         return carry
@@ -216,7 +216,7 @@
     return cells[j] if 0 <= j < SLICES else 0.0
 
 
-def own_kernel(counts, s0, s1, s2, s3, full, la, lb, by0, by1, by2, grad, noise, rr, edge_e, edge_o, u, y1, y2, end_e, end_o):
+def own_kernel(counts, s0, s1, s2, s3, full, la, lb, by0, by1, by2, grad, noise, rr, u, y1, y2, end_e, other):
     tm_count, lat_count = counts
     K0, K1, K2, _ = COEFFS
     odd, has_before = places(tm_count)
@@ -225,8 +225,7 @@
     mask = lat_mask(lat_count)
     back = 1.0 + has_before
 
-    end_e[...] = s1[...]
-    end_o[...] = s2[...]
+    tm_four = tm_count == 4
 
     def gather(tile, cols):
         first, last = below_above(lat_count, la, lb, 0, cols)
@@ -236,6 +235,11 @@
         u[2, :, cols] = joined(s2[:, cols], second, ahead)
         u[3, :, cols] = joined(s3[:, cols], down(second, 3), down(ahead, 5))
         sub = iota(8, 0)
+        end_e[:8, cols] = s1[:8, cols] + jnp.where(sub == 0, 3.0 * down(ahead, 1), 0.0)
+        end_e[8:, cols] = s1[8:, cols] + jnp.where(sub == 7, 3.0 * down(second, 7), 0.0)
+        if not tm_four:
+            other[:8, cols] = s2[:8, cols] + jnp.where(sub == 0, 3.0 * down(last, 6), 0.0)
+            other[8:, cols] = s2[8:, cols] + jnp.where(sub == 7, 3.0 * down(first, 2), 0.0)
         below = jnp.where(sub == 0, down(first, 5), down(second, 6))
         above = jnp.where(sub == 7, down(ahead, 3), down(last, 2))
         rr[:, cols] = joined(full[:, cols], below, above) + 6.0
@@ -268,51 +272,27 @@
         grad[:, cols] = -total
 
     each_tile(width, twice)
-    chunk = edge_e.shape[1]
+    if not tm_four:
+        return
+    chunk = other.shape[1]
     blocks = width // chunk
     sub = iota(8, 0)
-    for out, start, shifts in ((edge_o, 0, (3, 5)), (edge_e, 8, (0, 0))):
-        for tile in range(chunk // LANES):
-            for v in range(0, edge_rows(blocks), 8):
-                rows = jnp.zeros((8, LANES), F32)
-                for k in range(min(4, blocks - v // 2)):
-                    cols = pl.ds((v // 2 + k) * chunk + tile * LANES, LANES)
-                    below, above = below_above(lat_count, la, lb, start, cols)
-                    below = down(below, (shifts[0] + 2 * k + 1) % 8)
-                    above = down(above, (shifts[1] + 2 * k + 1) % 8)
-                    rows = jnp.where(sub == 2 * k, above, jnp.where(sub == 2 * k + 1, below, rows))
-                out[v : v + 8, tile * LANES : (tile + 1) * LANES] = rows
-
-
-def third_kernel(tm_count, noise, u, y1, y2, rr, _, out):
-    _, has_before = places(tm_count)
-    width = noise.shape[2]
-    tiles = width // LANES
-    K3 = COEFFS[3]
-    back = 1.0 + has_before
-
-    def thrice(tile, cols):
-        field = rr[:ROWS, cols]
-        c0 = [u[j, :ROWS, cols] for j in range(SLICES)]
-        c1 = [y1[j, :ROWS, cols] for j in range(SLICES)]
-        c2 = [y2[j, :ROWS, cols] for j in range(SLICES)]
-        for j in range(SLICES):
-            cells, beside = around(y2, j, tile, tiles)
-            three = beside[:ROWS] - field * cells[:ROWS]
-            three = three + 3.0 * (at(c2, j - 1) + at(c2, j + 1) + at(c1, j - 2) + at(c1, j + 2))
-            three = three + (3.0 * back if j == 0 else 6.0) * c1[j]
-            left, right = (1.0 + back if j == i else 3.0 for i in (1, 0))
-            three = three + (left * at(c0, j - 1) + right * at(c0, j + 1) + at(c0, j - 3) + at(c0, j + 3))
-            out[j, :, cols] = noise[j, :, cols] + K3 * three
-
-    each_tile(width, thrice)
+    for tile in range(chunk // LANES):
+        for v in range(0, edge_rows(blocks), 8):
+            rows = jnp.zeros((8, LANES), F32)
+            for k in range(min(4, blocks - v // 2)):
+                cols = pl.ds((v // 2 + k) * chunk + tile * LANES, LANES)
+                below, above = below_above(lat_count, la, lb, 0, cols)
+                below, above = down(below, (2 * k + 4) % 8), down(above, (2 * k + 6) % 8)
+                rows = jnp.where(sub == 2 * k, above, jnp.where(sub == 2 * k + 1, below, rows))
+            other[v : v + 8, tile * LANES : (tile + 1) * LANES] = rows
 
 
 def edge_rows(blocks):
     return (2 * blocks + 7) // 8 * 8
 
 
-def near_kernel(counts, forward, grad, near_e, near_o, la, lb, rr, edge_e, edge_o, by1, by2, *refs):
+def near_kernel(counts, forward, grad, near_e, near_o, la, lb, rr, edge_o, by1, by2, *refs):
     tm_count, lat_count = counts
     odd, has_before = places(tm_count)
     width = grad.shape[1]
@@ -342,40 +322,33 @@
             out = out - (add + (2.0 * c1[:ROWS] + beyond) * by2[j, :, cols][0])
         total[:, cols] = out
 
-    each_tile(width, once, unroll=2)
+    each_tile(width, once)
     if forward:
         t = lax.axis_index("tm")
         chunk = refs[2].shape[1]
         for i, out in enumerate(refs[2:6]):
             out[:ROWS] = total[:, pl.ds(pl.multiple_of((t ^ i) * chunk, chunk), chunk)]
-        refs[3][ROWS:] = edge_e[...]
         refs[5][ROWS:] = edge_o[...]
-def last_kernel(tm_count, own, u, y1, rr, near_e, near_o, end_e, end_o, edge_e, edge_o, *refs):
-    *parts, noise, gradient, out, total, beside_far, sems = refs
+def noise_kernel(tm_count, own, p0, p1, p2, u, y1, rr, near_e, near_o, end_e, end_o, noise, first, out, sems):
     odd, has_before = places(tm_count)
     width = own.shape[2]
     tiles = width // LANES
-    K0, K1, K2, K3 = COEFFS
-    chunk = total.shape[1]
-    for i, more in enumerate(parts):
-        total[...] = more[:ROWS] if i == 0 else total[...] + more[:ROWS]
-    copies = [pltpu.make_async_copy(total, gradient, sems.at[0])]
-    copies[0].start()
-    blocks = width // chunk
-    start = edge_e.shape[0] - edge_rows(blocks)
-    sub = iota(8, 0)
-    for i, ref in enumerate((edge_o, edge_e)):
-        for b in range(blocks):
-            for tile in range(chunk // LANES):
-                k, at = b % 4, start + b // 4 * 8
-                rows = ref[at : at + 8, tile * LANES : (tile + 1) * LANES]
-                rows = jnp.where(sub < 4, down(rows, (8 - 2 * k) % 8), down(rows, 6 - 2 * k))
-                beside_far[i, :, b * chunk + tile * LANES : b * chunk + (tile + 1) * LANES] = rows
+    _, K1, K2, K3 = COEFFS
+    back = 1.0 + has_before
     row, lane = iota(ROWS, 0), iota(ROWS, 1)
 
     def work(tile, cols):
         field = rr[:ROWS, cols]
-        result = [own[j, :, cols] for j in range(SLICES)]
+        c0, c1, c2 = ([ref[j, :ROWS, cols] for j in range(SLICES)] for ref in (p0, p1, p2))
+        result = []
+        for j in range(SLICES):
+            cells, beside = around(p2, j, tile, tiles)
+            three = beside[:ROWS] - field * cells[:ROWS]
+            three = three + 3.0 * (at(c2, j - 1) + at(c2, j + 1) + at(c1, j - 2) + at(c1, j + 2))
+            three = three + (3.0 * back if j == 0 else 6.0) * c1[j]
+            left, right = (1.0 + back if j == i else 3.0 for i in (1, 0))
+            three = three + (left * at(c0, j - 1) + right * at(c0, j + 1) + at(c0, j - 3) + at(c0, j + 3))
+            result.append(own[j, :, cols] + K3 * three)
         for i, (far, end) in enumerate(((near_o, end_o), (near_e, end_e))):
             cells, beside = around(y1, i, tile, tiles)
             n0, n1 = u[i, :ROWS, cols], cells[:ROWS]
@@ -385,9 +358,8 @@
             after = far[ROWS:, tile_at(lax.rem(tile + 1, tiles))]
             west = pltpu.roll(jnp.where(lane == LANES - 1, before, f0), 1, 1)
             east = pltpu.roll(jnp.where(lane == 0, after, f0), LANES - 1, 1)
-            edge = jnp.concatenate([beside_far[i, :, cols]] * 2, axis=0)
-            above = jnp.where(row == 0, edge, down(f0, 1))
-            below = jnp.where(row == ROWS - 1, edge, down(f0, ROWS - 1))
+            above = jnp.where(row == 0, 0.0, down(f0, 1))
+            below = jnp.where(row == ROWS - 1, 0.0, down(f0, ROWS - 1))
             f1 = west + east + (above + below) - field * f0
             beyond = 3.0 * f1 + end[:, cols]
             if i == 0:
@@ -396,9 +368,11 @@
             result[a] = result[a] + (K1 + 3.0 * K3) * n0 + K2 * (2.0 * n1 + f0) + K3 * (3.0 * n2 + beyond)
             result[b] = result[b] + K2 * n0 + K3 * (3.0 * n1 + f0)
             result[c] = result[c] + K3 * n0
-        for j in range(SLICES):
-            out[j, :, cols] = result[j]
-
+        first[:, cols] = result[0]
+        for j in range(1, SLICES):
+            out[j - 1, :, cols] = result[j]
+
+    copies = []
     per = min(4, tiles)
     for q in range(0, tiles, per):
 
@@ -408,12 +382,42 @@
 
         lax.fori_loop(q, q + per, step, 0, unroll=per)
         cols = pl.ds(q * LANES, per * LANES)
-        for j in range(SLICES):
+        for j in range(1, SLICES):
             copy = pltpu.make_async_copy(
-                out.at[j, :, cols], noise.at[mirrored(odd, j), :, cols], sems.at[1 + q // per * SLICES + j]
+                out.at[j - 1, :, cols],
+                noise.at[mirrored(odd, j), :, cols],
+                sems.at[q // per * (SLICES - 1) + j - 1],
             )
             copy.start()
             copies.append(copy)
+    for copy in copies:
+        copy.wait()
+
+
+def last_kernel(tm_count, _, first, *refs):
+    *parts, noise, gradient, out, total, sems = refs
+    odd, has_before = places(tm_count)
+    for i, more in enumerate(parts):
+        total[...] = more[:ROWS] if i == 0 else total[...] + more[:ROWS]
+    copies = [pltpu.make_async_copy(total, gradient, sems.at[0])]
+    copies[0].start()
+    chunk = total.shape[1]
+    blocks = first.shape[1] // chunk
+    scale = 3.0 * COEFFS[3] * has_before
+    sub = iota(8, 0)
+    if tm_count != 4:
+        out[...] = first[...]
+    else:
+        edges = parts[-1]
+        for b in range(blocks):
+            for tile in range(chunk // LANES):
+                k, at = b % 4, ROWS + b // 4 * 8
+                rows = scale * edges[at : at + 8, tile * LANES : (tile + 1) * LANES]
+                cols = pl.ds(b * chunk + tile * LANES, LANES)
+                out[:8, cols] = first[:8, cols] + jnp.where(sub == 0, down(rows, (8 - 2 * k) % 8), 0.0)
+                out[8:, cols] = first[8:, cols] + jnp.where(sub == 7, down(rows, 6 - 2 * k), 0.0)
+    copies.append(pltpu.make_async_copy(out, noise.at[mirrored(odd, 0)], sems.at[1]))
+    copies[1].start()
     for copy in copies:
         copy.wait()
 
@@ -453,20 +457,23 @@
     la1, lb1 = lax.ppermute(la1, "lat", lat_even), lax.ppermute(lb1, ("tm", "lat"), lat_odd)
     deep = shape_of(SLICES, HELD, width)
     own = shape_of(SLICES, ROWS, width)
-    edge = shape_of(extra, chunk)
-    grad, own, rr, edge_e, edge_o, *powers, end_e, end_o = call(
+    grad, own, rr, *powers, end_e, other = call(
         functools.partial(own_kernel, counts),
-        [one, own, shape_of(HELD, width), edge, edge, deep, deep, deep, one, one],
+        [one, own, shape_of(HELD, width), deep, deep, deep, one, shape_of(extra, chunk) if forward else one],
         *slabs,
         full,
         la1,
         lb1,
         *scales,
     )
-    end_e, end_o = lax.ppermute(end_e, "tm", even), lax.ppermute(end_o, ("tm", "lat"), inner)
+    end_e = lax.ppermute(end_e, "tm", even)
+    if forward:
+        end_o = lax.ppermute(near_e[ROWS:], "tm", y_pairs)
+    else:
+        end_o = lax.ppermute(other, ("tm", "lat"), inner)
     pair = shape_of(2, HELD, width)
     if forward:
-        outs = [shape_of(ROWS + more, chunk) for more in (0, extra, 0, extra)]
+        outs = [shape_of(ROWS + more, chunk) for more in (0, 0, 0, extra)]
     else:
         outs = [one]
     u, y1, *outs = call(
@@ -478,26 +485,20 @@
         la1,
         lb1,
         rr,
-        edge_e,
-        edge_o,
+        other,
         *scales[1:],
         scratch=[pltpu.VMEM((ROWS, width), F32)] if forward else (),
     )
-    own = call(
-        functools.partial(third_kernel, tm_count), shape_of(SLICES, ROWS, width), own, *powers, rr, u
-    )
     if forward:
-        g1, g2, g3 = (lax.ppermute(g, "tm", p) for g, p in zip(outs[1:], (even, y_pairs, odd)))
-        edge_e, edge_o = g1, g3
-        parts = (outs[0], g1, g2, g3)
+        parts = outs[0], *(lax.ppermute(g, "tm", p) for g, p in zip(outs[1:], (even, y_pairs, odd)))
     else:
         parts = (lax.psum_scatter(outs[0], "tm", scatter_dimension=1, tiled=True),)
-        edge_e, edge_o = lax.ppermute(edge_e, "tm", even), lax.ppermute(edge_o, "tm", odd)
-    tiles = width // LANES
-    return call(
-        functools.partial(last_kernel, tm_count),
-        [shape_of(SLICES, ROWS, width), shape_of(ROWS, chunk)],
+    quarters = width // LANES // min(4, width // LANES)
+    noise, first = call(
+        functools.partial(noise_kernel, tm_count),
+        [shape_of(SLICES, ROWS, width), one],
         own,
+        *powers,
         u,
         y1,
         rr,
@@ -505,16 +506,22 @@
         near_o,
         end_e,
         end_o,
-        edge_e,
-        edge_o,
+        out_specs=[ANYWHERE, IN_PLACE],
+        scratch=[
+            pltpu.VMEM((SLICES - 1, ROWS, width), F32),
+            pltpu.SemaphoreType.DMA((quarters * (SLICES - 1),)),
+        ],
+    )
+    return call(
+        functools.partial(last_kernel, tm_count),
+        [shape_of(SLICES, ROWS, width), shape_of(ROWS, chunk)],
+        noise,
+        first,
         *parts,
+        in_specs=[ANYWHERE] + [IN_PLACE] * (1 + len(parts)),
         out_specs=[ANYWHERE, ANYWHERE],
-        scratch=[
-            pltpu.VMEM((SLICES, ROWS, width), F32),
-            pltpu.VMEM((ROWS, chunk), F32),
-            pltpu.VMEM((2, 8, width), F32),
-            pltpu.SemaphoreType.DMA((1 + tiles // min(4, tiles) * SLICES,)),
-        ],
+        scratch=[pltpu.VMEM((ROWS, width), F32), pltpu.VMEM((ROWS, chunk), F32), pltpu.SemaphoreType.DMA((2,))],
+        aliases={0: 0},
     )
 
 

time: 30.8 us -> 29.8 us (0.968)
  Pallas kernels: 4.95 us -> 3.92 us
  starting transfers between devices: 13.1 us -> 13.9 us
  waiting for transfers between devices: 8.31 us -> 7.58 us
    ppermute x3, waiting for transfers between devices: 3.09 us -> 0.47 us  [body(): lax.ppermute(g, 'tm', p)]
    ppermute x2, waiting for transfers between devices: 0.01 us -> 1.85 us  [the longest x1 1.84 us: body(): end_o = lax.ppermute(near_e[ROWS:], 'tm', y_pairs)]
    pallas_call x6, Pallas kernels: 4.95 us -> 3.92 us  [call(): pl.pallas_call(kernel, out_shape=outs, in_specs=in_specs or [IN_PLACE] *...]
    ppermute x2, starting transfers between devices: 1.72 us -> 2.24 us  [the longest x1 1.88 us: body(): end_e = lax.ppermute(end_e, 'tm', even)]
  transfers between devices with their start and end apart: 12 -> 12, of which waited for: 3 -> 4; matrix products, arithmetic and copies ran while one was open for 5% -> 5% of each run, Pallas kernels for 12% -> 11%
where the time goes in v5:
time: 29.8 us; the launch traced here: 29.6 us
  starting transfers between devices  13.9 us (47%)
  waiting for transfers between devices  7.58 us (25%)
  Pallas kernels  3.92 us (13%)
  local copies, waits for them, and re-layouts  1.9 us (6%)
  other arithmetic  1.57 us (5%)
  between operations  0.73 us (2%)
    pallas_call x6, Pallas kernels, call(): pl.pallas_call(kernel, out_shape=outs, in_specs=in_specs or [IN_PLACE] *...  3.92 us
    ppermute x3, starting transfers between devices, body(): lax.ppermute(g, 'tm', p)  3.92 us
    ppermute x1, starting transfers between devices, body(): lax.ppermute(corner_e, 'tm', even)  3 us
    ppermute x1, waiting for transfers between devices, body(): lax.ppermute(lb1, ('tm', 'lat'), lat_odd)  2.97 us
    ppermute x1, waiting for transfers between devices, body(): field = [held, lax.ppermute(range_field, 'tm', y_pairs)]  2.26 us
    ppermute x1, starting transfers between devices, body(): lax.ppermute(near_e, 'tm', even)  1.95 us
    ppermute x1, starting transfers between devices, body(): end_e = lax.ppermute(end_e, 'tm', even)  1.88 us
    ppermute x1, waiting for transfers between devices, body(): end_o = lax.ppermute(near_e[ROWS:], 'tm', y_pairs)  1.84 us
  transfers between devices with their start and end apart: 12, of which 4 were waited for; matrix products, arithmetic and copies ran while one was open for 5% of the time, Pallas kernels for 11%

profile of v5, /device:TPU:0, one launch (start us, length us, event | category | flops | bytes accessed | tf_op | source)
XLA Modules:
  0.0 29.6 jit_solution(14651076399047945834)
XLA Ops:
  0.6 1.1 %dynamic-slice_bitcast_fusion = (f32[16,2048]{1,0:T(8,128)S(1)}, f32[16,2048]{1,0:T(8,128)S(1)}, f32[16,2048]{1,0:T(8,128)S(1)}, f32[16,2048]{1,0:T(8,128)S(1)}) fusion(f32[4,16,2048]{2,1,0:T(8,128)} %param.3, s32[]{:T(128)S(6)} %select_n.21, s32[]{:T(128)S(6)} %select_n.19, s32[]{:T(128)S(6)} %select_n.18, s32[]{:T(128)S(6)} %select_n.20), kind=kLoop, calls=%fused_computation.3 | loop fusion | bytes 1048592 | tf_op jit(solution)/shard_map/jit(dynamic_index_in_dim)/squeeze | solution.py:440
  1.8 0.0 copy-start
  1.8 0.7 %copy-done = f32[16,512]{1,0:T(8,128)S(1)} copy-done((f32[16,512]{1,0:T(8,128)S(1)}, f32[16,512]{1,0:T(8,128)}, u32[]{:S(2)}) %copy-start) | copy-done | bytes 32792
  2.6 3.0 %collective-permute-start = (f32[32,512]{1,0:T(8,128)S(1)}, f32[32,512]{1,0:T(8,128)S(1)}, u32[]{:S(2)}, u32[]{:S(2)}) collective-permute-start(f32[32,512]{1,0:T(8,128)S(1)} %get-tuple-element.26), channel_id=1, source_target_pairs={{0,8},{8,0},{16,24},{24,16},{1,9},{9,1},{17,25},{25,17},{2,10},{10... | collective-permute-start | bytes 196616 | tf_op jit(solution)/shard_map/ppermute | solution.py:447
  5.6 1.5 %collective-permute-start.1 = (f32[32,512]{1,0:T(8,128)S(1)}, f32[32,512]{1,0:T(8,128)S(1)}, u32[]{:S(2)}, u32[]{:S(2)}) collective-permute-start(f32[32,512]{1,0:T(8,128)S(1)} %get-tuple-element.27), channel_id=1, source_target_pairs={{0,24},{8,16},{16,8},{24,0},{1,25},{9,17},{17,9},{25,1},{2,26},{10... | collective-permute-start | bytes 196616 | tf_op jit(solution)/shard_map/ppermute | solution.py:447
  7.1 0.1 collective-permute-start.2
  7.1 1.9 %collective-permute-start.5 = (f32[32,2048]{1,0:T(8,128)S(1)}, f32[32,2048]{1,0:T(8,128)S(1)}, u32[]{:S(2)}, u32[]{:S(2)}) collective-permute-start(f32[32,2048]{1,0:T(8,128)S(1)} %get-tuple-element.37), channel_id=1, source_target_pairs={{0,8},{8,0},{16,24},{24,16},{1,9},{9,1},{17,25},{25,17},{2,10},{10... | collective-permute-start | bytes 786440 | tf_op jit(solution)/shard_map/ppermute | solution.py:452
  9.1 0.0 collective-permute-start.6
  9.1 2.3 %collective-permute-done.2.refs_7_ = f32[16,512]{1,0:T(8,128)S(1)} collective-permute-done((f32[16,512]{1,0:T(8,128)S(1)}, f32[16,512]{1,0:T(8,128)S(1)}, u32[]{:S(2)}, u32[]{:S(2)}) %collective-permute-start.2) | collective-permute-done | bytes 32800 | tf_op jit(solution)/shard_map/ppermute | solution.py:449
  11.4 0.0 collective-permute-done.refs_4_
  11.4 0.0 collective-permute-done.1.refs_5_
  11.4 0.1 shard_map.51
  11.5 0.1 collective-permute-start.3
  11.6 1.2 %collective-permute-start.4 = (f32[24,2048]{1,0:T(8,128)S(1)}, f32[24,2048]{1,0:T(8,128)S(1)}, u32[]{:S(2)}, u32[]{:S(2)}) collective-permute-start(f32[24,2048]{1,0:T(8,128)S(1)} %get-tuple-element.31), channel_id=1, source_target_pairs={{0,8},{1,2},{2,1},{3,4},{4,3},{5,6},{6,5},{7,15},{8,24},{9,10},{10... | collective-permute-start | bytes 589832 | tf_op jit(solution)/shard_map/ppermute | solution.py:457
  12.7 1.6 %multiply_bitcast_fusion = (f32[4,16,2048]{2,1,0:T(8,128)S(1)}, f32[4,16,2048]{2,1,0:T(8,128)S(1)}, f32[4,16,2048]{2,1,0:T(8,128)S(1)}) fusion(f32[3,4,16,2048]{3,2,1,0:T(8,128)} %param.4), kind=kLoop, calls=%fused_computation | loop fusion | flops 1179648 | bytes 3145728 | tf_op jit(solution)/shard_map/mul | solution.py:454
  14.3 0.0 collective-permute-done.3.la
  14.3 3.0 %collective-permute-done.4.lb = f32[24,2048]{1,0:T(8,128)S(1)} collective-permute-done((f32[24,2048]{1,0:T(8,128)S(1)}, f32[24,2048]{1,0:T(8,128)S(1)}, u32[]{:S(2)}, u32[]{:S(2)}) %collective-permute-start.4) | collective-permute-done | bytes 196640 | tf_op jit(solution)/shard_map/ppermute | solution.py:457
  17.3 1.2 %shard_map.52 = (f32[16,2048]{1,0:T(8,128)S(1)}, f32[4,16,2048]{2,1,0:T(8,128)S(1)}, f32[24,2048]{1,0:T(8,128)S(1)}, f32[4,24,2048]{2,1,0:T(8,128)S(1)}, f32[4,2...) custom-call(f32[16,2048]{1,0:T(8,128)S(1)} %get-tuple-element.55.s0.refs_0_, ...), custom_call_target="tpu_custom_call" | custom-call | tf_op jit(solution)/shard_map/pallas_call | solution.py:76
  18.5 1.9 %collective-permute-start.7 = (f32[16,2048]{1,0:T(8,128)S(1)}, f32[16,2048]{1,0:T(8,128)S(1)}, u32[]{:S(2)}, u32[]{:S(2)}) collective-permute-start(f32[16,2048]{1,0:T(8,128)S(1)} %get-tuple-element.43), channel_id=1, source_target_pairs={{0,8},{8,0},{16,24},{24,16},{1,9},{9,1},{17,25},{25,17},{2,10},{10... | collective-permute-start | bytes 393224 | tf_op jit(solution)/shard_map/ppermute | solution.py:469
  20.4 0.0 collective-permute-done.5.near_e
  20.4 0.4 %collective-permute-start.8 = (f32[16,2048]{1,0:T(8,128)S(1)}, f32[16,2048]{1,0:T(8,128)S(1)}, u32[]{:S(2)}, u32[]{:S(2)}) collective-permute-start(f32[16,2048]{1,0:T(8,128)S(1)} %slice.16), channel_id=1, source_target_pairs={{0,16},{8,24},{16,0},{24,8},{1,17},{9,25},{17,1},{25,9},{2,18},{10... | collective-permute-start | bytes 393224 | tf_op jit(solution)/shard_map/ppermute | solution.py:471
  20.7 0.0 collective-permute-done.6.near_o
  20.7 0.3 %shard_map.53 = (f32[2,24,2048]{2,1,0:T(8,128)S(1)}, f32[2,24,2048]{2,1,0:T(8,128)S(1)}, f32[16,512]{1,0:T(8,128)S(1)}, f32[16,512]{1,0:T(8,128)S(1)}, f32[16,512]{1,0:T(8,128)S(1)}, /*index=5*/f32[24,512]{1,0:T(8,128)S(1)}) custom-call(f32[16,2048]{1,0:T(8,128)S(1)} %get-tuple-element.36.grad, f32[32,2048]{1,0:T(8,128)S(1)} %collective-permute-done.5.near_e, ...), custom_call_target="tpu_custom_call" | custom-call | tf_op jit(solution)/shard_map/pallas_call | solution.py:76
  21.1 1.4 %collective-permute-start.11 = (f32[24,512]{1,0:T(8,128)S(1)}, f32[24,512]{1,0:T(8,128)S(1)}, u32[]{:S(2)}, u32[]{:S(2)}) collective-permute-start(f32[24,512]{1,0:T(8,128)S(1)} %get-tuple-element.49), channel_id=1, source_target_pairs={{0,24},{8,16},{16,8},{24,0},{1,25},{9,17},{17,9},{25,1},{2,26},{10... | collective-permute-start | bytes 147464 | tf_op jit(solution)/shard_map/ppermute | solution.py:493
  22.5 2.5 %collective-permute-start.10 = (f32[16,512]{1,0:T(8,128)S(1)}, f32[16,512]{1,0:T(8,128)S(1)}, u32[]{:S(2)}, u32[]{:S(2)}) collective-permute-start(f32[16,512]{1,0:T(8,128)S(1)} %get-tuple-element.48), channel_id=1, source_target_pairs={{0,16},{8,24},{16,0},{24,8},{1,17},{9,25},{17,1},{25,9},{2,18},{10... | collective-permute-start | bytes 98312 | tf_op jit(solution)/shard_map/ppermute | solution.py:493
  25.0 0.0 collective-permute-start.9
  25.0 0.0 collective-permute-done.7.end_e
  25.0 1.8 %collective-permute-done.8.end_o = f32[16,2048]{1,0:T(8,128)S(1)} collective-permute-done((f32[16,2048]{1,0:T(8,128)S(1)}, f32[16,2048]{1,0:T(8,128)S(1)}, u32[]{:S(2)}, u32[]{:S(2)}) %collective-permute-start.8) | collective-permute-done | bytes 131104 | tf_op jit(solution)/shard_map/ppermute | solution.py:471
  26.8 1.6 %shard_map.54 = (f32[4,16,2048]{2,1,0:T(8,128)}, f32[16,2048]{1,0:T(8,128)S(1)}) custom-call(f32[4,16,2048]{2,1,0:T(8,128)S(1)} %get-tuple-element.32.own, f32[4,24,2048]{2,1,0:T(8,128)S(1)} %get-tuple-element.33.p0, f32[4,24,2048]{2,1,0:T(8,128)S(1)} %get-tuple-element.34.p1, f32[4,24,2048]{2,1,0:T(8,128)S(1)} %get-tuple-element.35.p2, ...), custom_call_target="tpu_custom_call" | custom-call | tf_op jit(solution)/shard_map/pallas_call | solution.py:76
  28.4 0.0 collective-permute-done.10.refs_2_
  28.4 0.5 %collective-permute-done.9.refs_1_ = f32[16,512]{1,0:T(8,128)S(1)} collective-permute-done((f32[16,512]{1,0:T(8,128)S(1)}, f32[16,512]{1,0:T(8,128)S(1)}, u32[]{:S(2)}, u32[]{:S(2)}) %collective-permute-start.9) | collective-permute-done | bytes 32800 | tf_op jit(solution)/shard_map/ppermute | solution.py:493
  28.9 0.7 %shard_map.55 = (f32[4,16,2048]{2,1,0:T(8,128)}, f32[16,512]{1,0:T(8,128)}) custom-call(f32[4,16,2048]{2,1,0:T(8,128)} %get-tuple-element.44._, f32[16,2048]{1,0:T(8,128)S(1)} %get-tuple-element.45.first, f32[16,512]{1,0:T(8,128)S(1)} %get-tuple-element.46.refs_0_, f32[16,512]{1,0:T(8,128)S(1)} %collective-permute-done.9.refs_1_, ...), custom_call_target="tpu_custom_call", output_to_operand_aliasing={{0}: (0, {})} | custom-call | tf_op jit(solution)/shard_map/pallas_call | solution.py:76
  (3 shorter events, 0.1 us)
Async XLA Ops:
  1.8 0.8 %copy-start = (f32[16,512]{1,0:T(8,128)S(1)}, f32[16,512]{1,0:T(8,128)}, u32[]{:S(2)}) copy-start(f32[16,512]{1,0:T(8,128)} %rng.1) | copy-start | bytes 98308
  2.6 8.8 %collective-permute-start = (f32[32,512]{1,0:T(8,128)S(1)}, f32[32,512]{1,0:T(8,128)S(1)}, u32[]{:S(2)}, u32[]{:S(2)}) collective-permute-start(f32[32,512]{1,0:T(8,128)S(1)} %get-tuple-element.26), channel_id=1, source_target_pairs={{0,8},{8,0},{16,24},{24,16},{1,9},{9,1},{17,25},{25,17},{2,10},{10... | collective-permute-start | bytes 196616 | tf_op jit(solution)/shard_map/ppermute | solution.py:447
  5.6 5.8 %collective-permute-start.1 = (f32[32,512]{1,0:T(8,128)S(1)}, f32[32,512]{1,0:T(8,128)S(1)}, u32[]{:S(2)}, u32[]{:S(2)}) collective-permute-start(f32[32,512]{1,0:T(8,128)S(1)} %get-tuple-element.27), channel_id=1, source_target_pairs={{0,24},{8,16},{16,8},{24,0},{1,25},{9,17},{17,9},{25,1},{2,26},{10... | collective-permute-start | bytes 196616 | tf_op jit(solution)/shard_map/ppermute | solution.py:447
  7.1 4.3 %collective-permute-start.2 = (f32[16,512]{1,0:T(8,128)S(1)}, f32[16,512]{1,0:T(8,128)S(1)}, u32[]{:S(2)}, u32[]{:S(2)}) collective-permute-start(f32[16,512]{1,0:T(8,128)S(1)} %copy-done), channel_id=1, source_target_pairs={{0,16},{8,24},{16,0},{24,8},{1,17},{9,25},{17,1},{25,9},{2,18},{10... | collective-permute-start | bytes 98312 | tf_op jit(solution)/shard_map/ppermute | solution.py:449
  7.1 13.2 %collective-permute-start.5 = (f32[32,2048]{1,0:T(8,128)S(1)}, f32[32,2048]{1,0:T(8,128)S(1)}, u32[]{:S(2)}, u32[]{:S(2)}) collective-permute-start(f32[32,2048]{1,0:T(8,128)S(1)} %get-tuple-element.37), channel_id=1, source_target_pairs={{0,8},{8,0},{16,24},{24,16},{1,9},{9,1},{17,25},{25,17},{2,10},{10... | collective-permute-start | bytes 786440 | tf_op jit(solution)/shard_map/ppermute | solution.py:452
  9.1 11.7 %collective-permute-start.6 = (f32[32,2048]{1,0:T(8,128)S(1)}, f32[32,2048]{1,0:T(8,128)S(1)}, u32[]{:S(2)}, u32[]{:S(2)}) collective-permute-start(f32[32,2048]{1,0:T(8,128)S(1)} %get-tuple-element.38), channel_id=1, source_target_pairs={{0,1},{1,0},{2,3},{3,2},{4,5},{5,4},{6,7},{7,6},{8,16},{9,17},{10,... | collective-permute-start | bytes 786440 | tf_op jit(solution)/shard_map/ppermute | solution.py:452
  11.5 2.8 %collective-permute-start.3 = (f32[24,2048]{1,0:T(8,128)S(1)}, f32[24,2048]{1,0:T(8,128)S(1)}, u32[]{:S(2)}, u32[]{:S(2)}) collective-permute-start(f32[24,2048]{1,0:T(8,128)S(1)} %get-tuple-element.30), channel_id=1, source_target_pairs={{0,1},{1,0},{2,3},{3,2},{4,5},{5,4},{6,7},{7,6},{8,9},{9,8},{10,11... | collective-permute-start | bytes 589832 | tf_op jit(solution)/shard_map/ppermute | solution.py:457
  11.6 5.7 %collective-permute-start.4 = (f32[24,2048]{1,0:T(8,128)S(1)}, f32[24,2048]{1,0:T(8,128)S(1)}, u32[]{:S(2)}, u32[]{:S(2)}) collective-permute-start(f32[24,2048]{1,0:T(8,128)S(1)} %get-tuple-element.31), channel_id=1, source_target_pairs={{0,8},{1,2},{2,1},{3,4},{4,3},{5,6},{6,5},{7,15},{8,24},{9,10},{10... | collective-permute-start | bytes 589832 | tf_op jit(solution)/shard_map/ppermute | solution.py:457
  18.5 6.5 %collective-permute-start.7 = (f32[16,2048]{1,0:T(8,128)S(1)}, f32[16,2048]{1,0:T(8,128)S(1)}, u32[]{:S(2)}, u32[]{:S(2)}) collective-permute-start(f32[16,2048]{1,0:T(8,128)S(1)} %get-tuple-element.43), channel_id=1, source_target_pairs={{0,8},{8,0},{16,24},{24,16},{1,9},{9,1},{17,25},{25,17},{2,10},{10... | collective-permute-start | bytes 393224 | tf_op jit(solution)/shard_map/ppermute | solution.py:469
  20.4 6.4 %collective-permute-start.8 = (f32[16,2048]{1,0:T(8,128)S(1)}, f32[16,2048]{1,0:T(8,128)S(1)}, u32[]{:S(2)}, u32[]{:S(2)}) collective-permute-start(f32[16,2048]{1,0:T(8,128)S(1)} %slice.16), channel_id=1, source_target_pairs={{0,16},{8,24},{16,0},{24,8},{1,17},{9,25},{17,1},{25,9},{2,18},{10... | collective-permute-start | bytes 393224 | tf_op jit(solution)/shard_map/ppermute | solution.py:471
  21.1 7.8 %collective-permute-start.11 = (f32[24,512]{1,0:T(8,128)S(1)}, f32[24,512]{1,0:T(8,128)S(1)}, u32[]{:S(2)}, u32[]{:S(2)}) collective-permute-start(f32[24,512]{1,0:T(8,128)S(1)} %get-tuple-element.49), channel_id=1, source_target_pairs={{0,24},{8,16},{16,8},{24,0},{1,25},{9,17},{17,9},{25,1},{2,26},{10... | collective-permute-start | bytes 147464 | tf_op jit(solution)/shard_map/ppermute | solution.py:493
  22.5 5.9 %collective-permute-start.10 = (f32[16,512]{1,0:T(8,128)S(1)}, f32[16,512]{1,0:T(8,128)S(1)}, u32[]{:S(2)}, u32[]{:S(2)}) collective-permute-start(f32[16,512]{1,0:T(8,128)S(1)} %get-tuple-element.48), channel_id=1, source_target_pairs={{0,16},{8,24},{16,0},{24,8},{1,17},{9,25},{17,1},{25,9},{2,18},{10... | collective-permute-start | bytes 98312 | tf_op jit(solution)/shard_map/ppermute | solution.py:493
  25.0 3.9 %collective-permute-start.9 = (f32[16,512]{1,0:T(8,128)S(1)}, f32[16,512]{1,0:T(8,128)S(1)}, u32[]{:S(2)}, u32[]{:S(2)}) collective-permute-start(f32[16,512]{1,0:T(8,128)S(1)} %get-tuple-element.47), channel_id=1, source_target_pairs={{0,8},{8,0},{16,24},{24,16},{1,9},{9,1},{17,25},{25,17},{2,10},{10... | collective-permute-start | bytes 98312 | tf_op jit(solution)/shard_map/ppermute | solution.py:493

commit v6 on v5

--- a/solution.py
+++ b/solution.py
@@ -131,69 +131,68 @@
     return jnp.where(odd == 1, SLICES - 1 - j, j)
 
 
-def corner_rows(blocks):
-    return 8 * (blocks // 2)
-
-
-def corner_kernel(s0, s1, s2, s3, rng, even_out, odd_out, held, even_two, odd_two):
+def edge_rows(blocks):
+    return (2 * blocks + 7) // 8 * 8
+
+
+def corner_kernel(s0, s1, s2, s3, rng, even_out, odd_out, held, even_two, odd_one, across):
     held[...] = rng[...]
-    for out, cells in ((even_two, (s3, s2)), (odd_two, (s0, s1))):
-        for i in range(2):
-            out[i * ROWS : (i + 1) * ROWS] = cells[i][...]
+    even_two[:ROWS] = s3[...]
+    even_two[ROWS:] = s2[...]
+    odd_one[...] = s0[...]
     chunk = rng.shape[1]
-    per = chunk // LANES
-    half = s0.shape[1] // 2
+    blocks = s0.shape[1] // chunk
+    for b in range(blocks):
+        across[b * ROWS : (b + 1) * ROWS] = s1[:, b * chunk : (b + 1) * chunk]
+    across[blocks * ROWS :] = rng[...]
     sub = iota(8, 0)
     for cells, out in ((s3, even_out), (s0, odd_out)):
         out[:ROWS] = rng[...]
-        for tile in range(half // LANES):
-            left, right = (
-                jnp.where(sub < 4, cells[:8, cols], cells[ROWS - 8 :, cols])
-                for cols in (pl.ds(at + tile * LANES, LANES) for at in (0, half))
-            )
-            at = ROWS + tile // per * 8
-            inner = (sub >= 2) & (sub < 6)
-            out[at : at + 8, tile % per * LANES : (tile % per + 1) * LANES] = jnp.where(inner, down(right, 4), left)
-
-
-def corners(message, tile, tiles):
-    half, per = tiles // 2, message.shape[1] // LANES
-    place = lax.rem(tile, half)
-    at = pl.multiple_of(ROWS + lax.div(place, per) * 8, 8)
-    rows = message[pl.ds(at, 8), tile_at(lax.rem(place, per))]
-    return jnp.where(tile < half, rows, down(rows, 4))
+        for tile in range(chunk // LANES):
+            for v in range(0, edge_rows(blocks), 8):
+                rows = jnp.zeros((8, LANES), F32)
+                for k in range(min(4, blocks - v // 2)):
+                    cols = pl.ds((v // 2 + k) * chunk + tile * LANES, LANES)
+                    rows = jnp.where(sub == 2 * k, down(cells[:8, cols], 2 * k), rows)
+                    rows = jnp.where(sub == 2 * k + 1, down(cells[8:, cols], (2 * k + 2) % 8), rows)
+                out[ROWS + v : ROWS + v + 8, tile * LANES : (tile + 1) * LANES] = rows
+
+
+def slab(ref, tile):
+    per = ref.shape[1] // LANES
+    at = pl.multiple_of(lax.div(tile, per) * ROWS, ROWS)
+    return ref[pl.ds(at, ROWS), tile_at(lax.rem(tile, per))]
 
 
 def rows_kernel(forward, *refs):
     slabs, (near_e, near_o), refs = refs[:SLICES], refs[SLICES : SLICES + 2], refs[SLICES + 2 :]
-    tiles = slabs[0].shape[1] // LANES
     even_lat, _, _ = lat_places(2)
     *field, full, la, lb = refs
     if forward:
         t = lax.axis_index("tm")
         chunk = field[0].shape[1]
         for i, piece in enumerate((field[0], near_e, field[1], near_o)):
-            full[:, pl.ds(pl.multiple_of((t ^ i) * chunk, chunk), chunk)] = piece[:ROWS]
+            start = piece.shape[0] - ROWS if i == 2 else 0
+            full[:, pl.ds(pl.multiple_of((t ^ i) * chunk, chunk), chunk)] = piece[start : start + ROWS]
     else:
         full[...] = field[0][...]
     sub = iota(8, 0)
 
-    def work(tile, cols):
-        for i in range(SLICES // 2):
+    per = near_e.shape[1] // LANES
+    for tile in range(full.shape[1] // LANES):
+        cols = pl.ds(tile * LANES, LANES)
+        k, at = tile // per % 4, ROWS + tile // per // 4 * 8
+        for i, corner in enumerate((near_e, near_o)):
+            rows = corner[at : at + 8, tile % per * LANES : (tile % per + 1) * LANES]
             one, two, field = slabs[2 * i], slabs[2 * i + 1], full
             first = jnp.where(sub == 3, down(field[:8, cols], 3 - i), down(two[:8, cols], 5))
+            first = jnp.where(sub == 4, down(rows, (4 - 2 * k) % 8), first)
             first = jnp.where(sub < 3, one[:8, cols], first)
             last = jnp.where(sub == 4, down(field[8:, cols], 6 - i), down(two[8:, cols], 3))
+            last = jnp.where(sub == 3, down(rows, (2 - 2 * k) % 8), last)
             last = jnp.where(sub > 4, one[8:, cols], last)
             la[8 * i : 8 * i + 8, cols] = jnp.where(even_lat, last, first)
             lb[8 * i : 8 * i + 8, cols] = jnp.where(even_lat, first, last)
-        from_e, from_o = (corners(ref, tile, tiles) for ref in (near_e, near_o))
-        first = jnp.where(sub < 2, from_e, down(from_o, 2))
-        last = jnp.where(sub >= 6, from_e, down(from_o, 6))
-        la[16:, cols] = jnp.where(even_lat, last, first)
-        lb[16:, cols] = jnp.where(even_lat, first, last)
-
-    each_tile(full.shape[1], work)
 
 
 def below_above(lat_count, la, lb, at, cols):
@@ -235,11 +234,11 @@
         u[2, :, cols] = joined(s2[:, cols], second, ahead)
         u[3, :, cols] = joined(s3[:, cols], down(second, 3), down(ahead, 5))
         sub = iota(8, 0)
-        end_e[:8, cols] = s1[:8, cols] + jnp.where(sub == 0, 3.0 * down(ahead, 1), 0.0)
-        end_e[8:, cols] = s1[8:, cols] + jnp.where(sub == 7, 3.0 * down(second, 7), 0.0)
+        end_e[:8, cols] = s1[:8, cols] + jnp.where(sub == 0, 3.0 * (down(ahead, 1) + down(ahead, 7)), 0.0)
+        end_e[8:, cols] = s1[8:, cols] + jnp.where(sub == 7, 3.0 * (down(second, 7) + down(second, 1)), 0.0)
         if not tm_four:
-            other[:8, cols] = s2[:8, cols] + jnp.where(sub == 0, 3.0 * down(last, 6), 0.0)
-            other[8:, cols] = s2[8:, cols] + jnp.where(sub == 7, 3.0 * down(first, 2), 0.0)
+            other[:8, cols] = s2[:8, cols] + jnp.where(sub == 0, 3.0 * (down(last, 6) + down(last, 2)), 0.0)
+            other[8:, cols] = s2[8:, cols] + jnp.where(sub == 7, 3.0 * (down(first, 2) + down(first, 6)), 0.0)
         below = jnp.where(sub == 0, down(first, 5), down(second, 6))
         above = jnp.where(sub == 7, down(ahead, 3), down(last, 2))
         rr[:, cols] = joined(full[:, cols], below, above) + 6.0
@@ -283,16 +282,13 @@
             for k in range(min(4, blocks - v // 2)):
                 cols = pl.ds((v // 2 + k) * chunk + tile * LANES, LANES)
                 below, above = below_above(lat_count, la, lb, 0, cols)
-                below, above = down(below, (2 * k + 4) % 8), down(above, (2 * k + 6) % 8)
+                below = down(below, (2 * k + 4) % 8) + down(below, 2 * k)
+                above = down(above, (2 * k + 6) % 8) + down(above, (2 * k + 2) % 8)
                 rows = jnp.where(sub == 2 * k, above, jnp.where(sub == 2 * k + 1, below, rows))
             other[v : v + 8, tile * LANES : (tile + 1) * LANES] = rows
 
 
-def edge_rows(blocks):
-    return (2 * blocks + 7) // 8 * 8
-
-
-def near_kernel(counts, forward, grad, near_e, near_o, la, lb, rr, edge_o, by1, by2, *refs):
+def near_kernel(counts, forward, grad, near_e, near_o, far_o, la, lb, rr, edge_o, by1, by2, *refs):
     tm_count, lat_count = counts
     odd, has_before = places(tm_count)
     width = grad.shape[1]
@@ -300,22 +296,25 @@
     mask = lat_mask(lat_count)
     u, y1 = refs[:2]
     total = refs[-1] if forward else refs[2]
+    sub = iota(8, 0)
 
     def gather(tile, cols):
-        below, above = below_above(lat_count, la, lb, 16, cols)
-        u[0, :, cols] = joined(near_o[:ROWS, cols], down(below, 6), down(above, 2)) * has_before
-        u[1, :, cols] = joined(near_e[:ROWS, cols], below, above)
+        for i, cells in ((1, near_e), (0, near_o)):
+            below, above = below_above(lat_count, la, lb, 8 - 8 * i, cols)
+            edge = jnp.where(sub == 0, down(below, 4), jnp.where(sub == 7, down(above, 4), 0.0))
+            cells = jnp.concatenate([cells[:ROWS, cols], edge], axis=0)
+            u[i, :, cols] = cells if i else cells * has_before
 
     each_tile(width, gather)
 
     def once(tile, cols):
         field = rr[:, cols]
         out = grad[:, cols]
-        for i, two in enumerate((near_o, near_e)):
+        for i in range(2):
             cells, beside = around(u, i, tile, tiles)
             c1 = (beside - field * cells) * mask
             y1[i, :, cols] = c1
-            beyond = two[ROWS:, cols] * has_before if i == 0 else two[ROWS:, cols]
+            beyond = slab(far_o, tile) * has_before if i == 0 else near_e[ROWS:, cols]
             j, inner = (0, 1) if i == 0 else (SLICES - 1, SLICES - 2)
             j, inner = pl.ds(mirrored(odd, j), 1), pl.ds(mirrored(odd, inner), 1)
             add = cells[:ROWS] * (by1[j, :, cols][0] + by2[inner, :, cols][0])
@@ -329,7 +328,7 @@
         for i, out in enumerate(refs[2:6]):
             out[:ROWS] = total[:, pl.ds(pl.multiple_of((t ^ i) * chunk, chunk), chunk)]
         refs[5][ROWS:] = edge_o[...]
-def noise_kernel(tm_count, own, p0, p1, p2, u, y1, rr, near_e, near_o, end_e, end_o, noise, first, out, sems):
+def noise_kernel(tm_count, own, p0, p1, p2, u, y1, rr, near_e, far_o, end_e, end_o, noise, first, out, sems):
     odd, has_before = places(tm_count)
     width = own.shape[2]
     tiles = width // LANES
@@ -349,13 +348,14 @@
             left, right = (1.0 + back if j == i else 3.0 for i in (1, 0))
             three = three + (left * at(c0, j - 1) + right * at(c0, j + 1) + at(c0, j - 3) + at(c0, j + 3))
             result.append(own[j, :, cols] + K3 * three)
-        for i, (far, end) in enumerate(((near_o, end_o), (near_e, end_e))):
+        for i, end in enumerate((end_o, end_e)):
+            far = (lambda at: slab(far_o, at)) if i == 0 else (lambda at: near_e[ROWS:, tile_at(at)])
             cells, beside = around(y1, i, tile, tiles)
             n0, n1 = u[i, :ROWS, cols], cells[:ROWS]
             n2 = beside[:ROWS] - field * n1
-            f0 = far[ROWS:, cols]
-            before = far[ROWS:, tile_at(lax.rem(tile + tiles - 1, tiles))]
-            after = far[ROWS:, tile_at(lax.rem(tile + 1, tiles))]
+            f0 = far(tile)
+            before = far(lax.rem(tile + tiles - 1, tiles))
+            after = far(lax.rem(tile + 1, tiles))
             west = pltpu.roll(jnp.where(lane == LANES - 1, before, f0), 1, 1)
             east = pltpu.roll(jnp.where(lane == 0, after, f0), LANES - 1, 1)
             above = jnp.where(row == 0, 0.0, down(f0, 1))
@@ -439,20 +439,23 @@
     slabs = [
         lax.dynamic_index_in_dim(cotangent, jnp.where(flip, SLICES - 1 - j, j), 0, False) for j in range(SLICES)
     ]
-    message = shape_of(ROWS + corner_rows(width // chunk), chunk)
+    message = shape_of(ROWS + edge_rows(width // chunk), chunk)
     two = shape_of(2 * ROWS, width)
-    corner_e, corner_o, held, near_e, near_o = call(
-        corner_kernel, [message, message, shape_of(ROWS, chunk), two, two], *slabs, range_field
+    corner_e, corner_o, held, near_e, near_o, across = call(
+        corner_kernel, [message, message, shape_of(ROWS, chunk), two, one, shape_of(width // chunk * ROWS + ROWS, chunk)], *slabs, range_field
     )
     corner_e, corner_o = lax.ppermute(corner_e, "tm", even), lax.ppermute(corner_o, "tm", odd)
     if forward:
-        field = [held, lax.ppermute(range_field, "tm", y_pairs)]
+        across = lax.ppermute(across, "tm", y_pairs)
+        field = [held, across]
+        far_o = lax.ppermute(across[: width // chunk * ROWS], "tm", [(0, 1), (1, 3), (3, 2), (2, 0)])
     else:
         field = [lax.all_gather(range_field, "tm", axis=1, tiled=True)]
+        far_o = lax.ppermute(across[: width // chunk * ROWS], ("tm", "lat"), inner)
     near_e, near_o = lax.ppermute(near_e, "tm", even), lax.ppermute(near_o, ("tm", "lat"), inner)
     x1, x2, x3 = iterates[0], iterates[1], iterates[2]
     scales = (W3 * x3 + W2 * x2 + W1 * x1, (W2 * W3) * x2 + (W1 * SUM2) * x1, (W1 * PROD2) * x1)
-    pair = shape_of(24, width)
+    pair = shape_of(16, width)
     full, la1, lb1 = call(functools.partial(rows_kernel, forward), [one, pair, pair], *slabs, corner_e, corner_o, *field)
     la1, lb1 = lax.ppermute(la1, "lat", lat_even), lax.ppermute(lb1, ("tm", "lat"), lat_odd)
     deep = shape_of(SLICES, HELD, width)
@@ -482,6 +485,7 @@
         grad,
         near_e,
         near_o,
+        far_o,
         la1,
         lb1,
         rr,
@@ -503,7 +507,7 @@
         y1,
         rr,
         near_e,
-        near_o,
+        far_o,
         end_e,
         end_o,
         out_specs=[ANYWHERE, IN_PLACE],

time: 29.8 us -> 28.2 us (0.946)
  other arithmetic: 1.57 us -> 0.26 us
  starting transfers between devices: 13.9 us -> 13.2 us
  waiting for transfers between devices: 7.58 us -> 7.88 us
    ppermute x1 -> x2, starting transfers between devices: 0.05 us -> 4.24 us  [the longest x1 3.03 us: body(): across = lax.ppermute(across, 'tm', y_pairs)]
    ppermute x1, waiting for transfers between devices: 0.01 us -> 2.57 us  [body(): lax.ppermute(near_e, 'tm', even)]
    ppermute x1, waiting for transfers between devices: 0.03 us -> 2.46 us  [body(): lax.ppermute(corner_o, 'tm', odd)]
    ppermute x1 -> x2, waiting for transfers between devices: 2.26 us -> 0.23 us  [the longest x1 0.23 us: body(): lax.ppermute(across[:width // chunk * ROWS], 'tm', [(0, 1), (1, 3), (3, 2...]
    ppermute x1, waiting for transfers between devices: 2.97 us -> 1.07 us  [body(): lax.ppermute(lb1, ('tm', 'lat'), lat_odd)]
    ppermute x1, waiting for transfers between devices: 1.84 us -> 0.01 us  [body(): end_o = lax.ppermute(near_e[ROWS:], 'tm', y_pairs)]
    ppermute x1, starting transfers between devices: 3 us -> 1.49 us  [body(): lax.ppermute(corner_e, 'tm', even)]
    ppermute x1, starting transfers between devices: 1.49 us -> 0.05 us  [body(): lax.ppermute(corner_o, 'tm', odd)]
  transfers between devices with their start and end apart: 12 -> 13, of which waited for: 4 -> 6; matrix products, arithmetic and copies ran while one was open for 5% -> 1% of each run, Pallas kernels for 11% -> 11%
where the time goes in v6:
time: 28.2 us; the launch traced here: 27.9 us
  starting transfers between devices  13.2 us (47%)
  waiting for transfers between devices  7.88 us (28%)
  Pallas kernels  3.93 us (14%)
  local copies, waits for them, and re-layouts  1.91 us (7%)
  between operations  0.76 us (3%)
    pallas_call x6, Pallas kernels, call(): pl.pallas_call(kernel, out_shape=outs, in_specs=in_specs or [IN_PLACE] *...  3.93 us
    ppermute x3, starting transfers between devices, body(): lax.ppermute(g, 'tm', p)  3.55 us
    ppermute x1, starting transfers between devices, body(): across = lax.ppermute(across, 'tm', y_pairs)  3.03 us
    ppermute x1, waiting for transfers between devices, body(): lax.ppermute(near_e, 'tm', even)  2.57 us
    ppermute x1, waiting for transfers between devices, body(): lax.ppermute(corner_o, 'tm', odd)  2.46 us
    ppermute x1, starting transfers between devices, body(): lax.ppermute(near_e, 'tm', even)  1.92 us
    ppermute x1, starting transfers between devices, body(): lax.ppermute(corner_e, 'tm', even)  1.49 us
    ppermute x1, starting transfers between devices, body(): end_e = lax.ppermute(end_e, 'tm', even)  1.36 us
  transfers between devices with their start and end apart: 13, of which 6 were waited for; matrix products, arithmetic and copies ran while one was open for 1% of the time, Pallas kernels for 11%

profile of v6, /device:TPU:0, one launch (start us, length us, event | category | flops | bytes accessed | tf_op | source)
XLA Modules:
  0.0 27.9 jit_solution(20219041980285980)
XLA Ops:
  0.6 1.1 %dynamic-slice_bitcast_fusion = (f32[16,2048]{1,0:T(8,128)S(1)}, f32[16,2048]{1,0:T(8,128)S(1)}, f32[16,2048]{1,0:T(8,128)S(1)}, f32[16,2048]{1,0:T(8,128)S(1)}) fusion(f32[4,16,2048]{2,1,0:T(8,128)} %param.3, s32[]{:T(128)S(6)} %select_n.21, s32[]{:T(128)S(6)} %select_n.19, s32[]{:T(128)S(6)} %select_n.18, s32[]{:T(128)S(6)} %select_n.20), kind=kLoop, calls=%fused_computation.3 | loop fusion | bytes 1048592 | tf_op jit(solution)/shard_map/jit(dynamic_index_in_dim)/squeeze | solution.py:440
  1.8 0.0 copy-start
  1.8 0.7 %copy-done = f32[16,512]{1,0:T(8,128)S(1)} copy-done((f32[16,512]{1,0:T(8,128)S(1)}, f32[16,512]{1,0:T(8,128)}, u32[]{:S(2)}) %copy-start) | copy-done | bytes 32792
  2.6 3.0 %collective-permute-start.2 = (f32[80,512]{1,0:T(8,128)S(1)}, f32[80,512]{1,0:T(8,128)S(1)}, u32[]{:S(2)}, u32[]{:S(2)}) collective-permute-start(f32[80,512]{1,0:T(8,128)S(1)} %get-tuple-element.30), channel_id=1, source_target_pairs={{0,16},{8,24},{16,0},{24,8},{1,17},{9,25},{17,1},{25,9},{2,18},{10... | collective-permute-start | bytes 491528 | tf_op jit(solution)/shard_map/ppermute | solution.py:449
  5.6 1.5 %collective-permute-start = (f32[24,512]{1,0:T(8,128)S(1)}, f32[24,512]{1,0:T(8,128)S(1)}, u32[]{:S(2)}, u32[]{:S(2)}) collective-permute-start(f32[24,512]{1,0:T(8,128)S(1)} %get-tuple-element.27), channel_id=1, source_target_pairs={{0,8},{8,0},{16,24},{24,16},{1,9},{9,1},{17,25},{25,17},{2,10},{10... | collective-permute-start | bytes 147464 | tf_op jit(solution)/shard_map/ppermute | solution.py:447
  7.1 0.0 collective-permute-start.1
  7.2 1.9 %collective-permute-start.5 = (f32[32,2048]{1,0:T(8,128)S(1)}, f32[32,2048]{1,0:T(8,128)S(1)}, u32[]{:S(2)}, u32[]{:S(2)}) collective-permute-start(f32[32,2048]{1,0:T(8,128)S(1)} %get-tuple-element.39), channel_id=1, source_target_pairs={{0,8},{8,0},{16,24},{24,16},{1,9},{9,1},{17,25},{25,17},{2,10},{10... | collective-permute-start | bytes 786440 | tf_op jit(solution)/shard_map/ppermute | solution.py:455
  9.1 0.0 collective-permute-start.6
  9.1 1.1 %collective-permute-done.refs_4_ = f32[24,512]{1,0:T(8,128)S(1)} collective-permute-done((f32[24,512]{1,0:T(8,128)S(1)}, f32[24,512]{1,0:T(8,128)S(1)}, u32[]{:S(2)}, u32[]{:S(2)}) %collective-permute-start) | collective-permute-done | bytes 49184 | tf_op jit(solution)/shard_map/ppermute | solution.py:447
  10.2 2.5 %collective-permute-done.1.refs_5_ = f32[24,512]{1,0:T(8,128)S(1)} collective-permute-done((f32[24,512]{1,0:T(8,128)S(1)}, f32[24,512]{1,0:T(8,128)S(1)}, u32[]{:S(2)}, u32[]{:S(2)}) %collective-permute-start.1) | collective-permute-done | bytes 49184 | tf_op jit(solution)/shard_map/ppermute | solution.py:447
  12.7 0.0 collective-permute-done.2.refs_7_
  12.7 0.1 shard_map.51
  12.8 0.1 collective-permute-start.3
  12.9 0.4 %collective-permute-start.4 = (f32[16,2048]{1,0:T(8,128)S(1)}, f32[16,2048]{1,0:T(8,128)S(1)}, u32[]{:S(2)}, u32[]{:S(2)}) collective-permute-start(f32[16,2048]{1,0:T(8,128)S(1)} %get-tuple-element.33), channel_id=1, source_target_pairs={{0,8},{1,2},{2,1},{3,4},{4,3},{5,6},{6,5},{7,15},{8,24},{9,10},{10... | collective-permute-start | bytes 393224 | tf_op jit(solution)/shard_map/ppermute | solution.py:460
  13.3 1.2 %collective-permute-start.7 = (f32[64,512]{1,0:T(8,128)S(1)}, f32[64,512]{1,0:T(8,128)S(1)}, u32[]{:S(2)}, u32[]{:S(2)}) collective-permute-start(f32[64,512]{1,0:T(8,128)S(1)} %slice.20), channel_id=1, source_target_pairs={{0,8},{8,24},{24,16},{16,0},{1,9},{9,25},{25,17},{17,1},{2,10},{10... | collective-permute-start | bytes 393224 | tf_op jit(solution)/shard_map/ppermute | solution.py:451
  14.5 0.3 multiply_bitcast_fusion
  14.8 2.6 %collective-permute-done.5.near_e = f32[32,2048]{1,0:T(8,128)S(1)} collective-permute-done((f32[32,2048]{1,0:T(8,128)S(1)}, f32[32,2048]{1,0:T(8,128)S(1)}, u32[]{:S(2)}, u32[]{:S(2)}) %collective-permute-start.5) | collective-permute-done | bytes 262176 | tf_op jit(solution)/shard_map/ppermute | solution.py:455
  17.4 0.1 collective-permute-start.9
  17.5 0.0 collective-permute-done.3.la
  17.5 1.1 %collective-permute-done.4.lb = f32[16,2048]{1,0:T(8,128)S(1)} collective-permute-done((f32[16,2048]{1,0:T(8,128)S(1)}, f32[16,2048]{1,0:T(8,128)S(1)}, u32[]{:S(2)}, u32[]{:S(2)}) %collective-permute-start.4) | collective-permute-done | bytes 131104 | tf_op jit(solution)/shard_map/ppermute | solution.py:460
  18.5 1.2 %shard_map.52 = (f32[16,2048]{1,0:T(8,128)S(1)}, f32[4,16,2048]{2,1,0:T(8,128)S(1)}, f32[24,2048]{1,0:T(8,128)S(1)}, f32[4,24,2048]{2,1,0:T(8,128)S(1)}, f32[4,2...) custom-call(f32[16,2048]{1,0:T(8,128)S(1)} %get-tuple-element.57.s0.refs_0_, ...), custom_call_target="tpu_custom_call" | custom-call | tf_op jit(solution)/shard_map/pallas_call | solution.py:76
  19.7 1.4 %collective-permute-start.8 = (f32[16,2048]{1,0:T(8,128)S(1)}, f32[16,2048]{1,0:T(8,128)S(1)}, u32[]{:S(2)}, u32[]{:S(2)}) collective-permute-start(f32[16,2048]{1,0:T(8,128)S(1)} %get-tuple-element.45), channel_id=1, source_target_pairs={{0,8},{8,0},{16,24},{24,16},{1,9},{9,1},{17,25},{25,17},{2,10},{10... | collective-permute-start | bytes 393224 | tf_op jit(solution)/shard_map/ppermute | solution.py:472
  21.1 0.0 collective-permute-done.6.near_o
  21.1 0.2 collective-permute-done.7.far_o
  21.3 0.3 %shard_map.53 = (f32[2,24,2048]{2,1,0:T(8,128)S(1)}, f32[2,24,2048]{2,1,0:T(8,128)S(1)}, f32[16,512]{1,0:T(8,128)S(1)}, f32[16,512]{1,0:T(8,128)S(1)}, f32[16,512]{1,0:T(8,128)S(1)}, /*index=5*/f32[24,512]{1,0:T(8,128)S(1)}) custom-call(f32[16,2048]{1,0:T(8,128)S(1)} %get-tuple-element.38.grad, f32[32,2048]{1,0:T(8,128)S(1)} %collective-permute-done.5.near_e, ...), custom_call_target="tpu_custom_call" | custom-call | tf_op jit(solution)/shard_map/pallas_call | solution.py:76
  21.7 1.0 %collective-permute-start.12 = (f32[24,512]{1,0:T(8,128)S(1)}, f32[24,512]{1,0:T(8,128)S(1)}, u32[]{:S(2)}, u32[]{:S(2)}) collective-permute-start(f32[24,512]{1,0:T(8,128)S(1)} %get-tuple-element.51), channel_id=1, source_target_pairs={{0,24},{8,16},{16,8},{24,0},{1,25},{9,17},{17,9},{25,1},{2,26},{10... | collective-permute-start | bytes 147464 | tf_op jit(solution)/shard_map/ppermute | solution.py:497
  22.7 0.5 %collective-permute-start.10 = (f32[16,512]{1,0:T(8,128)S(1)}, f32[16,512]{1,0:T(8,128)S(1)}, u32[]{:S(2)}, u32[]{:S(2)}) collective-permute-start(f32[16,512]{1,0:T(8,128)S(1)} %get-tuple-element.49), channel_id=1, source_target_pairs={{0,8},{8,0},{16,24},{24,16},{1,9},{9,1},{17,25},{25,17},{2,10},{10... | collective-permute-start | bytes 98312 | tf_op jit(solution)/shard_map/ppermute | solution.py:497
  23.2 2.0 %collective-permute-start.11 = (f32[16,512]{1,0:T(8,128)S(1)}, f32[16,512]{1,0:T(8,128)S(1)}, u32[]{:S(2)}, u32[]{:S(2)}) collective-permute-start(f32[16,512]{1,0:T(8,128)S(1)} %get-tuple-element.50), channel_id=1, source_target_pairs={{0,16},{8,24},{16,0},{24,8},{1,17},{9,25},{17,1},{25,9},{2,18},{10... | collective-permute-start | bytes 98312 | tf_op jit(solution)/shard_map/ppermute | solution.py:497
  25.2 0.4 %collective-permute-done.8.end_e = f32[16,2048]{1,0:T(8,128)S(1)} collective-permute-done((f32[16,2048]{1,0:T(8,128)S(1)}, f32[16,2048]{1,0:T(8,128)S(1)}, u32[]{:S(2)}, u32[]{:S(2)}) %collective-permute-start.8) | collective-permute-done | bytes 131104 | tf_op jit(solution)/shard_map/ppermute | solution.py:472
  25.6 1.6 %shard_map.54 = (f32[4,16,2048]{2,1,0:T(8,128)}, f32[16,2048]{1,0:T(8,128)S(1)}) custom-call(f32[4,16,2048]{2,1,0:T(8,128)S(1)} %get-tuple-element.34.own, f32[4,24,2048]{2,1,0:T(8,128)S(1)} %get-tuple-element.35.p0, f32[4,24,2048]{2,1,0:T(8,128)S(1)} %get-tuple-element.36.p1, f32[4,24,2048]{2,1,0:T(8,128)S(1)} %get-tuple-element.37.p2, ...), custom_call_target="tpu_custom_call" | custom-call | tf_op jit(solution)/shard_map/pallas_call | solution.py:76
  27.2 0.0 collective-permute-done.12.refs_3_
  27.2 0.7 %shard_map.55 = (f32[4,16,2048]{2,1,0:T(8,128)}, f32[16,512]{1,0:T(8,128)}) custom-call(f32[4,16,2048]{2,1,0:T(8,128)} %get-tuple-element.46._, f32[16,2048]{1,0:T(8,128)S(1)} %get-tuple-element.47.first, f32[16,512]{1,0:T(8,128)S(1)} %get-tuple-element.48.refs_0_, f32[16,512]{1,0:T(8,128)S(1)} %collective-permute-done.10.refs_1_, ...), custom_call_target="tpu_custom_call", output_to_operand_aliasing={{0}: (0, {})} | custom-call | tf_op jit(solution)/shard_map/pallas_call | solution.py:76
  (8 shorter events, 0.1 us)
Async XLA Ops:
  1.8 0.8 %copy-start = (f32[16,512]{1,0:T(8,128)S(1)}, f32[16,512]{1,0:T(8,128)}, u32[]{:S(2)}) copy-start(f32[16,512]{1,0:T(8,128)} %rng.1) | copy-start | bytes 98308
  2.5 12.0 %copy-start.1 = (f32[3,4,16,2048]{3,2,1,0:T(8,128)S(1)}, f32[3,4,16,2048]{3,2,1,0:T(8,128)}, u32[]{:S(2)}) copy-start(f32[3,4,16,2048]{3,2,1,0:T(8,128)} %param.4) | copy-start | bytes 4718596
  2.6 10.1 %collective-permute-start.2 = (f32[80,512]{1,0:T(8,128)S(1)}, f32[80,512]{1,0:T(8,128)S(1)}, u32[]{:S(2)}, u32[]{:S(2)}) collective-permute-start(f32[80,512]{1,0:T(8,128)S(1)} %get-tuple-element.30), channel_id=1, source_target_pairs={{0,16},{8,24},{16,0},{24,8},{1,17},{9,25},{17,1},{25,9},{2,18},{10... | collective-permute-start | bytes 491528 | tf_op jit(solution)/shard_map/ppermute | solution.py:449
  5.6 4.6 %collective-permute-start = (f32[24,512]{1,0:T(8,128)S(1)}, f32[24,512]{1,0:T(8,128)S(1)}, u32[]{:S(2)}, u32[]{:S(2)}) collective-permute-start(f32[24,512]{1,0:T(8,128)S(1)} %get-tuple-element.27), channel_id=1, source_target_pairs={{0,8},{8,0},{16,24},{24,16},{1,9},{9,1},{17,25},{25,17},{2,10},{10... | collective-permute-start | bytes 147464 | tf_op jit(solution)/shard_map/ppermute | solution.py:447
  7.1 5.6 %collective-permute-start.1 = (f32[24,512]{1,0:T(8,128)S(1)}, f32[24,512]{1,0:T(8,128)S(1)}, u32[]{:S(2)}, u32[]{:S(2)}) collective-permute-start(f32[24,512]{1,0:T(8,128)S(1)} %get-tuple-element.28), channel_id=1, source_target_pairs={{0,24},{8,16},{16,8},{24,0},{1,25},{9,17},{17,9},{25,1},{2,26},{10... | collective-permute-start | bytes 147464 | tf_op jit(solution)/shard_map/ppermute | solution.py:447
  7.2 10.2 %collective-permute-start.5 = (f32[32,2048]{1,0:T(8,128)S(1)}, f32[32,2048]{1,0:T(8,128)S(1)}, u32[]{:S(2)}, u32[]{:S(2)}) collective-permute-start(f32[32,2048]{1,0:T(8,128)S(1)} %get-tuple-element.39), channel_id=1, source_target_pairs={{0,8},{8,0},{16,24},{24,16},{1,9},{9,1},{17,25},{25,17},{2,10},{10... | collective-permute-start | bytes 786440 | tf_op jit(solution)/shard_map/ppermute | solution.py:455
  9.1 12.0 %collective-permute-start.6 = (f32[16,2048]{1,0:T(8,128)S(1)}, f32[16,2048]{1,0:T(8,128)S(1)}, u32[]{:S(2)}, u32[]{:S(2)}) collective-permute-start(f32[16,2048]{1,0:T(8,128)S(1)} %get-tuple-element.40), channel_id=1, source_target_pairs={{0,1},{1,0},{2,3},{3,2},{4,5},{5,4},{6,7},{7,6},{8,16},{9,17},{10,... | collective-permute-start | bytes 393224 | tf_op jit(solution)/shard_map/ppermute | solution.py:455
  12.8 4.7 %collective-permute-start.3 = (f32[16,2048]{1,0:T(8,128)S(1)}, f32[16,2048]{1,0:T(8,128)S(1)}, u32[]{:S(2)}, u32[]{:S(2)}) collective-permute-start(f32[16,2048]{1,0:T(8,128)S(1)} %get-tuple-element.32), channel_id=1, source_target_pairs={{0,1},{1,0},{2,3},{3,2},{4,5},{5,4},{6,7},{7,6},{8,9},{9,8},{10,11... | collective-permute-start | bytes 393224 | tf_op jit(solution)/shard_map/ppermute | solution.py:460
  12.9 5.7 %collective-permute-start.4 = (f32[16,2048]{1,0:T(8,128)S(1)}, f32[16,2048]{1,0:T(8,128)S(1)}, u32[]{:S(2)}, u32[]{:S(2)}) collective-permute-start(f32[16,2048]{1,0:T(8,128)S(1)} %get-tuple-element.33), channel_id=1, source_target_pairs={{0,8},{1,2},{2,1},{3,4},{4,3},{5,6},{6,5},{7,15},{8,24},{9,10},{10... | collective-permute-start | bytes 393224 | tf_op jit(solution)/shard_map/ppermute | solution.py:460
  13.3 8.0 %collective-permute-start.7 = (f32[64,512]{1,0:T(8,128)S(1)}, f32[64,512]{1,0:T(8,128)S(1)}, u32[]{:S(2)}, u32[]{:S(2)}) collective-permute-start(f32[64,512]{1,0:T(8,128)S(1)} %slice.20), channel_id=1, source_target_pairs={{0,8},{8,24},{24,16},{16,0},{1,9},{9,25},{25,17},{17,1},{2,10},{10... | collective-permute-start | bytes 393224 | tf_op jit(solution)/shard_map/ppermute | solution.py:451
  17.4 7.8 %collective-permute-start.9 = (f32[16,2048]{1,0:T(8,128)S(1)}, f32[16,2048]{1,0:T(8,128)S(1)}, u32[]{:S(2)}, u32[]{:S(2)}) collective-permute-start(f32[16,2048]{1,0:T(8,128)S(1)} %slice.21), channel_id=1, source_target_pairs={{0,16},{8,24},{16,0},{24,8},{1,17},{9,25},{17,1},{25,9},{2,18},{10... | collective-permute-start | bytes 393224 | tf_op jit(solution)/shard_map/ppermute | solution.py:474
  19.7 5.9 %collective-permute-start.8 = (f32[16,2048]{1,0:T(8,128)S(1)}, f32[16,2048]{1,0:T(8,128)S(1)}, u32[]{:S(2)}, u32[]{:S(2)}) collective-permute-start(f32[16,2048]{1,0:T(8,128)S(1)} %get-tuple-element.45), channel_id=1, source_target_pairs={{0,8},{8,0},{16,24},{24,16},{1,9},{9,1},{17,25},{25,17},{2,10},{10... | collective-permute-start | bytes 393224 | tf_op jit(solution)/shard_map/ppermute | solution.py:472
  21.7 5.6 %collective-permute-start.12 = (f32[24,512]{1,0:T(8,128)S(1)}, f32[24,512]{1,0:T(8,128)S(1)}, u32[]{:S(2)}, u32[]{:S(2)}) collective-permute-start(f32[24,512]{1,0:T(8,128)S(1)} %get-tuple-element.51), channel_id=1, source_target_pairs={{0,24},{8,16},{16,8},{24,0},{1,25},{9,17},{17,9},{25,1},{2,26},{10... | collective-permute-start | bytes 147464 | tf_op jit(solution)/shard_map/ppermute | solution.py:497
  22.7 4.5 %collective-permute-start.10 = (f32[16,512]{1,0:T(8,128)S(1)}, f32[16,512]{1,0:T(8,128)S(1)}, u32[]{:S(2)}, u32[]{:S(2)}) collective-permute-start(f32[16,512]{1,0:T(8,128)S(1)} %get-tuple-element.49), channel_id=1, source_target_pairs={{0,8},{8,0},{16,24},{24,16},{1,9},{9,1},{17,25},{25,17},{2,10},{10... | collective-permute-start | bytes 98312 | tf_op jit(solution)/shard_map/ppermute | solution.py:497
  23.2 4.0 %collective-permute-start.11 = (f32[16,512]{1,0:T(8,128)S(1)}, f32[16,512]{1,0:T(8,128)S(1)}, u32[]{:S(2)}, u32[]{:S(2)}) collective-permute-start(f32[16,512]{1,0:T(8,128)S(1)} %get-tuple-element.50), channel_id=1, source_target_pairs={{0,16},{8,24},{16,0},{24,8},{1,17},{9,25},{17,1},{25,9},{2,18},{10... | collective-permute-start | bytes 98312 | tf_op jit(solution)/shard_map/ppermute | solution.py:497
